TPU v7x, 32 devices: a whole 2x2x4 slice. The times are simulated.
32 devices in a mesh: parts: 2 (over x), seq: 16 (over z, y, core).
Axes of the slice: x: 2, y: 2, z: 4, core: 2. Of those that a mesh axis runs over, the one named last changes fastest.
Arguments:
- pore_features: bfloat16 [12288, 1024], P(('parts', 'seq')), parts along dimension 0, may hold values from -21 to 21
- pore_order: int32 [12288], P(('parts', 'seq')), parts along dimension 0, may hold values from 0 to 6143, as said below
- block_lists: int32 [96, 8], P(('parts', 'seq')), parts along dimension 0, may hold values from 0 to 47, as said below
- block_counts: int32 [96], P(('parts', 'seq')), parts along dimension 0, may hold values from 3 to 8
- norm1_gain: float32 [1024], replicated, may hold values from 0.5 to 1.5
- w_qkv: bfloat16 [1024, 3072], replicated, may hold values from -0.1875 to 0.1875
- query_gain: float32 [64], replicated, may hold values from 0.25 to 1.75
- key_gain: float32 [64], replicated, may hold values from 0.25 to 1.75
- w_attn_out: bfloat16 [1024, 1024], replicated, may hold values from -0.1875 to 0.1875
- norm2_gain: float32 [1024], replicated, may hold values from 0.5 to 1.5
- w_in: bfloat16 [4096, 1024], P('seq'), may hold values from -0.1875 to 0.1875
- w_out: bfloat16 [4096, 1024], P('seq'), may hold values from -0.09375 to 0.09375
Outputs:
- attended: bfloat16 [12288, 1024], P(('parts', 'seq')), parts along dimension 0
- layer_output: bfloat16 [12288, 1024], P(('parts', 'seq')), parts along dimension 0
There are 2 independent parts, one for each index of `parts`. A program takes and returns all parts, laid end to end along the dimension named above; an argument that names none is the same for every part. Nothing has to cross between parts.
Inputs may be any that keep to these rules, and one draw needn't show every extreme that they name: `pore_order`: for every k, entries k * 384 to (k + 1) * 384 - 1 are a permutation of those same numbers. block_lists[b, 0] = b; block_lists[b, 1] is a block of the next lower seq index and block_lists[b, 2] one of the next higher seq index along the closed cycle; the entries of a row are distinct; the seq index of a block c is c // 3, and every listed block lies at most 2 seq indices from that of b along the closed cycle of 16 indices.
All inputs are finite; a program needn't handle non-finite values.
Results may differ from a plain program's by a relative error of at most 0.0057.
Values may be sent and summed in bfloat16 or wider, within the bound.
No kernel may reach another device: no remote copies, remote signals or barrier semaphores. Data moves between devices by JAX's collectives and lax.ppermute only.
A program may use at most 128 MiB of HBM per device.

v0:
```python
import math

import jax
import jax.numpy as jnp
from jax import lax
from jax.sharding import PartitionSpec as P

HEADS = 16
BLOCK = 128
REACH = 2
MAXNZ = 8


def shifted(value, axis, steps):
    count = lax.axis_size(axis)
    pairs = [(source, (source + steps) % count) for source in range(count)]
    return lax.ppermute(value, axis, pairs)


def rms_scale(values, gain):
    widened = values.astype(jnp.float32)
    factor = lax.rsqrt(jnp.mean(widened * widened, axis=-1, keepdims=True) + 1e-06)
    return (widened * factor * gain).astype(jnp.bfloat16)


def head_norm(values, gain, factor_scale):
    shaped = values.reshape(values.shape[0], HEADS, values.shape[1] // HEADS)
    factor = lax.rsqrt(jnp.mean(shaped * shaped, axis=-1, keepdims=True) + 1e-06)
    return (shaped * factor * gain * factor_scale).astype(jnp.bfloat16)


def attend_group(queries, keys, values, keep_mask):
    scores = jnp.einsum("bqhd,bkhd->bhqk", queries, keys, preferred_element_type=jnp.float32)
    weights = jnp.where(keep_mask[:, None], jnp.exp(scores), 0.0)
    totals = jnp.sum(weights, axis=-1)
    summed = jnp.einsum(
        "bhqk,bkhd->bqhd", weights.astype(jnp.bfloat16), values, preferred_element_type=jnp.float32
    )
    return summed / jnp.transpose(totals, (0, 2, 1))[..., None]


def attend_heads(queries, keys, values, keep_mask):
    group_size = 4
    group_total = HEADS // group_size

    def one_group(group_index):
        first_head = group_index * group_size
        q_part = lax.dynamic_slice_in_dim(queries, first_head, group_size, 2)
        k_part = lax.dynamic_slice_in_dim(keys, first_head, group_size, 2)
        v_part = lax.dynamic_slice_in_dim(values, first_head, group_size, 2)
        return attend_group(q_part, k_part, v_part, keep_mask).astype(jnp.bfloat16)

    stacked = lax.map(one_group, jnp.arange(group_total))
    return jnp.moveaxis(stacked, 0, 2)


def unit_terms(rows_in, in_rows, out_rows):
    pre_act = lax.dot_general(
        rows_in, in_rows, (((1,), (1,)), ((), ())), preferred_element_type=jnp.float32
    )
    active = jax.nn.gelu(pre_act, approximate=True).astype(jnp.bfloat16)
    return jnp.dot(active, out_rows, preferred_element_type=jnp.float32)


def shards(
    pore_features,
    pore_order,
    block_lists,
    block_counts,
    norm1_gain,
    w_qkv,
    query_gain,
    key_gain,
    w_attn_out,
    norm2_gain,
    w_in,
    w_out,
):
    local_rows = pore_features.shape[0]
    width = pore_features.shape[1]
    head_dim = width // HEADS
    blocks_here = local_rows // BLOCK
    cycle_size = lax.axis_size("seq")
    my_index = lax.axis_index("seq")
    ordered = jnp.take(pore_features, pore_order - my_index * local_rows, axis=0)
    normed = rms_scale(ordered, norm1_gain)
    projected = jnp.dot(normed, w_qkv, preferred_element_type=jnp.float32)
    queries = head_norm(projected[:, :width], query_gain, 2.0 / math.sqrt(head_dim))
    keys = head_norm(projected[:, width : 2 * width], key_gain, 1.0).reshape(local_rows, width)
    values = projected[:, 2 * width :].astype(jnp.bfloat16)
    key_value = jnp.concatenate([keys, values], axis=1)
    lower_side = []
    upper_side = []
    from_lower = key_value
    from_upper = key_value
    for distance in range(REACH):
        from_lower = shifted(from_lower, "seq", 1)
        from_upper = shifted(from_upper, "seq", -1)
        lower_side.append(from_lower)
        upper_side.append(from_upper)
    window = jnp.concatenate(lower_side[::-1] + [key_value] + upper_side, axis=0)
    offsets = (block_lists // blocks_here - my_index) % cycle_size
    offsets = jnp.where(offsets > cycle_size // 2, offsets - cycle_size, offsets)
    positions = (offsets + REACH) * blocks_here + block_lists % blocks_here
    in_force = jnp.arange(MAXNZ)[None, :] < block_counts[:, None]
    window_count = window.shape[0] // BLOCK
    matches = (positions[:, :, None] == jnp.arange(window_count)[None, None, :]) & in_force[
        :, :, None
    ]
    allowed = jnp.any(matches, axis=1)
    keep_mask = jnp.repeat(jnp.repeat(allowed, BLOCK, axis=0), BLOCK, axis=1)[None]
    all_keys = window[:, :width].reshape(1, -1, HEADS, head_dim)
    all_values = window[:, width:].reshape(1, -1, HEADS, head_dim)
    head_outputs = attend_heads(
        queries.reshape(1, local_rows, HEADS, head_dim), all_keys, all_values, keep_mask
    )
    attention = head_outputs.reshape(local_rows, width)
    attn_proj = jnp.dot(attention, w_attn_out, preferred_element_type=jnp.float32)
    attended = (ordered.astype(jnp.float32) + attn_proj).astype(jnp.bfloat16)
    second = rms_scale(attended, norm2_gain)
    feed_forward = unit_terms(
        second,
        lax.all_gather(w_in, "seq", axis=0, tiled=True),
        lax.all_gather(w_out, "seq", axis=0, tiled=True),
    )
    layer_output = (attended.astype(jnp.float32) + feed_forward).astype(jnp.bfloat16)
    return (attended, layer_output)


def solution(mesh):
    return jax.shard_map(
        shards,
        mesh=mesh,
        in_specs=(
            P(("parts", "seq"), None),
            P(("parts", "seq")),
            P(("parts", "seq"), None),
            P(("parts", "seq")),
            P(),
            P(),
            P(),
            P(),
            P(),
            P(),
            P("seq", None),
            P("seq", None),
        ),
        out_specs=(P(("parts", "seq"), None), P(("parts", "seq"), None)),
        check_vma=False,
    )
```

profile of v0, /device:TPU:0, one launch (start us, length us, event | category | flops | bytes accessed | tf_op | source)
XLA Modules:
  0.0 233.5 jit_solution(10448857464439033997)
XLA Ops:
  13.6 5.2 %fusion.63 = f32[384,3072]{1,0:T(8,128)S(1)} fusion(bf16[1024,3072]{1,0:T(8,128)(2,1)} %param.19, f32[1024]{0:T(1024)S(1)} %copy-done.8, f32[384]{0:T(512)S(1)} %add_rsqrt_fusion.3, bf16[384,1024]{1,0:T(8,128)(2,1)} %gather_fusion, pred[384]{0:T(512)(128)(4,1)S(1)} %get-tuple-element.78), kind=kOutput, calls=%fused_computation.59 | convolution fusion | flops 2417885184 | bytes 11802496 | tf_op jit(solution)/shard_map/dot_general | solution.py:87
  22.2 3.0 %copy.33 = f32[384,1024]{0,1:T(8,128)} copy(f32[384,1024]{1,0:T(8,128)} %slice_multiply_fusion) | data formatting | bytes 3145728 | tf_op jit(solution)/shard_map/mul | solution.py:28
  31.2 5.0 %slice_multiply_fusion.1 = (f32[384,1024]{1,0:T(8,128)}, bf16[384,1024]{1,0:T(8,128)(2,1)S(1)}, f32[384,1024]{1,0:T(8,128)}) fusion(f32[384,3072]{1,0:T(8,128)} %copy-done.4, f32[1024]{0:T(1024)S(1)} %mul.162, f32[384,1024]{1,0:T(8,128)} %copy.34), kind=kLoop, calls=%fused_computation.98 | loop fusion | flops 1572864 | bytes 8654848 | tf_op jit(solution)/shard_map/mul | solution.py:28
  38.9 5.0 %collective-permute-start.2 = (bf16[384,2048]{1,0:T(8,128)(2,1)}, bf16[384,2048]{1,0:T(8,128)(2,1)}, u32[]{:S(2)}, u32[]{:S(2)}) collective-permute-start(bf16[384,2048]{1,0:T(8,128)(2,1)} %pad_maximum_fusion), channel_id=1, source_target_pairs={{0,15},{1,0},{2,1},{3,2},{4,3},{5,4},{6,5},{7,6},{8,7},{9,8},{10,9... | collective-permute-start | bytes 4718600 | tf_op jit(solution)/shard_map/ppermute | solution.py:17
  43.9 35.5 %collective-permute-done = bf16[384,2048]{1,0:T(8,128)(2,1)} collective-permute-done((bf16[384,2048]{1,0:T(8,128)(2,1)}, bf16[384,2048]{1,0:T(8,128)(2,1)}, u32[]{:S(2)}, u32[]{:S(2)}) %collective-permute-start) | collective-permute-done | bytes 1572896 | tf_op jit(solution)/shard_map/ppermute | solution.py:17
  79.4 19.2 %collective-permute-start.1 = (bf16[384,2048]{1,0:T(8,128)(2,1)}, bf16[384,2048]{1,0:T(8,128)(2,1)}, u32[]{:S(2)}, u32[]{:S(2)}) collective-permute-start(bf16[384,2048]{1,0:T(8,128)(2,1)} %collective-permute-done), channel_id=1, source_target_pairs={{0,1},{1,2},{2,3},{3,4},{4,5},{5,6},{6,7},{7,8},{8,9},{9,10},{10,1... | collective-permute-start | bytes 4718600 | tf_op jit(solution)/shard_map/ppermute | solution.py:17
  98.5 3.1 %copy.37 = f32[384,1024]{0,1:T(8,128)} copy(f32[384,1024]{1,0:T(8,128)} %get-tuple-element.84) | data formatting | bytes 3145728 | tf_op jit(solution)/shard_map/mul | solution.py:28
  103.9 3.1 %copy.36 = f32[384,1024]{0,1:T(8,128)} copy(f32[384,1024]{1,0:T(8,128)} %get-tuple-element.86) | data formatting | bytes 3145728 | tf_op jit(solution)/shard_map/slice | solution.py:88
  109.6 8.2 %collective-permute-done.1 = bf16[384,2048]{1,0:T(8,128)(2,1)} collective-permute-done((bf16[384,2048]{1,0:T(8,128)(2,1)}, bf16[384,2048]{1,0:T(8,128)(2,1)}, u32[]{:S(2)}, u32[]{:S(2)}) %collective-permute-start.1) | collective-permute-done | bytes 1572896 | tf_op jit(solution)/shard_map/ppermute | solution.py:17
  122.5 9.4 %collective-permute-done.3 = bf16[384,2048]{1,0:T(8,128)(2,1)} collective-permute-done((bf16[384,2048]{1,0:T(8,128)(2,1)}, bf16[384,2048]{1,0:T(8,128)(2,1)}, u32[]{:S(2)}, u32[]{:S(2)}) %collective-permute-start.3) | collective-permute-done | bytes 1572896 | tf_op jit(solution)/shard_map/ppermute | solution.py:17
  133.4 3.6 %fusion.82 = (bf16[1920,1024]{1,0:T(8,128)(2,1)}, bf16[1920,1024]{1,0:T(8,128)(2,1)}) fusion(bf16[1920,2048]{1,0:T(8,128)(2,1)S(1)} %constant_dynamic-update-slice_fusion), kind=kLoop, calls=%fused_computation.99 | loop fusion | bytes 15728640 | tf_op jit(solution)/shard_map/slice | solution.py:112
  137.0 6.2 %copy.35 = bf16[1920,1024]{0,1:T(8,128)(2,1)} copy(bf16[1920,1024]{1,0:T(8,128)(2,1)} %get-tuple-element.83) | data formatting | bytes 7864320 | tf_op jit(solution)/shard_map/slice | solution.py:113
  143.2 6.4 %copy.38 = bf16[1920,1024]{0,1:T(8,128)(2,1)} copy(bf16[1920,1024]{1,0:T(8,128)(2,1)} %get-tuple-element.82) | data formatting | bytes 7864320 | tf_op jit(solution)/shard_map/slice | solution.py:112
  149.6 52.1 %while.11 = (s32[]{:T(128)}, bf16[4,1,384,4,64]{2,4,3,1,0:T(8,128)(2,1)}, s32[4]{0:T(128)S(1)}, bf16[1,1920,16,64]{1,3,2,0:T(8,128)(2,1)}, bf16[1,384,16,64]{1,3...) while((s32[]{:T(128)}, ...), condition=%wide.region_6.7_spmd.clone, body=%wide.region_4.6_spmd.clone.sunk | while | flops 766966272 | bytes 29658412 | solution.py:53
  154.1 4.4 %fusion.94 = (f32[4,384]{1,0:T(4,128)S(1)}, f32[4,384,1920]{2,1,0:T(8,128)S(1)}) fusion(pred[384,1920]{1,0:T(8,128)(4,1)S(1)} %copy.42, bf16[1,1920,16,64]{1,3,2,0:T(8,128)(2,1)} %get-tuple-element.163, s32[]{:T(128)S(6)} %select_n.101, bf16[1,384,16,64]{1,3,2,0:T(8,128)(2,1)} %get-tuple-element.162), kind=kOutput, calls=%fused_computation.3.clone.1 | convolution fusion | flops 383384064 | bytes 13720576 | tf_op jit(solution)/shard_map/while/body/eval_jaxpr/bqhd,bkhd->bhqk/dot_general | solution.py:33
  158.5 4.0 %fusion.95 = bf16[4,1,384,4,64]{2,4,3,1,0:T(8,128)(2,1)} fusion(bf16[4,1,384,4,64]{2,4,3,1,0:T(8,128)(2,1)} %get-tuple-element.148, s32[]{:T(128)} %get-tuple-element.147, f32[4,384,1920]{2,1,0:T(8,128)S(1)} %get-tuple-element.134, pred[384,1920]{1,0:T(8,128)(4,1)S(1)} %copy.42, bf16[1,1920,16,64]{1,3,2,0:T(8,128)(2,1)} %get-tuple-element.161, ...), kind=kOutput, calls=%fused_computation.12.clone.1 | convolution fusion | flops 383582208 | bytes 13720068 | tf_op jit(solution)/shard_map/while/body/eval_jaxpr/bhqk,bkhd->bqhd/dot_general | solution.py:36
  167.0 4.4 %fusion.94 = (f32[4,384]{1,0:T(4,128)S(1)}, f32[4,384,1920]{2,1,0:T(8,128)S(1)}) fusion(pred[384,1920]{1,0:T(8,128)(4,1)S(1)} %copy.42, bf16[1,1920,16,64]{1,3,2,0:T(8,128)(2,1)} %get-tuple-element.163, s32[]{:T(128)S(6)} %select_n.101, bf16[1,384,16,64]{1,3,2,0:T(8,128)(2,1)} %get-tuple-element.162), kind=kOutput, calls=%fused_computation.3.clone.1 | convolution fusion | flops 383384064 | bytes 13720576 | tf_op jit(solution)/shard_map/while/body/eval_jaxpr/bqhd,bkhd->bhqk/dot_general | solution.py:33
  171.4 4.3 %fusion.95 = bf16[4,1,384,4,64]{2,4,3,1,0:T(8,128)(2,1)} fusion(bf16[4,1,384,4,64]{2,4,3,1,0:T(8,128)(2,1)} %get-tuple-element.148, s32[]{:T(128)} %get-tuple-element.147, f32[4,384,1920]{2,1,0:T(8,128)S(1)} %get-tuple-element.134, pred[384,1920]{1,0:T(8,128)(4,1)S(1)} %copy.42, bf16[1,1920,16,64]{1,3,2,0:T(8,128)(2,1)} %get-tuple-element.161, ...), kind=kOutput, calls=%fused_computation.12.clone.1 | convolution fusion | flops 383582208 | bytes 13720068 | tf_op jit(solution)/shard_map/while/body/eval_jaxpr/bhqk,bkhd->bqhd/dot_general | solution.py:36
  180.2 4.4 %fusion.94 = (f32[4,384]{1,0:T(4,128)S(1)}, f32[4,384,1920]{2,1,0:T(8,128)S(1)}) fusion(pred[384,1920]{1,0:T(8,128)(4,1)S(1)} %copy.42, bf16[1,1920,16,64]{1,3,2,0:T(8,128)(2,1)} %get-tuple-element.163, s32[]{:T(128)S(6)} %select_n.101, bf16[1,384,16,64]{1,3,2,0:T(8,128)(2,1)} %get-tuple-element.162), kind=kOutput, calls=%fused_computation.3.clone.1 | convolution fusion | flops 383384064 | bytes 13720576 | tf_op jit(solution)/shard_map/while/body/eval_jaxpr/bqhd,bkhd->bhqk/dot_general | solution.py:33
  184.6 4.0 %fusion.95 = bf16[4,1,384,4,64]{2,4,3,1,0:T(8,128)(2,1)} fusion(bf16[4,1,384,4,64]{2,4,3,1,0:T(8,128)(2,1)} %get-tuple-element.148, s32[]{:T(128)} %get-tuple-element.147, f32[4,384,1920]{2,1,0:T(8,128)S(1)} %get-tuple-element.134, pred[384,1920]{1,0:T(8,128)(4,1)S(1)} %copy.42, bf16[1,1920,16,64]{1,3,2,0:T(8,128)(2,1)} %get-tuple-element.161, ...), kind=kOutput, calls=%fused_computation.12.clone.1 | convolution fusion | flops 383582208 | bytes 13720068 | tf_op jit(solution)/shard_map/while/body/eval_jaxpr/bhqk,bkhd->bqhd/dot_general | solution.py:36
  193.1 4.4 %fusion.94 = (f32[4,384]{1,0:T(4,128)S(1)}, f32[4,384,1920]{2,1,0:T(8,128)S(1)}) fusion(pred[384,1920]{1,0:T(8,128)(4,1)S(1)} %copy.42, bf16[1,1920,16,64]{1,3,2,0:T(8,128)(2,1)} %get-tuple-element.163, s32[]{:T(128)S(6)} %select_n.101, bf16[1,384,16,64]{1,3,2,0:T(8,128)(2,1)} %get-tuple-element.162), kind=kOutput, calls=%fused_computation.3.clone.1 | convolution fusion | flops 383384064 | bytes 13720576 | tf_op jit(solution)/shard_map/while/body/eval_jaxpr/bqhd,bkhd->bhqk/dot_general | solution.py:33
  197.5 4.1 %fusion.95 = bf16[4,1,384,4,64]{2,4,3,1,0:T(8,128)(2,1)} fusion(bf16[4,1,384,4,64]{2,4,3,1,0:T(8,128)(2,1)} %get-tuple-element.148, s32[]{:T(128)} %get-tuple-element.147, f32[4,384,1920]{2,1,0:T(8,128)S(1)} %get-tuple-element.134, pred[384,1920]{1,0:T(8,128)(4,1)S(1)} %copy.42, bf16[1,1920,16,64]{1,3,2,0:T(8,128)(2,1)} %get-tuple-element.161, ...), kind=kOutput, calls=%fused_computation.12.clone.1 | convolution fusion | flops 383582208 | bytes 13720068 | tf_op jit(solution)/shard_map/while/body/eval_jaxpr/bhqk,bkhd->bqhd/dot_general | solution.py:36
  204.2 8.7 %all-gather.5.cloned.1.call-done = bf16[4096,1024]{1,0:T(8,128)(2,1)} async-done(((bf16[256,1024]{1,0:T(8,128)(2,1)}), bf16[4096,1024]{1,0:T(8,128)(2,1)}) %all-gather.5.cloned.1.call-update) | async-done | bytes 8388624 | tf_op jit(solution)/shard_map/all_gather | solution.py:124
  212.9 13.8 %fusion.54 = bf16[384,1024]{1,0:T(8,128)(2,1)} fusion(bf16[384,1024]{1,0:T(8,128)(2,1)S(1)} %get-tuple-element.88, bf16[4096,1024]{1,0:T(8,128)(2,1)} %all-gather.5.cloned.1.call-done, bf16[4096,1024]{1,0:T(8,128)(2,1)} %all-gather.3.cloned.1.call-done, f32[1024]{0:T(1024)S(1)} %copy-done.9, f32[384]{0:T(512)S(1)} %add_rsqrt_fusion.2), kind=kOutput, calls=%fused_computation.50 | convolution fusion | flops 6459359232 | bytes 18355712 | tf_op jit(solution)/shard_map/dot_general | solution.py:62
  (77 shorter events, 47.2 us)
Async XLA Ops:
  7.2 194.5 %copy-start = (bf16[1024,1024]{1,0:T(8,128)(2,1)S(1)}, bf16[1024,1024]{1,0:T(8,128)(2,1)}, u32[]{:S(2)}) copy-start(bf16[1024,1024]{1,0:T(8,128)(2,1)} %param.22) | copy-start | bytes 6291460
  7.2 2.2 copy-start.1
  7.2 197.0 %all-gather.3.cloned.1.call-start = ((), (), s32[]{:S(2)}) async-start(), calls=%async_computation | async-start | bytes 8912896 | tf_op jit(solution)/shard_map/all_gather | solution.py:123
  7.9 204.9 %all-gather.5.cloned.1.call-start = ((), (), s32[]{:S(2)}) async-start(), calls=%async_computation.1 | async-start | bytes 8912896 | tf_op jit(solution)/shard_map/all_gather | solution.py:124
  9.4 4.2 %copy-start.8 = (f32[1024]{0:T(1024)S(1)}, f32[1024]{0:T(1024)}, u32[]{:S(2)}) copy-start(f32[1024]{0:T(1024)} %param.18) | copy-start | bytes 12292
  18.8 2.1 copy-start.4
  25.3 5.9 %copy-start.6 = (f32[64]{0:T(128)S(1)}, f32[64]{0:T(128)}, u32[]{:S(2)}) copy-start(f32[64]{0:T(128)} %param.21) | copy-start | bytes 772
  36.2 0.9 copy-start.2
  37.1 64.5 %copy-start.10 = (s32[3]{0:T(128)S(1)}, s32[3]{0:T(128)}, u32[]{:S(2)}) copy-start(s32[3]{0:T(128)} %param.17) | copy-start | bytes 40
  37.1 64.6 %copy-start.5 = (s32[3,8]{1,0:T(4,128)S(1)}, s32[3,8]{1,0:T(4,128)}, u32[]{:S(2)}) copy-start(s32[3,8]{1,0:T(4,128)} %param.16) | copy-start | bytes 292
  38.4 40.9 %collective-permute-start = (bf16[384,2048]{1,0:T(8,128)(2,1)}, bf16[384,2048]{1,0:T(8,128)(2,1)}, u32[]{:S(2)}, u32[]{:S(2)}) collective-permute-start(bf16[384,2048]{1,0:T(8,128)(2,1)} %pad_maximum_fusion), channel_id=1, source_target_pairs={{0,1},{1,2},{2,3},{3,4},{4,5},{5,6},{6,7},{7,8},{8,9},{9,10},{10,1... | collective-permute-start | bytes 4718600 | tf_op jit(solution)/shard_map/ppermute | solution.py:17
  38.9 63.2 %collective-permute-start.2 = (bf16[384,2048]{1,0:T(8,128)(2,1)}, bf16[384,2048]{1,0:T(8,128)(2,1)}, u32[]{:S(2)}, u32[]{:S(2)}) collective-permute-start(bf16[384,2048]{1,0:T(8,128)(2,1)} %pad_maximum_fusion), channel_id=1, source_target_pairs={{0,15},{1,0},{2,1},{3,2},{4,3},{5,4},{6,5},{7,6},{8,7},{9,8},{10,9... | collective-permute-start | bytes 4718600 | tf_op jit(solution)/shard_map/ppermute | solution.py:17
  79.4 38.4 %collective-permute-start.1 = (bf16[384,2048]{1,0:T(8,128)(2,1)}, bf16[384,2048]{1,0:T(8,128)(2,1)}, u32[]{:S(2)}, u32[]{:S(2)}) collective-permute-start(bf16[384,2048]{1,0:T(8,128)(2,1)} %collective-permute-done), channel_id=1, source_target_pairs={{0,1},{1,2},{2,3},{3,4},{4,5},{5,6},{6,7},{7,8},{8,9},{9,10},{10,1... | collective-permute-start | bytes 4718600 | tf_op jit(solution)/shard_map/ppermute | solution.py:17
  101.7 5.4 %copy-start.7 = (f32[64]{0:T(128)S(1)}, f32[64]{0:T(128)}, u32[]{:S(2)}) copy-start(f32[64]{0:T(128)} %param.20) | copy-start | bytes 772
  102.1 29.8 %collective-permute-start.3 = (bf16[384,2048]{1,0:T(8,128)(2,1)}, bf16[384,2048]{1,0:T(8,128)(2,1)}, u32[]{:S(2)}, u32[]{:S(2)}) collective-permute-start(bf16[384,2048]{1,0:T(8,128)(2,1)} %collective-permute-done.2), channel_id=1, source_target_pairs={{0,15},{1,0},{2,1},{3,2},{4,3},{5,4},{6,5},{7,6},{8,7},{9,8},{10,9... | collective-permute-start | bytes 4718600 | tf_op jit(solution)/shard_map/ppermute | solution.py:17
  109.6 11.2 %copy-start.3 = (bf16[384,1024]{1,0:T(8,128)(2,1)S(1)}, bf16[384,1024]{1,0:T(8,128)(2,1)}, u32[]{:S(2)}) copy-start(bf16[384,1024]{1,0:T(8,128)(2,1)} %copy-done.2) | copy-start | bytes 2359300
  201.6 11.3 %copy-start.9 = (f32[1024]{0:T(1024)S(1)}, f32[1024]{0:T(1024)}, u32[]{:S(2)}) copy-start(f32[1024]{0:T(1024)} %param.23) | copy-start | bytes 12292
  204.1 22.6 %copy-start.11 = (bf16[384,1024]{1,0:T(8,128)(2,1)}, bf16[384,1024]{1,0:T(8,128)(2,1)S(1)}, u32[]{:S(2)}) copy-start(bf16[384,1024]{1,0:T(8,128)(2,1)S(1)} %get-tuple-element.88) | copy-start | bytes 2359300
Sparse Core Ops, SparseCore 0:
  10.2 120.4 all-gather.2
  132.8 79.9 all-gather.4
where the time goes:
time: 235 us; the launch traced here: 234 us
  waiting for transfers between devices  63.1 us (27%)
  local copies, waits for them, and re-layouts  57.2 us (24%)
  matrix products  55.5 us (24%)
  starting transfers between devices  24.9 us (11%)
  other arithmetic  15.8 us (7%)
  between operations  14.3 us (6%)
  loops' own time  2.62 us (1%)
    ppermute x4, waiting for transfers between devices, shifted(): return lax.ppermute(value, axis, pairs)  53 us
    ppermute x4, starting transfers between devices, shifted(): return lax.ppermute(value, axis, pairs)  24.9 us
    dot_general x4, matrix products, attend_group(): jnp.einsum('bqhd,bkhd->bhqk', queries, keys, preferred_element_type=jnp.f...  17.7 us
    dot_general x4, matrix products, attend_group(): jnp.einsum('bhqk,bkhd->bqhd', weights.astype(jnp.bfloat16), values, prefe...  16.4 us
    dot_general x1, matrix products, unit_terms(): return jnp.dot(active, out_rows, preferred_element_type=jnp.float32)  13.8 us
    slice x2, local copies, waits for them, and re-layouts, shards(): all_keys = window[:, :width].reshape(1, -1, HEADS, head_dim)  10 us
    all_gather x1, waiting for transfers between devices, shards(): lax.all_gather(w_out, 'seq', axis=0, tiled=True)  8.69 us
    broadcast_in_dim x4, local copies, waits for them, and re-layouts, attend_group(): weights = jnp.where(keep_mask[:, None], jnp.exp(scores), 0.0)  8.33 us
  transfers between devices with their start and end apart: 6, of which 4 were waited for; matrix products, arithmetic and copies ran while one was open for 48% of the time, Pallas kernels for 0%

commit v1 on v0

v1 whole, which is shorter than its diff:
```python
import functools
import math

import jax
import jax.numpy as jnp
from jax import lax
from jax.experimental import pallas as pl
from jax.experimental.pallas import tpu as pltpu
from jax.sharding import PartitionSpec as P

HEADS = 16
BLOCK = 128
REACH = 2
MAXNZ = 8
EPS = 1e-06
MIB = 1024 * 1024


def chip_grid(chips):
    columns = 1 << ((chips.bit_length() - 1) // 2)
    return chips // columns, columns


def chip_cycle(chips):
    rows, columns = chip_grid(chips)
    if columns < 2 or rows % 2:
        return list(range(chips))
    order = [(row, 0) for row in range(rows)]
    for row in reversed(range(rows)):
        inner = list(range(1, columns))
        order += [(row, column) for column in (inner if (rows - 1 - row) % 2 == 0 else inner[::-1])]
    return [row * columns + column for row, column in order]


def prep_kernel(features, order, gain, ordered, normed):
    rows = features.shape[0]
    place = lax.broadcasted_iota(jnp.int32, (rows, rows), 0)
    chosen = (place == order[...]).astype(jnp.bfloat16)
    picked = lax.dot_general(
        chosen, features[...], (((0,), (0,)), ((), ())), preferred_element_type=jnp.float32
    )
    ordered[...] = picked.astype(jnp.bfloat16)
    factor = lax.rsqrt(jnp.mean(picked * picked, axis=-1, keepdims=True) + EPS)
    normed[...] = (picked * factor * gain[...]).astype(jnp.bfloat16)


def prepare(features, order, gain):
    rows, width = features.shape
    shape = jax.ShapeDtypeStruct((rows, width), jnp.bfloat16)
    return pl.pallas_call(
        prep_kernel,
        out_shape=(shape, shape),
        compiler_params=pltpu.CompilerParams(vmem_limit_bytes=24 * MIB),
        cost_estimate=pl.CostEstimate(
            flops=2 * rows * rows * width, bytes_accessed=6 * rows * width, transcendentals=rows
        ),
        name="prepare",
    )(features, order.reshape(1, rows), gain.reshape(1, width))


def head_scale(values, head_dim, gain):
    columns = values.shape[1]
    row = lax.broadcasted_iota(jnp.int32, (columns, columns), 0) // head_dim
    column = lax.broadcasted_iota(jnp.int32, (columns, columns), 1) // head_dim
    same = (row == column).astype(jnp.bfloat16)
    sums = jnp.dot(
        (values * values).astype(jnp.bfloat16), same, preferred_element_type=jnp.float32
    )
    factor = lax.rsqrt(sums * (1.0 / head_dim) + EPS)
    return (values * factor * gain).astype(jnp.bfloat16)


def project_kernel(
    tiles, head_dim, scale, own, mate, weights, query_gain, key_gain, queries, keys, values
):
    step = pl.program_id(0)
    rows = own.shape[0]
    block = weights[...]

    @pl.when(step < tiles)
    def _():
        found = jnp.dot(own[...], block, preferred_element_type=jnp.float32)
        queries[...] = head_scale(found, head_dim, query_gain[...] * scale)

    @pl.when((step >= tiles) & (step < 2 * tiles))
    def _():
        for at, source in enumerate((own, mate)):
            found = jnp.dot(source[...], block, preferred_element_type=jnp.float32)
            keys[at * rows : (at + 1) * rows, :] = head_scale(found, head_dim, key_gain[...])

    @pl.when(step >= 2 * tiles)
    def _():
        for at, source in enumerate((own, mate)):
            found = jnp.dot(source[...], block, preferred_element_type=jnp.float32)
            values[at * rows : (at + 1) * rows, :] = found.astype(jnp.bfloat16)


def project_own(own, mate, weights, query_gain, key_gain, window_rows):
    rows, width = own.shape
    head_dim = query_gain.shape[0]
    columns = 4 * head_dim
    tiles = width // columns
    window = jax.ShapeDtypeStruct((window_rows, width), jnp.bfloat16)
    whole = pl.BlockSpec((rows, width), lambda i: (0, 0))
    gain = pl.BlockSpec((1, columns), lambda i: (0, 0))
    return pl.pallas_call(
        functools.partial(project_kernel, tiles, head_dim, 2.0 / math.sqrt(head_dim)),
        out_shape=(jax.ShapeDtypeStruct((rows, width), jnp.bfloat16), window, window),
        grid=(3 * tiles,),
        in_specs=[whole, whole, pl.BlockSpec((width, columns), lambda i: (0, i)), gain, gain],
        out_specs=(
            pl.BlockSpec((rows, columns), lambda i: (0, jnp.minimum(i, tiles - 1))),
            pl.BlockSpec((2 * rows, columns), lambda i: (0, jnp.clip(i - tiles, 0, tiles - 1))),
            pl.BlockSpec((2 * rows, columns), lambda i: (0, jnp.maximum(i - 2 * tiles, 0))),
        ),
        compiler_params=pltpu.CompilerParams(vmem_limit_bytes=24 * MIB),
        cost_estimate=pl.CostEstimate(
            flops=10 * rows * width * width,
            bytes_accessed=6 * width * width + 14 * rows * width,
            transcendentals=3 * rows * width,
        ),
        name="project_own",
    )(own, mate, weights, jnp.tile(query_gain, 4)[None], jnp.tile(key_gain, 4)[None])


def window_kernel(tiles, head_dim, count, *refs):
    sources = refs[:count]
    weights, key_gain, _, _, keys, values = refs[count:]
    step = pl.program_id(0)
    rows = sources[0].shape[0]
    block = weights[...]

    @pl.when(step < tiles)
    def _():
        for at, source in enumerate(sources):
            found = jnp.dot(source[...], block, preferred_element_type=jnp.float32)
            keys[at * rows : (at + 1) * rows, :] = head_scale(found, head_dim, key_gain[...])

    @pl.when(step >= tiles)
    def _():
        for at, source in enumerate(sources):
            found = jnp.dot(source[...], block, preferred_element_type=jnp.float32)
            values[at * rows : (at + 1) * rows, :] = found.astype(jnp.bfloat16)


def project_window(sources, first, weights, key_gain, keys, values):
    count = len(sources)
    rows, width = sources[0].shape
    head_dim = key_gain.shape[0]
    columns = 4 * head_dim
    tiles = width // columns
    at = first // count
    window = jax.ShapeDtypeStruct(keys.shape, jnp.bfloat16)
    anywhere = pl.BlockSpec(memory_space=pl.ANY)
    return pl.pallas_call(
        functools.partial(window_kernel, tiles, head_dim, count),
        out_shape=(window, window),
        grid=(2 * tiles,),
        in_specs=[pl.BlockSpec((rows, width), lambda i: (0, 0))] * count
        + [
            pl.BlockSpec((width, columns), lambda i: (0, i + tiles)),
            pl.BlockSpec((1, columns), lambda i: (0, 0)),
            anywhere,
            anywhere,
        ],
        out_specs=(
            pl.BlockSpec((count * rows, columns), lambda i: (at, jnp.minimum(i, tiles - 1))),
            pl.BlockSpec((count * rows, columns), lambda i: (at, jnp.maximum(i - tiles, 0))),
        ),
        input_output_aliases={count + 2: 0, count + 3: 1},
        compiler_params=pltpu.CompilerParams(vmem_limit_bytes=24 * MIB),
        cost_estimate=pl.CostEstimate(
            flops=4 * count * rows * width * width,
            bytes_accessed=4 * width * width + 6 * count * rows * width,
            transcendentals=count * rows * width,
        ),
        name="project_window",
    )(*sources, weights, jnp.tile(key_gain, 4)[None], keys, values)


def attend_kernel(
    axis, cycle, lists, counts, queries, keys, values, ordered, weights, gain, attended, second,
    sums, mixed,
):
    rows, width = queries.shape
    blocks = rows // BLOCK
    pairs = sums.shape[0]
    pair = width // pairs
    me = lax.axis_index(axis)
    side = 1 - 2 * lax.rem(me, 2)
    window_blocks = keys.shape[0] // BLOCK
    lane = lax.broadcasted_iota(jnp.int32, (BLOCK, pair), 1)
    low = lane < pair // 2
    key_lane = lax.broadcasted_iota(jnp.int32, (2 * BLOCK, 2 * BLOCK), 1)
    ones = jnp.ones((2 * BLOCK, pair), jnp.bfloat16)

    def place(block):
        holder = lax.div(block, blocks)
        away = lax.rem(holder - me + REACH + cycle, cycle) - REACH
        turned = away * side
        slot = jnp.where(turned > 0, 2 * turned - 1, -2 * turned)
        found = slot * blocks + lax.rem(block, blocks)
        return pl.multiple_of(jnp.clip(found, 0, window_blocks - 1) * BLOCK, BLOCK)

    for at in range(blocks):
        count = counts[at]
        here = pl.ds(at * BLOCK, BLOCK)

        def two_blocks(step, carry, at=at, count=count, here=here):
            one = pl.ds(place(lists[at, 2 * step]), BLOCK)
            other = pl.ds(place(lists[at, 2 * step + 1]), BLOCK)
            limit = jnp.where(2 * step + 1 < count, 2 * BLOCK, BLOCK)
            kept = key_lane < limit
            for index in range(pairs):
                columns = pl.ds(index * pair, pair)
                asked = queries[here, columns]
                none = jnp.zeros_like(asked)
                both = jnp.concatenate(
                    [jnp.where(low, asked, none), jnp.where(low, none, asked)], axis=0
                )
                known = jnp.concatenate([keys[one, columns], keys[other, columns]], axis=0)
                held = jnp.concatenate([values[one, columns], values[other, columns]], axis=0)
                scores = lax.dot_general(
                    both, known, (((1,), (1,)), ((), ())), preferred_element_type=jnp.float32
                )
                shares = jnp.where(kept, jnp.exp(scores), 0.0).astype(jnp.bfloat16)
                found = jnp.dot(
                    shares,
                    jnp.concatenate([held, ones], axis=1),
                    preferred_element_type=jnp.float32,
                )
                sums[index] = jnp.where(step == 0, found, sums[index] + found)
            return carry

        lax.fori_loop(0, lax.div(count + 1, 2), two_blocks, 0)
        for index in range(pairs):
            total = sums[index]
            share = total[:, :pair] / total[:, pair:]
            mixed[here, pl.ds(index * pair, pair)] = jnp.where(
                low, share[:BLOCK], share[BLOCK:]
            ).astype(jnp.bfloat16)

    product = jnp.dot(mixed[...], weights[...], preferred_element_type=jnp.float32)
    result = (ordered[...].astype(jnp.float32) + product).astype(jnp.bfloat16)
    attended[...] = result
    widened = result.astype(jnp.float32)
    factor = lax.rsqrt(jnp.mean(widened * widened, axis=-1, keepdims=True) + EPS)
    second[...] = (widened * factor * gain[...]).astype(jnp.bfloat16)


def attend(axis, cycle, lists, counts, queries, keys, values, ordered, weights, gain):
    rows, width = queries.shape
    shape = jax.ShapeDtypeStruct((rows, width), jnp.bfloat16)
    scalars = pl.BlockSpec(memory_space=pltpu.SMEM)
    local = pl.BlockSpec(memory_space=pltpu.VMEM)
    pairs = width // BLOCK
    work = 2 * rows * MAXNZ * BLOCK * width
    return pl.pallas_call(
        functools.partial(attend_kernel, axis, cycle),
        out_shape=(shape, shape),
        in_specs=[scalars, scalars] + [local] * 6,
        out_specs=(local, local),
        scratch_shapes=[
            pltpu.VMEM((pairs, 2 * BLOCK, 2 * BLOCK), jnp.float32),
            pltpu.VMEM((rows, width), jnp.bfloat16),
        ],
        compiler_params=pltpu.CompilerParams(vmem_limit_bytes=40 * MIB),
        cost_estimate=pl.CostEstimate(
            flops=4 * work + 2 * rows * width * width,
            bytes_accessed=4 * keys.size + 8 * rows * width + 2 * width * width,
            transcendentals=rows * MAXNZ * BLOCK * HEADS,
        ),
        name="attend",
    )(lists, counts, queries, keys, values, ordered, weights, gain.reshape(1, width))


def feed_kernel(steps, second, first_rows, second_rows, attended, result, total):
    step = pl.program_id(0)
    before = lax.dot_general(
        second[...], first_rows[...], (((1,), (1,)), ((), ())), preferred_element_type=jnp.float32
    )
    active = jax.nn.gelu(before, approximate=True).astype(jnp.bfloat16)
    part = jnp.dot(active, second_rows[...], preferred_element_type=jnp.float32)

    @pl.when(step == 0)
    def _():
        total[...] = part

    @pl.when(step > 0)
    def _():
        total[...] += part

    @pl.when(step == steps - 1)
    def _():
        result[...] = (attended[...].astype(jnp.float32) + total[...]).astype(jnp.bfloat16)


def feed_forward(second, first_rows, second_rows, attended):
    rows, width = second.shape
    hidden = first_rows.shape[0]
    chunk = min(512, hidden)
    steps = hidden // chunk
    whole = pl.BlockSpec((rows, width), lambda i: (0, 0))
    part = pl.BlockSpec((chunk, width), lambda i: (i, 0))
    return pl.pallas_call(
        functools.partial(feed_kernel, steps),
        out_shape=jax.ShapeDtypeStruct((rows, width), jnp.bfloat16),
        grid=(steps,),
        in_specs=[whole, part, part, whole],
        out_specs=whole,
        scratch_shapes=[pltpu.VMEM((rows, width), jnp.float32)],
        compiler_params=pltpu.CompilerParams(vmem_limit_bytes=40 * MIB),
        cost_estimate=pl.CostEstimate(
            flops=4 * rows * width * hidden,
            bytes_accessed=4 * hidden * width + 6 * rows * width,
            transcendentals=rows * hidden,
        ),
        name="feed_forward",
    )(second, first_rows, second_rows, attended)


def shards(
    pore_features,
    pore_order,
    block_lists,
    block_counts,
    norm1_gain,
    w_qkv,
    query_gain,
    key_gain,
    w_attn_out,
    norm2_gain,
    w_in,
    w_out,
):
    rows = pore_features.shape[0]
    cycle = lax.axis_size("seq")
    me = lax.axis_index("seq")

    def moved(value, where):
        return lax.ppermute(value, "seq", [(i, where(i) % cycle) for i in range(cycle)])

    def mate_of(value):
        return moved(value, lambda i: i + 1 - 2 * (i % 2))

    ring = [2 * chip + core for chip in chip_cycle(cycle // 2) for core in range(2)]
    gathered_in = lax.all_gather(w_in, "seq", axis=0, tiled=True, axis_index_groups=[ring])
    gathered_out = lax.all_gather(w_out, "seq", axis=0, tiled=True, axis_index_groups=[ring])

    ordered, normed = prepare(pore_features, pore_order - me * rows, norm1_gain)
    near = moved(normed, lambda i: i - 1 + 2 * (i % 2))
    far = moved(normed, lambda i: i + 2 - 4 * (i % 2))
    mate = mate_of(normed)
    queries, keys, values = project_own(
        normed, mate, w_qkv, query_gain, key_gain, (2 * REACH + 1) * rows
    )
    across = mate_of(near)
    keys, values = project_window([near, across], 2, w_qkv, key_gain, keys, values)
    keys, values = project_window([far], 4, w_qkv, key_gain, keys, values)
    attended, second = attend(
        "seq", cycle, block_lists, block_counts, queries, keys, values, ordered, w_attn_out,
        norm2_gain,
    )
    layer_output = feed_forward(second, gathered_in, gathered_out, attended)
    return (attended, layer_output)


def solution(mesh):
    return jax.shard_map(
        shards,
        mesh=mesh,
        in_specs=(
            P(("parts", "seq"), None),
            P(("parts", "seq")),
            P(("parts", "seq"), None),
            P(("parts", "seq")),
            P(),
            P(),
            P(),
            P(),
            P(),
            P(),
            P("seq", None),
            P("seq", None),
        ),
        out_specs=(P(("parts", "seq"), None), P(("parts", "seq"), None)),
        check_vma=False,
    )
```

time: 235 us -> 169 us (0.72)
  matrix products: 55.5 us -> 0 us
  Pallas kernels: 0 us -> 49 us
  local copies, waits for them, and re-layouts: 57.2 us -> 11.6 us
  other arithmetic: 15.8 us -> 0.69 us
  waiting for transfers between devices: 63.1 us -> 74.4 us
  starting transfers between devices: 24.9 us -> 18.9 us
  loops' own time: 2.62 us -> 0 us
    dot_general x11 -> x0, matrix products: 55.5 us -> none  [the longest x4 17.7 us: attend_group(): jnp.einsum('bqhd,bkhd->bhqk', queries, keys, preferred_element_type=jnp.f...]
    pallas_call x0 -> x6, Pallas kernels: none -> 49 us  [the longest x2 13.5 us: project_window(): pl.pallas_call(functools.partial(window_kernel, tiles, head_dim, count),...]
    all_gather x2, waiting for transfers between devices: 8.71 us -> 45.4 us  [the longest x1 45.4 us: shards(): lax.all_gather(w_out, 'seq', axis=0, tiled=True, axis_index_groups=[ring])]
    ppermute x4, waiting for transfers between devices: 53 us -> 27.6 us  [moved(): lax.ppermute(value, 'seq', [(i, where(i) % cycle) for i in range(cycle)])]
    slice x5 -> x0, local copies, waits for them, and re-layouts: 19.4 us -> none  [the longest x2 10 us: shards(): all_keys = window[:, :width].reshape(1, -1, HEADS, head_dim)]
    broadcast_in_dim x8 -> x0, local copies, waits for them, and re-layouts: 13 us -> none  [the longest x4 8.33 us: attend_group(): weights = jnp.where(keep_mask[:, None], jnp.exp(scores), 0.0)]
    mul x6 -> x0, local copies, waits for them, and re-layouts: 10.5 us -> none  [the longest x2 6.17 us: head_norm(): shaped * shaped]
    mul x2 -> x0, other arithmetic: 6.36 us -> none  [head_norm(): shaped * shaped]
  transfers between devices with their start and end apart: 6 -> 6, of which waited for: 4 -> 3; matrix products, arithmetic and copies ran while one was open for 48% -> 1% of each run, Pallas kernels for 0% -> 21%
where the time goes in v1:
time: 169 us
  waiting for transfers between devices  74.4 us (44%)
  Pallas kernels  49 us (29%)
  starting transfers between devices  18.9 us (11%)
  between operations  14.2 us (8%)
  local copies, waits for them, and re-layouts  11.6 us (7%)
    all_gather x1, waiting for transfers between devices, shards(): lax.all_gather(w_out, 'seq', axis=0, tiled=True, axis_index_groups=[ring])  45.4 us
    ppermute x4, waiting for transfers between devices, moved(): lax.ppermute(value, 'seq', [(i, where(i) % cycle) for i in range(cycle)])  27.6 us
    ppermute x4, starting transfers between devices, moved(): lax.ppermute(value, 'seq', [(i, where(i) % cycle) for i in range(cycle)])  18.8 us
    pallas_call x2, Pallas kernels, project_window(): pl.pallas_call(functools.partial(window_kernel, tiles, head_dim, count),...  13.5 us
    pallas_call x1, Pallas kernels, feed_forward(): pl.pallas_call(functools.partial(feed_kernel, steps), out_shape=jax.Shape...  13 us
    pallas_call x1, Pallas kernels, project_own(): pl.pallas_call(functools.partial(project_kernel, tiles, head_dim, 2.0 / m...  12.9 us
    unnamed x24, local copies, waits for them, and re-layouts  10.1 us
    pallas_call x1, Pallas kernels, attend(): pl.pallas_call(functools.partial(attend_kernel, axis, cycle), out_shape=(...  8.9 us
  transfers between devices with their start and end apart: 6, of which 3 were waited for; matrix products, arithmetic and copies ran while one was open for 1% of the time, Pallas kernels for 21%

profile of v1, /device:TPU:0, one launch (start us, length us, event | category | flops | bytes accessed | tf_op | source)
XLA Modules:
  0.0 168.7 jit_solution(9436352645418237271)
XLA Ops:
  7.2 0.7 all-gather.3.cloned.1.call-update
  7.9 0.7 all-gather.5.cloned.1.call-update
  8.7 0.7 broadcast_subtract_fusion
  9.3 1.1 copy-done.4
  10.5 0.7 copy-done.5
  11.2 0.7 prepare.1
  11.9 0.9 copy-done.10
  12.8 5.4 %collective-permute-start.2 = (bf16[384,1024]{1,0:T(8,128)(2,1)S(1)}, bf16[384,1024]{1,0:T(8,128)(2,1)S(1)}, u32[]{:S(2)}, u32[]{:S(2)}) collective-permute-start(bf16[384,1024]{1,0:T(8,128)(2,1)S(1)} %get-tuple-element.13.own), channel_id=1, source_target_pairs={{0,15},{1,2},{2,1},{3,4},{4,3},{5,6},{6,5},{7,8},{8,7},{9,10},{10,... | collective-permute-start | bytes 2359304 | tf_op jit(solution)/shard_map/ppermute | solution.py:341
  18.2 18.7 %collective-permute-done.2.refs_0_ = bf16[384,1024]{1,0:T(8,128)(2,1)S(1)} collective-permute-done((bf16[384,1024]{1,0:T(8,128)(2,1)S(1)}, bf16[384,1024]{1,0:T(8,128)(2,1)S(1)}, u32[]{:S(2)}, u32[]{:S(2)}) %collective-permute-start.2) | collective-permute-done | bytes 786464 | tf_op jit(solution)/shard_map/ppermute | solution.py:341
  37.0 11.0 %collective-permute-start.3 = (bf16[384,1024]{1,0:T(8,128)(2,1)S(1)}, bf16[384,1024]{1,0:T(8,128)(2,1)S(1)}, u32[]{:S(2)}, u32[]{:S(2)}) collective-permute-start(bf16[384,1024]{1,0:T(8,128)(2,1)S(1)} %collective-permute-done.2.refs_0_), channel_id=1, source_target_pairs={{0,1},{1,0},{2,3},{3,2},{4,5},{5,4},{6,7},{7,6},{8,9},{9,8},{10,11... | collective-permute-start | bytes 2359304 | tf_op jit(solution)/shard_map/ppermute | solution.py:341
  47.9 2.4 %collective-permute-start.1 = (bf16[384,1024]{1,0:T(8,128)(2,1)S(1)}, bf16[384,1024]{1,0:T(8,128)(2,1)S(1)}, u32[]{:S(2)}, u32[]{:S(2)}) collective-permute-start(bf16[384,1024]{1,0:T(8,128)(2,1)S(1)} %get-tuple-element.13.own), channel_id=1, source_target_pairs={{0,2},{1,15},{2,4},{3,1},{4,6},{5,3},{6,8},{7,5},{8,10},{9,7},{10,... | collective-permute-start | bytes 2359304 | tf_op jit(solution)/shard_map/ppermute | solution.py:341
  50.3 0.7 tile.4
  51.0 0.1 broadcast_in_dim_tile.8.query_gain
  51.0 0.7 tile.5
  51.8 2.9 %copy-done = bf16[1024,3072]{1,0:T(8,128)(2,1)S(1)} copy-done((bf16[1024,3072]{1,0:T(8,128)(2,1)S(1)}, bf16[1024,3072]{1,0:T(8,128)(2,1)}, u32[]{:S(2)}) %copy-start) | copy-done | bytes 6291480
  54.7 12.9 %project_own.1 = (bf16[384,1024]{1,0:T(8,128)(2,1)S(1)}, bf16[1920,1024]{1,0:T(8,128)(2,1)S(1)}, bf16[1920,1024]{1,0:T(8,128)(2,1)S(1)}) custom-call(bf16[384,1024]{1,0:T(8,128)(2,1)S(1)} %get-tuple-element.13.own, bf16[384,1024]{1,0:T(8,128)(2,1)} %collective-permute-done.mate, bf16[1024,3072]{1,0:T(8,128)(2,1)S(1)} %copy-done, ...), custom_call_target="tpu_custom_call" | custom-call | flops 4026531840 | bytes 11796480 | tf_op jit(solution)/shard_map/project_own/pallas_call | solution.py:106
  67.6 8.6 %project_window.2 = (bf16[1920,1024]{1,0:T(8,128)(2,1)S(1)}, bf16[1920,1024]{1,0:T(8,128)(2,1)S(1)}) custom-call(bf16[384,1024]{1,0:T(8,128)(2,1)S(1)} %collective-permute-done.2.refs_0_, bf16[384,1024]{1,0:T(8,128)(2,1)S(1)} %collective-permute-done.3.refs_1_, bf16[1024,3072]{1,0:T(8,128)(2,1)S(1)} %copy-done.1, ...), custom_call_target="tpu_custom_call", output_to_operand_aliasing={{0}: (4, {}), {1}: (5, {})} | custom-call | flops 3221225472 | bytes 8912896 | tf_op jit(solution)/shard_map/project_window/pallas_call | solution.py:155
  76.2 8.9 %collective-permute-done.1.refs_0_ = bf16[384,1024]{1,0:T(8,128)(2,1)S(1)} collective-permute-done((bf16[384,1024]{1,0:T(8,128)(2,1)S(1)}, bf16[384,1024]{1,0:T(8,128)(2,1)S(1)}, u32[]{:S(2)}, u32[]{:S(2)}) %collective-permute-start.1) | collective-permute-done | bytes 786464 | tf_op jit(solution)/shard_map/ppermute | solution.py:341
  85.1 4.9 %project_window.3 = (bf16[1920,1024]{1,0:T(8,128)(2,1)S(1)}, bf16[1920,1024]{1,0:T(8,128)(2,1)S(1)}) custom-call(bf16[384,1024]{1,0:T(8,128)(2,1)S(1)} %collective-permute-done.1.refs_0_, bf16[1024,3072]{1,0:T(8,128)(2,1)S(1)} %copy-done.1, f32[1,256]{1,0:T(1,128)S(1)} %broadcast_in_dim_tile.9.key_gain.refs_3_.refs_2_, ...), custom_call_target="tpu_custom_call", output_to_operand_aliasing={{0}: (3, {}), {1}: (4, {})} | custom-call | flops 1610612736 | bytes 6553600 | tf_op jit(solution)/shard_map/project_window/pallas_call | solution.py:155
  90.1 8.9 %attend.1 = (bf16[384,1024]{1,0:T(8,128)(2,1)}, bf16[384,1024]{1,0:T(8,128)(2,1)S(1)}) custom-call(s32[3,8]{1,0:T(4,128)S(1)} %copy-done.7, s32[3]{0:T(128)S(1)} %copy-done.8, bf16[384,1024]{1,0:T(8,128)(2,1)S(1)} %get-tuple-element.14.queries, bf16[1920,1024]{1,0:T(8,128)(2,1)S(1)} %get-tuple-element.19.keys, ...), custom_call_target="tpu_custom_call" | custom-call | flops 4026531840 | bytes 13107200 | tf_op jit(solution)/shard_map/attend/pallas_call | solution.py:258
  99.0 45.4 %all-gather.5.cloned.1.call-done.second_rows = bf16[4096,1024]{1,0:T(8,128)(2,1)} async-done(((bf16[256,1024]{1,0:T(8,128)(2,1)}), bf16[4096,1024]{1,0:T(8,128)(2,1)}) %all-gather.5.cloned.1.call-update) | async-done | bytes 8388624 | tf_op jit(solution)/shard_map/all_gather | solution.py:348
  144.4 3.4 %copy-done.2 = bf16[4096,1024]{1,0:T(8,128)(2,1)S(1)} copy-done((bf16[4096,1024]{1,0:T(8,128)(2,1)S(1)}, bf16[4096,1024]{1,0:T(8,128)(2,1)}, u32[]{:S(2)}) %copy-start.2) | copy-done | bytes 8388632
  147.7 1.1 copy-done.9
  148.9 13.0 %feed_forward.1 = bf16[384,1024]{1,0:T(8,128)(2,1)} custom-call(bf16[384,1024]{1,0:T(8,128)(2,1)S(1)} %get-tuple-element.23.second, bf16[4096,1024]{1,0:T(8,128)(2,1)S(1)} %copy-done.2, bf16[4096,1024]{1,0:T(8,128)(2,1)} %all-gather.5.cloned.1.call-done.second_rows, bf16[384,1024]{1,0:T(8,128)(2,1)S(1)} %copy-done.9), custom_call_target="tpu_custom_call" | custom-call | flops 6442450944 | bytes 19136512 | tf_op jit(solution)/shard_map/feed_forward/pallas_call | solution.py:305
  (26 shorter events, 0.2 us)
Async XLA Ops:
  7.2 91.8 %all-gather.3.cloned.1.call-start = ((), (), s32[]{:S(2)}) async-start(), calls=%async_computation | async-start | bytes 8912896 | tf_op jit(solution)/shard_map/all_gather | solution.py:347
  7.9 136.5 %all-gather.5.cloned.1.call-start = ((), (), s32[]{:S(2)}) async-start(), calls=%async_computation.1 | async-start | bytes 8912896 | tf_op jit(solution)/shard_map/all_gather | solution.py:348
  9.3 1.1 copy-start.4
  10.5 0.7 copy-start.5
  11.9 0.9 copy-start.10
  12.8 24.2 %collective-permute-start.2 = (bf16[384,1024]{1,0:T(8,128)(2,1)S(1)}, bf16[384,1024]{1,0:T(8,128)(2,1)S(1)}, u32[]{:S(2)}, u32[]{:S(2)}) collective-permute-start(bf16[384,1024]{1,0:T(8,128)(2,1)S(1)} %get-tuple-element.13.own), channel_id=1, source_target_pairs={{0,15},{1,2},{2,1},{3,4},{4,3},{5,6},{6,5},{7,8},{8,7},{9,10},{10,... | collective-permute-start | bytes 2359304 | tf_op jit(solution)/shard_map/ppermute | solution.py:341
  18.2 33.5 %collective-permute-start = (bf16[384,1024]{1,0:T(8,128)(2,1)S(1)}, bf16[384,1024]{1,0:T(8,128)(2,1)}, u32[]{:S(2)}, u32[]{:S(2)}) collective-permute-start(bf16[384,1024]{1,0:T(8,128)(2,1)S(1)} %get-tuple-element.13.own), channel_id=1, source_target_pairs={{0,1},{1,0},{2,3},{3,2},{4,5},{5,4},{6,7},{7,6},{8,9},{9,8},{10,11... | collective-permute-start | bytes 2359304 | tf_op jit(solution)/shard_map/ppermute | solution.py:341
  37.0 30.6 %collective-permute-start.3 = (bf16[384,1024]{1,0:T(8,128)(2,1)S(1)}, bf16[384,1024]{1,0:T(8,128)(2,1)S(1)}, u32[]{:S(2)}, u32[]{:S(2)}) collective-permute-start(bf16[384,1024]{1,0:T(8,128)(2,1)S(1)} %collective-permute-done.2.refs_0_), channel_id=1, source_target_pairs={{0,1},{1,0},{2,3},{3,2},{4,5},{5,4},{6,7},{7,6},{8,9},{9,8},{10,11... | collective-permute-start | bytes 2359304 | tf_op jit(solution)/shard_map/ppermute | solution.py:341
  47.9 37.1 %collective-permute-start.1 = (bf16[384,1024]{1,0:T(8,128)(2,1)S(1)}, bf16[384,1024]{1,0:T(8,128)(2,1)S(1)}, u32[]{:S(2)}, u32[]{:S(2)}) collective-permute-start(bf16[384,1024]{1,0:T(8,128)(2,1)S(1)} %get-tuple-element.13.own), channel_id=1, source_target_pairs={{0,2},{1,15},{2,4},{3,1},{4,6},{5,3},{6,8},{7,5},{8,10},{9,7},{10,... | collective-permute-start | bytes 2359304 | tf_op jit(solution)/shard_map/ppermute | solution.py:341
  51.8 2.9 %copy-start = (bf16[1024,3072]{1,0:T(8,128)(2,1)S(1)}, bf16[1024,3072]{1,0:T(8,128)(2,1)}, u32[]{:S(2)}) copy-start(bf16[1024,3072]{1,0:T(8,128)(2,1)} %refs_1_.1) | copy-start | bytes 18874372
  54.7 12.9 %copy-start.1 = (bf16[1024,3072]{1,0:T(8,128)(2,1)S(1)}, bf16[1024,3072]{1,0:T(8,128)(2,1)}, u32[]{:S(2)}) copy-start(bf16[1024,3072]{1,0:T(8,128)(2,1)} %refs_1_.1) | copy-start | bytes 18874372
  85.1 5.0 %copy-start.3 = (bf16[1024,1024]{1,0:T(8,128)(2,1)S(1)}, bf16[1024,1024]{1,0:T(8,128)(2,1)}, u32[]{:S(2)}) copy-start(bf16[1024,1024]{1,0:T(8,128)(2,1)} %weights.3) | copy-start | bytes 6291460
  85.1 5.0 %copy-start.6 = (f32[1024]{0:T(1024)S(1)}, f32[1024]{0:T(1024)}, u32[]{:S(2)}) copy-start(f32[1024]{0:T(1024)} %param.21) | copy-start | bytes 12292
  85.1 5.0 %copy-start.7 = (s32[3,8]{1,0:T(4,128)S(1)}, s32[3,8]{1,0:T(4,128)}, u32[]{:S(2)}) copy-start(s32[3,8]{1,0:T(4,128)} %lists.1) | copy-start | bytes 292
  85.1 5.0 %copy-start.8 = (s32[3]{0:T(128)S(1)}, s32[3]{0:T(128)}, u32[]{:S(2)}) copy-start(s32[3]{0:T(128)} %counts.1) | copy-start | bytes 40
  85.1 5.0 %copy-start.11 = (bf16[384,1024]{1,0:T(8,128)(2,1)S(1)}, bf16[384,1024]{1,0:T(8,128)(2,1)}, u32[]{:S(2)}) copy-start(bf16[384,1024]{1,0:T(8,128)(2,1)} %copy-done.10) | copy-start | bytes 2359300
  144.4 3.4 %copy-start.2 = (bf16[4096,1024]{1,0:T(8,128)(2,1)S(1)}, bf16[4096,1024]{1,0:T(8,128)(2,1)}, u32[]{:S(2)}) copy-start(bf16[4096,1024]{1,0:T(8,128)(2,1)} %all-gather.3.cloned.1.call-done.first_rows) | copy-start | bytes 25165828
  147.7 1.1 copy-start.9
Sparse Core Ops, SparseCore 0:
  9.6 82.3 all-gather.2
  93.6 50.7 all-gather.4

commit v2 on v1

--- a/solution.py
+++ b/solution.py
@@ -70,125 +70,80 @@
     return (values * factor * gain).astype(jnp.bfloat16)
 
 
-def project_kernel(
-    tiles, head_dim, scale, own, mate, weights, query_gain, key_gain, queries, keys, values
-):
+def project_kernel(tiles, head_dim, scale, source, weights, query_gain, key_gain, *outs):
     step = pl.program_id(0)
-    rows = own.shape[0]
-    block = weights[...]
-
-    @pl.when(step < tiles)
+    queries, key_values = outs if len(outs) == 2 else (None, outs[0])
+    first = tiles if queries is not None else 0
+    found = jnp.dot(source[...], weights[...], preferred_element_type=jnp.float32)
+
+    if queries is not None:
+
+        @pl.when(step < tiles)
+        def _():
+            queries[...] = head_scale(found, head_dim, query_gain[...] * scale)
+
+    @pl.when((step >= first) & (step < first + tiles))
     def _():
-        found = jnp.dot(own[...], block, preferred_element_type=jnp.float32)
-        queries[...] = head_scale(found, head_dim, query_gain[...] * scale)
-
-    @pl.when((step >= tiles) & (step < 2 * tiles))
+        key_values[...] = head_scale(found, head_dim, key_gain[...])
+
+    @pl.when(step >= first + tiles)
     def _():
-        for at, source in enumerate((own, mate)):
-            found = jnp.dot(source[...], block, preferred_element_type=jnp.float32)
-            keys[at * rows : (at + 1) * rows, :] = head_scale(found, head_dim, key_gain[...])
-
-    @pl.when(step >= 2 * tiles)
-    def _():
-        for at, source in enumerate((own, mate)):
-            found = jnp.dot(source[...], block, preferred_element_type=jnp.float32)
-            values[at * rows : (at + 1) * rows, :] = found.astype(jnp.bfloat16)
-
-
-def project_own(own, mate, weights, query_gain, key_gain, window_rows):
-    rows, width = own.shape
+        key_values[...] = found.astype(jnp.bfloat16)
+
+
+def project(source, weights, query_gain, key_gain, with_queries):
+    rows, width = source.shape
     head_dim = query_gain.shape[0]
     columns = 4 * head_dim
     tiles = width // columns
-    window = jax.ShapeDtypeStruct((window_rows, width), jnp.bfloat16)
-    whole = pl.BlockSpec((rows, width), lambda i: (0, 0))
+    skipped = 0 if with_queries else tiles
+    steps = 3 * tiles - skipped
     gain = pl.BlockSpec((1, columns), lambda i: (0, 0))
+    shapes = [jax.ShapeDtypeStruct((rows, 2 * width), jnp.bfloat16)]
+    specs = [pl.BlockSpec((rows, columns), lambda i: (0, jnp.maximum(i - tiles + skipped, 0)))]
+    if with_queries:
+        shapes.insert(0, jax.ShapeDtypeStruct((rows, width), jnp.bfloat16))
+        specs.insert(0, pl.BlockSpec((rows, columns), lambda i: (0, jnp.minimum(i, tiles - 1))))
     return pl.pallas_call(
         functools.partial(project_kernel, tiles, head_dim, 2.0 / math.sqrt(head_dim)),
-        out_shape=(jax.ShapeDtypeStruct((rows, width), jnp.bfloat16), window, window),
-        grid=(3 * tiles,),
-        in_specs=[whole, whole, pl.BlockSpec((width, columns), lambda i: (0, i)), gain, gain],
-        out_specs=(
-            pl.BlockSpec((rows, columns), lambda i: (0, jnp.minimum(i, tiles - 1))),
-            pl.BlockSpec((2 * rows, columns), lambda i: (0, jnp.clip(i - tiles, 0, tiles - 1))),
-            pl.BlockSpec((2 * rows, columns), lambda i: (0, jnp.maximum(i - 2 * tiles, 0))),
-        ),
-        compiler_params=pltpu.CompilerParams(vmem_limit_bytes=24 * MIB),
+        out_shape=shapes,
+        grid=(steps,),
+        in_specs=[
+            pl.BlockSpec((rows, width), lambda i: (0, 0)),
+            pl.BlockSpec((width, columns), lambda i: (0, i + skipped)),
+            gain,
+            gain,
+        ],
+        out_specs=specs,
+        compiler_params=pltpu.CompilerParams(vmem_limit_bytes=16 * MIB),
         cost_estimate=pl.CostEstimate(
-            flops=10 * rows * width * width,
-            bytes_accessed=6 * width * width + 14 * rows * width,
-            transcendentals=3 * rows * width,
-        ),
-        name="project_own",
-    )(own, mate, weights, jnp.tile(query_gain, 4)[None], jnp.tile(key_gain, 4)[None])
-
-
-def window_kernel(tiles, head_dim, count, *refs):
-    sources = refs[:count]
-    weights, key_gain, _, _, keys, values = refs[count:]
-    step = pl.program_id(0)
-    rows = sources[0].shape[0]
-    block = weights[...]
-
-    @pl.when(step < tiles)
-    def _():
-        for at, source in enumerate(sources):
-            found = jnp.dot(source[...], block, preferred_element_type=jnp.float32)
-            keys[at * rows : (at + 1) * rows, :] = head_scale(found, head_dim, key_gain[...])
-
-    @pl.when(step >= tiles)
-    def _():
-        for at, source in enumerate(sources):
-            found = jnp.dot(source[...], block, preferred_element_type=jnp.float32)
-            values[at * rows : (at + 1) * rows, :] = found.astype(jnp.bfloat16)
-
-
-def project_window(sources, first, weights, key_gain, keys, values):
-    count = len(sources)
-    rows, width = sources[0].shape
-    head_dim = key_gain.shape[0]
-    columns = 4 * head_dim
-    tiles = width // columns
-    at = first // count
-    window = jax.ShapeDtypeStruct(keys.shape, jnp.bfloat16)
-    anywhere = pl.BlockSpec(memory_space=pl.ANY)
-    return pl.pallas_call(
-        functools.partial(window_kernel, tiles, head_dim, count),
-        out_shape=(window, window),
-        grid=(2 * tiles,),
-        in_specs=[pl.BlockSpec((rows, width), lambda i: (0, 0))] * count
-        + [
-            pl.BlockSpec((width, columns), lambda i: (0, i + tiles)),
-            pl.BlockSpec((1, columns), lambda i: (0, 0)),
-            anywhere,
-            anywhere,
-        ],
-        out_specs=(
-            pl.BlockSpec((count * rows, columns), lambda i: (at, jnp.minimum(i, tiles - 1))),
-            pl.BlockSpec((count * rows, columns), lambda i: (at, jnp.maximum(i - tiles, 0))),
-        ),
-        input_output_aliases={count + 2: 0, count + 3: 1},
-        compiler_params=pltpu.CompilerParams(vmem_limit_bytes=24 * MIB),
-        cost_estimate=pl.CostEstimate(
-            flops=4 * count * rows * width * width,
-            bytes_accessed=4 * width * width + 6 * count * rows * width,
-            transcendentals=count * rows * width,
-        ),
-        name="project_window",
-    )(*sources, weights, jnp.tile(key_gain, 4)[None], keys, values)
+            flops=2 * rows * width * columns * steps,
+            bytes_accessed=2 * width * columns * steps + 8 * rows * width,
+            transcendentals=rows * width,
+        ),
+        name="project",
+    )(source, weights, jnp.tile(query_gain, 4)[None], jnp.tile(key_gain, 4)[None])
 
 
 def attend_kernel(
-    axis, cycle, lists, counts, queries, keys, values, ordered, weights, gain, attended, second,
-    sums, mixed,
+    axis, cycle, lists, counts, queries, own, mate, near, across, far, ordered, weights, gain,
+    attended, second, sums, mixed, window, arrived,
 ):
     rows, width = queries.shape
+    copies = [
+        pltpu.make_async_copy(source, window.at[pl.ds(slot * rows, rows)], arrived.at[slot])
+        for slot, source in enumerate((own, mate, near, across, far))
+    ]
+    for copy in copies:
+        copy.start()
+    for copy in copies:
+        copy.wait()
     blocks = rows // BLOCK
     pairs = sums.shape[0]
     pair = width // pairs
     me = lax.axis_index(axis)
     side = 1 - 2 * lax.rem(me, 2)
-    window_blocks = keys.shape[0] // BLOCK
+    window_blocks = window.shape[0] // BLOCK
     lane = lax.broadcasted_iota(jnp.int32, (BLOCK, pair), 1)
     low = lane < pair // 2
     key_lane = lax.broadcasted_iota(jnp.int32, (2 * BLOCK, 2 * BLOCK), 1)
@@ -218,8 +173,9 @@
                 both = jnp.concatenate(
                     [jnp.where(low, asked, none), jnp.where(low, none, asked)], axis=0
                 )
-                known = jnp.concatenate([keys[one, columns], keys[other, columns]], axis=0)
-                held = jnp.concatenate([values[one, columns], values[other, columns]], axis=0)
+                known = jnp.concatenate([window[one, columns], window[other, columns]], axis=0)
+                later = pl.ds(width + index * pair, pair)
+                held = jnp.concatenate([window[one, later], window[other, later]], axis=0)
                 scores = lax.dot_general(
                     both, known, (((1,), (1,)), ((), ())), preferred_element_type=jnp.float32
                 )
@@ -248,30 +204,84 @@
     second[...] = (widened * factor * gain[...]).astype(jnp.bfloat16)
 
 
-def attend(axis, cycle, lists, counts, queries, keys, values, ordered, weights, gain):
+def attend(axis, cycle, lists, counts, queries, sources, ordered, weights, gain):
     rows, width = queries.shape
     shape = jax.ShapeDtypeStruct((rows, width), jnp.bfloat16)
     scalars = pl.BlockSpec(memory_space=pltpu.SMEM)
     local = pl.BlockSpec(memory_space=pltpu.VMEM)
+    anywhere = pl.BlockSpec(memory_space=pl.ANY)
     pairs = width // BLOCK
+    slots = len(sources)
     work = 2 * rows * MAXNZ * BLOCK * width
     return pl.pallas_call(
         functools.partial(attend_kernel, axis, cycle),
         out_shape=(shape, shape),
-        in_specs=[scalars, scalars] + [local] * 6,
+        in_specs=[scalars, scalars, local] + [anywhere] * slots + [local] * 3,
         out_specs=(local, local),
         scratch_shapes=[
             pltpu.VMEM((pairs, 2 * BLOCK, 2 * BLOCK), jnp.float32),
             pltpu.VMEM((rows, width), jnp.bfloat16),
+            pltpu.VMEM((slots * rows, 2 * width), jnp.bfloat16),
+            pltpu.SemaphoreType.DMA((slots,)),
         ],
-        compiler_params=pltpu.CompilerParams(vmem_limit_bytes=40 * MIB),
+        compiler_params=pltpu.CompilerParams(vmem_limit_bytes=32 * MIB),
         cost_estimate=pl.CostEstimate(
             flops=4 * work + 2 * rows * width * width,
-            bytes_accessed=4 * keys.size + 8 * rows * width + 2 * width * width,
+            bytes_accessed=4 * slots * rows * width + 8 * rows * width + 2 * width * width,
             transcendentals=rows * MAXNZ * BLOCK * HEADS,
         ),
         name="attend",
-    )(lists, counts, queries, keys, values, ordered, weights, gain.reshape(1, width))
+    )(lists, counts, queries, *sources, ordered, weights, gain.reshape(1, width))
+
+
+def pieces_kernel(axis, swaps, has_base, *refs):
+    count = len(swaps)
+    second = refs[0]
+    firsts = refs[1 : 1 + count]
+    seconds = refs[1 + count : 1 + 2 * count]
+    base = refs[1 + 2 * count] if has_base else None
+    result = refs[-1]
+    straight = lax.axis_index(axis) == 0
+    rows = second[...]
+    total = base[...] if has_base else None
+    for index, swapped in enumerate(swaps):
+        first_rows, second_rows = firsts[index][...], seconds[index][...]
+        if swapped:
+            first_rows, second_rows = (
+                jnp.where(straight, first_rows, second_rows),
+                jnp.where(straight, second_rows, first_rows),
+            )
+        before = lax.dot_general(
+            rows, first_rows, (((1,), (1,)), ((), ())), preferred_element_type=jnp.float32
+        )
+        active = jax.nn.gelu(before, approximate=True).astype(jnp.bfloat16)
+        part = jnp.dot(active, second_rows, preferred_element_type=jnp.float32)
+        total = part if total is None else total + part
+    result[...] = total.astype(result.dtype)
+
+
+def feed_pieces(axis, second, pieces, base, dtype):
+    rows, width = second.shape
+    hidden = sum(piece[0].shape[0] for piece in pieces)
+    operands = [second] + [piece[0] for piece in pieces] + [piece[1] for piece in pieces]
+    if base is not None:
+        operands.append(base)
+    local = pl.BlockSpec(memory_space=pltpu.VMEM)
+    return pl.pallas_call(
+        functools.partial(
+            pieces_kernel, axis, tuple(piece[2] for piece in pieces), base is not None
+        ),
+        out_shape=jax.ShapeDtypeStruct((rows, width), dtype),
+        in_specs=[local] * len(operands),
+        out_specs=local,
+        compiler_params=pltpu.CompilerParams(vmem_limit_bytes=32 * MIB),
+        cost_estimate=pl.CostEstimate(
+            flops=4 * rows * width * hidden,
+            bytes_accessed=4 * hidden * width + 8 * rows * width,
+            transcendentals=rows * hidden,
+        ),
+        name="feed_pieces",
+    )(*operands)
 
 
 def feed_kernel(steps, second, first_rows, second_rows, attended, result, total):
@@ -343,25 +353,64 @@
     def mate_of(value):
         return moved(value, lambda i: i + 1 - 2 * (i % 2))
 
-    ring = [2 * chip + core for chip in chip_cycle(cycle // 2) for core in range(2)]
-    gathered_in = lax.all_gather(w_in, "seq", axis=0, tiled=True, axis_index_groups=[ring])
-    gathered_out = lax.all_gather(w_out, "seq", axis=0, tiled=True, axis_index_groups=[ring])
+    chip_rows, chip_columns = chip_grid(cycle // 2)
+    shared = (chip_rows, chip_columns) == (4, 2) and lax.axis_size("parts") == 2
+    lane = 2 * chip_columns
+
+    def along(value, targets):
+        pairs = [(lane * a + k, lane * b + k) for a, b in targets for k in range(lane)]
+        return lax.ppermute(value, "seq", pairs)
+
+    def beside(value):
+        return moved(value, lambda i: i + 2 - 4 * (i // 2 % 2))
+
+    def over(value):
+        return lax.ppermute(value, "parts", [(0, 1), (1, 0)])
 
     ordered, normed = prepare(pore_features, pore_order - me * rows, norm1_gain)
     near = moved(normed, lambda i: i - 1 + 2 * (i % 2))
     far = moved(normed, lambda i: i + 2 - 4 * (i % 2))
-    mate = mate_of(normed)
-    queries, keys, values = project_own(
-        normed, mate, w_qkv, query_gain, key_gain, (2 * REACH + 1) * rows
+
+    if shared:
+        row = me // lane
+        inner = (row == 1) | (row == 2)
+        prime = jnp.where(lax.axis_index("parts") == 0, w_in, w_out)
+        pair_rows = along(prime, [(0, 1), (1, 0), (2, 3), (3, 2)])
+        inner_own = along(prime, [(1, 2), (2, 1)])
+        inner_pair = along(pair_rows, [(1, 2), (2, 1)])
+        outer_own = along(inner_own, [(1, 0), (2, 3)])
+        outer_pair = along(inner_pair, [(1, 0), (2, 3)])
+        third = jnp.where(inner, inner_own, outer_own)
+        fourth = jnp.where(inner, inner_pair, outer_pair)
+        pieces = [(w_in, w_out, False), (mate_of(w_in), mate_of(w_out), False)]
+        for prime_rows in (pair_rows, third, fourth):
+            other_rows = over(prime_rows)
+            pieces.append((prime_rows, other_rows, True))
+            pieces.append((mate_of(prime_rows), mate_of(other_rows), True))
+
+    queries, own_kv = project(normed, w_qkv, query_gain, key_gain, True)
+    mate_kv = mate_of(own_kv)
+    (near_kv,) = project(near, w_qkv, query_gain, key_gain, False)
+    across_kv = mate_of(near_kv)
+    (far_kv,) = project(far, w_qkv, query_gain, key_gain, False)
+    attended, second = attend(
+        "seq", cycle, block_lists, block_counts, queries,
+        [own_kv, mate_kv, near_kv, across_kv, far_kv], ordered, w_attn_out, norm2_gain,
     )
-    across = mate_of(near)
-    keys, values = project_window([near, across], 2, w_qkv, key_gain, keys, values)
-    keys, values = project_window([far], 4, w_qkv, key_gain, keys, values)
-    attended, second = attend(
-        "seq", cycle, block_lists, block_counts, queries, keys, values, ordered, w_attn_out,
-        norm2_gain,
-    )
-    layer_output = feed_forward(second, gathered_in, gathered_out, attended)
+    if shared:
+        guest = beside(second)
+        early = feed_pieces("parts", second, pieces[:6], None, jnp.float32)
+        guest_part = feed_pieces("parts", guest, pieces, None, jnp.bfloat16)
+        returned = beside(guest_part)
+        own_part = feed_pieces("parts", second, pieces[6:], early, jnp.float32)
+        layer_output = (
+            attended.astype(jnp.float32) + own_part + returned.astype(jnp.float32)
+        ).astype(jnp.bfloat16)
+    else:
+        ring = [2 * chip + core for chip in chip_cycle(cycle // 2) for core in range(2)]
+        gathered_in = lax.all_gather(w_in, "seq", axis=0, tiled=True, axis_index_groups=[ring])
+        gathered_out = lax.all_gather(w_out, "seq", axis=0, tiled=True, axis_index_groups=[ring])
+        layer_output = feed_forward(second, gathered_in, gathered_out, attended)
     return (attended, layer_output)
 
 

time: 169 us -> 139 us (0.82)
  waiting for transfers between devices: 74.4 us -> 57.3 us
  between operations: 14.2 us -> 0.93 us
  other arithmetic: 0.69 us -> 6.2 us
  Pallas kernels: 49 us -> 43.7 us
  local copies, waits for them, and re-layouts: 11.6 us -> 8.54 us
  starting transfers between devices: 18.9 us -> 21.9 us
    all_gather x2 -> x0, waiting for transfers between devices: 45.4 us -> none  [the longest x1 45.4 us: shards(): lax.all_gather(w_out, 'seq', axis=0, tiled=True, axis_index_groups=[ring])]
    ppermute x0 -> x8, waiting for transfers between devices: none -> 28.9 us  [the longest x3 19 us: over(): return lax.ppermute(value, 'parts', [(0, 1), (1, 0)])]
    ppermute x0 -> x8, starting transfers between devices: none -> 9.08 us  [the longest x5 5.49 us: along(): return lax.ppermute(value, 'seq', pairs)]
    pallas_call x4 -> x6, Pallas kernels: 39.4 us -> 30.8 us  [the longest x3 19.9 us: project(): pl.pallas_call(functools.partial(project_kernel, tiles, head_dim, 2.0 / m...]
    ppermute x4 -> x14, starting transfers between devices: 18.8 us -> 12.9 us  [moved(): lax.ppermute(value, 'seq', [(i, where(i) % cycle) for i in range(cycle)])]
    select_n x0 -> x3, other arithmetic: none -> 4.27 us  [the longest x1 1.9 us: shards(): prime = jnp.where(lax.axis_index('parts') == 0, w_in, w_out)]
    pallas_call x1, Pallas kernels: 8.9 us -> 11.3 us  [attend(): pl.pallas_call(functools.partial(attend_kernel, axis, cycle), out_shape=(...]
    unnamed x24 -> x36, local copies, waits for them, and re-layouts: 10.1 us -> 8.36 us
  transfers between devices with their start and end apart: 6 -> 22, of which waited for: 3 -> 6; matrix products, arithmetic and copies ran while one was open for 1% -> 3% of each run, Pallas kernels for 21% -> 27%
where the time goes in v2:
time: 139 us
  waiting for transfers between devices  57.3 us (41%)
  Pallas kernels  43.7 us (31%)
  starting transfers between devices  21.9 us (16%)
  local copies, waits for them, and re-layouts  8.54 us (6%)
  other arithmetic  6.2 us (4%)
    ppermute x14, waiting for transfers between devices, moved(): lax.ppermute(value, 'seq', [(i, where(i) % cycle) for i in range(cycle)])  28.4 us
    pallas_call x3, Pallas kernels, project(): pl.pallas_call(functools.partial(project_kernel, tiles, head_dim, 2.0 / m...  19.9 us
    ppermute x3, waiting for transfers between devices, over(): return lax.ppermute(value, 'parts', [(0, 1), (1, 0)])  19 us
    ppermute x14, starting transfers between devices, moved(): lax.ppermute(value, 'seq', [(i, where(i) % cycle) for i in range(cycle)])  12.9 us
    pallas_call x1, Pallas kernels, attend(): pl.pallas_call(functools.partial(attend_kernel, axis, cycle), out_shape=(...  11.3 us
    pallas_call x3, Pallas kernels, feed_pieces(): pl.pallas_call(functools.partial(pieces_kernel, axis, tuple((piece[2] for...  10.9 us
    ppermute x5, waiting for transfers between devices, along(): return lax.ppermute(value, 'seq', pairs)  9.9 us
    unnamed x36, local copies, waits for them, and re-layouts  8.36 us
  transfers between devices with their start and end apart: 22, of which 6 were waited for; matrix products, arithmetic and copies ran while one was open for 3% of the time, Pallas kernels for 27%

profile of v2, /device:TPU:0, one launch (start us, length us, event | category | flops | bytes accessed | tf_op | source)
XLA Modules:
  0.0 138.6 jit_solution(6180146297420332645)
XLA Ops:
  3.2 1.6 %prepare.1 = (bf16[384,1024]{1,0:T(8,128)(2,1)S(1)}, bf16[384,1024]{1,0:T(8,128)(2,1)}) custom-call(bf16[384,1024]{1,0:T(8,128)(2,1)S(1)} %copy-done.6, s32[1,384]{1,0:T(1,128)S(1)} %reshape.15.order, f32[1,1024]{1,0:T(1,128)S(1)} %bitcast.2), custom_call_target="tpu_custom_call" | custom-call | flops 301989888 | bytes 2359296 | tf_op jit(solution)/shard_map/prepare/pallas_call | solution.py:50
  5.7 5.4 %collective-permute-start.1 = (bf16[384,1024]{1,0:T(8,128)(2,1)}, bf16[384,1024]{1,0:T(8,128)(2,1)S(1)}, u32[]{:S(2)}, u32[]{:S(2)}) collective-permute-start(bf16[384,1024]{1,0:T(8,128)(2,1)} %get-tuple-element.8.source), channel_id=1, source_target_pairs={{0,15},{1,2},{2,1},{3,4},{4,3},{5,6},{6,5},{7,8},{8,7},{9,10},{10,... | collective-permute-start | bytes 2359304 | tf_op jit(solution)/shard_map/ppermute | solution.py:351
  11.2 1.9 %broadcast_select_fusion = bf16[256,1024]{1,0:T(8,128)(2,1)} fusion(bf16[256,1024]{1,0:T(8,128)(2,1)} %refs_1_.3, bf16[256,1024]{1,0:T(8,128)(2,1)} %refs_9_.1, pred[]{:T(512)S(6)} %eq.11), kind=kLoop, calls=%fused_computation.1 | loop fusion | flops 262144 | bytes 1572865 | tf_op jit(solution)/shard_map/jit(_where)/select_n | solution.py:377
  13.1 1.5 %collective-permute-start.12 = (bf16[256,1024]{1,0:T(8,128)(2,1)}, bf16[256,1024]{1,0:T(8,128)(2,1)}, u32[]{:S(2)}, u32[]{:S(2)}) collective-permute-start(bf16[256,1024]{1,0:T(8,128)(2,1)} %broadcast_select_fusion), channel_id=1, source_target_pairs={{4,8},{5,9},{6,10},{7,11},{8,4},{9,5},{10,6},{11,7},{20,24},{21,25... | collective-permute-start | bytes 1572872 | tf_op jit(solution)/shard_map/ppermute | solution.py:362
  14.7 2.8 %copy-done = bf16[1024,3072]{1,0:T(8,128)(2,1)S(1)} copy-done((bf16[1024,3072]{1,0:T(8,128)(2,1)S(1)}, bf16[1024,3072]{1,0:T(8,128)(2,1)}, u32[]{:S(2)}) %copy-start) | copy-done | bytes 6291480
  17.5 10.1 %project.3 = (bf16[384,1024]{1,0:T(8,128)(2,1)S(1)}, bf16[384,2048]{1,0:T(8,128)(2,1)}) custom-call(bf16[384,1024]{1,0:T(8,128)(2,1)} %get-tuple-element.8.source, bf16[1024,3072]{1,0:T(8,128)(2,1)S(1)} %copy-done, f32[1,256]{1,0:T(1,128)S(1)} %broadcast_in_dim_tile.4.query_gain, f32[1,256]{1,0:T(1,128)S(1)} %broadcast_in_dim_tile.5.key_gain), custom_call_target="tpu_custom_call" | custom-call | flops 2415919104 | bytes 9437184 | tf_op jit(solution)/shard_map/project/pallas_call | solution.py:107
  27.7 4.9 %project.4.near = bf16[384,2048]{1,0:T(8,128)(2,1)S(1)} custom-call(bf16[384,1024]{1,0:T(8,128)(2,1)S(1)} %collective-permute-done.1.source, bf16[1024,3072]{1,0:T(8,128)(2,1)S(1)} %copy-done.1, f32[1,256]{1,0:T(1,128)S(1)} %broadcast_in_dim_tile.4.query_gain, f32[1,256]{1,0:T(1,128)S(1)} %broadcast_in_dim_tile.5.key_gain), custom_call_target="tpu_custom_call" | custom-call | flops 1610612736 | bytes 7340032 | tf_op jit(solution)/shard_map/project/pallas_call | solution.py:107
  33.8 1.5 %collective-permute-start.5 = (bf16[256,1024]{1,0:T(8,128)(2,1)S(1)}, bf16[256,1024]{1,0:T(8,128)(2,1)}, u32[]{:S(2)}, u32[]{:S(2)}) collective-permute-start(bf16[256,1024]{1,0:T(8,128)(2,1)S(1)} %collective-permute-done.4.refs_3_), channel_id=1, source_target_pairs={{4,8},{5,9},{6,10},{7,11},{8,4},{9,5},{10,6},{11,7},{20,24},{21,25... | collective-permute-start | bytes 1572872 | tf_op jit(solution)/shard_map/ppermute | solution.py:362
  37.8 14.2 %collective-permute-done.3.source = bf16[384,1024]{1,0:T(8,128)(2,1)S(1)} collective-permute-done((bf16[384,1024]{1,0:T(8,128)(2,1)}, bf16[384,1024]{1,0:T(8,128)(2,1)S(1)}, u32[]{:S(2)}, u32[]{:S(2)}) %collective-permute-start.3) | collective-permute-done | bytes 786464 | tf_op jit(solution)/shard_map/ppermute | solution.py:351
  53.1 2.8 %copy-done.2 = bf16[1024,3072]{1,0:T(8,128)(2,1)S(1)} copy-done((bf16[1024,3072]{1,0:T(8,128)(2,1)S(1)}, bf16[1024,3072]{1,0:T(8,128)(2,1)}, u32[]{:S(2)}) %copy-start.2) | copy-done | bytes 6291480
  55.9 4.9 %project.5.far = bf16[384,2048]{1,0:T(8,128)(2,1)S(1)} custom-call(bf16[384,1024]{1,0:T(8,128)(2,1)S(1)} %collective-permute-done.3.source, bf16[1024,3072]{1,0:T(8,128)(2,1)S(1)} %copy-done.2, f32[1,256]{1,0:T(1,128)S(1)} %broadcast_in_dim_tile.4.query_gain, f32[1,256]{1,0:T(1,128)S(1)} %broadcast_in_dim_tile.5.key_gain), custom_call_target="tpu_custom_call" | custom-call | flops 1610612736 | bytes 7340032 | tf_op jit(solution)/shard_map/project/pallas_call | solution.py:107
  62.2 9.9 %collective-permute-done.6 = bf16[256,1024]{1,0:T(8,128)(2,1)} collective-permute-done((bf16[256,1024]{1,0:T(8,128)(2,1)}, bf16[256,1024]{1,0:T(8,128)(2,1)}, u32[]{:S(2)}, u32[]{:S(2)}) %collective-permute-start.6) | collective-permute-done | bytes 524320 | tf_op jit(solution)/shard_map/ppermute | solution.py:362
  73.2 1.6 %collective-permute-start.16 = (bf16[256,1024]{1,0:T(8,128)(2,1)S(1)}, bf16[256,1024]{1,0:T(8,128)(2,1)S(1)}, u32[]{:S(2)}, u32[]{:S(2)}) collective-permute-start(bf16[256,1024]{1,0:T(8,128)(2,1)S(1)} %collective-permute-done.4.refs_3_), channel_id=1, source_target_pairs={{0,16},{16,0},{1,17},{17,1},{2,18},{18,2},{3,19},{19,3},{4,20},{20... | collective-permute-start | bytes 1572872 | tf_op jit(solution)/shard_map/ppermute | solution.py:368
  75.5 1.5 %collective-permute-start.8 = (bf16[256,1024]{1,0:T(8,128)(2,1)S(1)}, bf16[256,1024]{1,0:T(8,128)(2,1)S(1)}, u32[]{:S(2)}, u32[]{:S(2)}) collective-permute-start(bf16[256,1024]{1,0:T(8,128)(2,1)S(1)} %broadcast_select_fusion.2.refs_1_.refs_7_), channel_id=1, source_target_pairs={{0,16},{16,0},{1,17},{17,1},{2,18},{18,2},{3,19},{19,3},{4,20},{20... | collective-permute-start | bytes 1572872 | tf_op jit(solution)/shard_map/ppermute | solution.py:368
  77.0 11.3 %attend.1 = (bf16[384,1024]{1,0:T(8,128)(2,1)}, bf16[384,1024]{1,0:T(8,128)(2,1)S(1)}) custom-call(s32[3,8]{1,0:T(4,128)S(1)} %copy-done.9, s32[3]{0:T(128)S(1)} %copy-done.10, bf16[384,1024]{1,0:T(8,128)(2,1)S(1)} %copy-done.14, bf16[384,2048]{1,0:T(8,128)(2,1)} %get-tuple-element.10.own, bf16[384,2048]{1,0:T(8,128)(2,1)} %collective-permute-done.mate, ...), custom_call_target="tpu_custom_call" | custom-call | flops 4026531840 | bytes 13107200 | tf_op jit(solution)/shard_map/attend/pallas_call | solution.py:216
  88.4 2.2 %collective-permute-start.20 = (bf16[384,1024]{1,0:T(8,128)(2,1)S(1)}, bf16[384,1024]{1,0:T(8,128)(2,1)S(1)}, u32[]{:S(2)}, u32[]{:S(2)}) collective-permute-start(bf16[384,1024]{1,0:T(8,128)(2,1)S(1)} %get-tuple-element.13.refs_0_), channel_id=1, source_target_pairs={{0,2},{1,3},{2,0},{3,1},{4,6},{5,7},{6,4},{7,5},{8,10},{9,11},{10,... | collective-permute-start | bytes 2359304 | tf_op jit(solution)/shard_map/ppermute | solution.py:351
  91.1 8.1 %collective-permute-done.18.refs_11_.refs_13_ = bf16[256,1024]{1,0:T(8,128)(2,1)S(1)} collective-permute-done((bf16[256,1024]{1,0:T(8,128)(2,1)S(1)}, bf16[256,1024]{1,0:T(8,128)(2,1)S(1)}, u32[]{:S(2)}, u32[]{:S(2)}) %collective-permute-start.18) | collective-permute-done | bytes 524320 | tf_op jit(solution)/shard_map/ppermute | solution.py:368
  99.2 10.8 %collective-permute-done.8.refs_3_.refs_15_ = bf16[256,1024]{1,0:T(8,128)(2,1)S(1)} collective-permute-done((bf16[256,1024]{1,0:T(8,128)(2,1)S(1)}, bf16[256,1024]{1,0:T(8,128)(2,1)S(1)}, u32[]{:S(2)}, u32[]{:S(2)}) %collective-permute-start.8) | collective-permute-done | bytes 524320 | tf_op jit(solution)/shard_map/ppermute | solution.py:368
  110.1 1.9 %collective-permute-done.9.refs_4_.refs_16_ = bf16[256,1024]{1,0:T(8,128)(2,1)S(1)} collective-permute-done((bf16[256,1024]{1,0:T(8,128)(2,1)S(1)}, bf16[256,1024]{1,0:T(8,128)(2,1)S(1)}, u32[]{:S(2)}, u32[]{:S(2)}) %collective-permute-start.9) | collective-permute-done | bytes 524320 | tf_op jit(solution)/shard_map/ppermute | solution.py:351
  112.0 5.3 %feed_pieces.5 = bf16[384,1024]{1,0:T(8,128)(2,1)S(1)} custom-call(bf16[384,1024]{1,0:T(8,128)(2,1)S(1)} %collective-permute-done.20.refs_0_, bf16[256,1024]{1,0:T(8,128)(2,1)S(1)} %copy-done.3, bf16[256,1024]{1,0:T(8,128)(2,1)S(1)} %collective-permute-done.10.refs_2_, bf16[256,1024]{1,0:T(8,128)(2,1)S(1)} %collective-permute-done.4.refs_3_, ...), custom_call_target="tpu_custom_call" | custom-call | flops 3221225472 | bytes 11534336 | tf_op jit(solution)/shard_map/feed_pieces/pallas_call | solution.py:270
  117.3 2.2 %collective-permute-start.21 = (bf16[384,1024]{1,0:T(8,128)(2,1)S(1)}, bf16[384,1024]{1,0:T(8,128)(2,1)S(1)}, u32[]{:S(2)}, u32[]{:S(2)}) collective-permute-start(bf16[384,1024]{1,0:T(8,128)(2,1)S(1)} %feed_pieces.5), channel_id=1, source_target_pairs={{0,2},{1,3},{2,0},{3,1},{4,6},{5,7},{6,4},{7,5},{8,10},{9,11},{10,... | collective-permute-start | bytes 2359304 | tf_op jit(solution)/shard_map/ppermute | solution.py:351
  119.5 3.9 %feed_pieces.3.refs_5_ = f32[384,1024]{1,0:T(8,128)S(1)} custom-call(bf16[384,1024]{1,0:T(8,128)(2,1)S(1)} %get-tuple-element.13.refs_0_, bf16[256,1024]{1,0:T(8,128)(2,1)S(1)} %copy-done.3, bf16[256,1024]{1,0:T(8,128)(2,1)S(1)} %collective-permute-done.10.refs_2_, bf16[256,1024]{1,0:T(8,128)(2,1)S(1)} %collective-permute-done.4.refs_3_, ...), custom_call_target="tpu_custom_call" | custom-call | flops 2415919104 | bytes 9437184 | tf_op jit(solution)/shard_map/feed_pieces/pallas_call | solution.py:270
  123.4 1.6 %feed_pieces.4 = f32[384,1024]{1,0:T(8,128)S(1)} custom-call(bf16[384,1024]{1,0:T(8,128)(2,1)S(1)} %get-tuple-element.13.refs_0_, bf16[256,1024]{1,0:T(8,128)(2,1)S(1)} %broadcast_select_fusion.2.refs_1_.refs_7_, bf16[256,1024]{1,0:T(8,128)(2,1)S(1)} %collective-permute-done.7.refs_2_.refs_8_, bf16[256,1024]{1,0:T(8,128)(2,1)S(1)} %collective-permute-done.8.refs_3_.refs_15_, ...), custom_call_target="tpu_custom_call" | custom-call | flops 805306368 | bytes 5242880 | tf_op jit(solution)/shard_map/feed_pieces/pallas_call | solution.py:270
  125.0 12.3 %collective-permute-done.21 = bf16[384,1024]{1,0:T(8,128)(2,1)S(1)} collective-permute-done((bf16[384,1024]{1,0:T(8,128)(2,1)S(1)}, bf16[384,1024]{1,0:T(8,128)(2,1)S(1)}, u32[]{:S(2)}, u32[]{:S(2)}) %collective-permute-start.21) | collective-permute-done | bytes 786464 | tf_op jit(solution)/shard_map/ppermute | solution.py:351
  (74 shorter events, 13.5 us)
Async XLA Ops:
  5.7 21.9 %collective-permute-start.1 = (bf16[384,1024]{1,0:T(8,128)(2,1)}, bf16[384,1024]{1,0:T(8,128)(2,1)S(1)}, u32[]{:S(2)}, u32[]{:S(2)}) collective-permute-start(bf16[384,1024]{1,0:T(8,128)(2,1)} %get-tuple-element.8.source), channel_id=1, source_target_pairs={{0,15},{1,2},{2,1},{3,4},{4,3},{5,6},{6,5},{7,8},{8,7},{9,10},{10,... | collective-permute-start | bytes 2359304 | tf_op jit(solution)/shard_map/ppermute | solution.py:351
  13.1 20.7 %collective-permute-start.4 = (bf16[256,1024]{1,0:T(8,128)(2,1)}, bf16[256,1024]{1,0:T(8,128)(2,1)S(1)}, u32[]{:S(2)}, u32[]{:S(2)}) collective-permute-start(bf16[256,1024]{1,0:T(8,128)(2,1)} %broadcast_select_fusion), channel_id=1, source_target_pairs={{0,4},{1,5},{2,6},{3,7},{4,0},{5,1},{6,2},{7,3},{8,12},{9,13},{10,... | collective-permute-start | bytes 1572872 | tf_op jit(solution)/shard_map/ppermute | solution.py:362
  13.1 22.2 %collective-permute-start.12 = (bf16[256,1024]{1,0:T(8,128)(2,1)}, bf16[256,1024]{1,0:T(8,128)(2,1)}, u32[]{:S(2)}, u32[]{:S(2)}) collective-permute-start(bf16[256,1024]{1,0:T(8,128)(2,1)} %broadcast_select_fusion), channel_id=1, source_target_pairs={{4,8},{5,9},{6,10},{7,11},{8,4},{9,5},{10,6},{11,7},{20,24},{21,25... | collective-permute-start | bytes 1572872 | tf_op jit(solution)/shard_map/ppermute | solution.py:362
  27.6 24.4 %copy-start.3 = (bf16[256,1024]{1,0:T(8,128)(2,1)S(1)}, bf16[256,1024]{1,0:T(8,128)(2,1)}, u32[]{:S(2)}) copy-start(bf16[256,1024]{1,0:T(8,128)(2,1)} %refs_1_.3) | copy-start | bytes 1572868
  27.6 47.3 %collective-permute-start = (bf16[384,2048]{1,0:T(8,128)(2,1)}, bf16[384,2048]{1,0:T(8,128)(2,1)}, u32[]{:S(2)}, u32[]{:S(2)}) collective-permute-start(bf16[384,2048]{1,0:T(8,128)(2,1)} %get-tuple-element.10.own), channel_id=1, source_target_pairs={{0,1},{1,0},{2,3},{3,2},{4,5},{5,4},{6,7},{7,6},{8,9},{9,8},{10,11... | collective-permute-start | bytes 4718600 | tf_op jit(solution)/shard_map/ppermute | solution.py:351
  32.6 42.9 %collective-permute-start.2 = (bf16[384,2048]{1,0:T(8,128)(2,1)S(1)}, bf16[384,2048]{1,0:T(8,128)(2,1)}, u32[]{:S(2)}, u32[]{:S(2)}) collective-permute-start(bf16[384,2048]{1,0:T(8,128)(2,1)S(1)} %project.4.near), channel_id=1, source_target_pairs={{0,1},{1,0},{2,3},{3,2},{4,5},{5,4},{6,7},{7,6},{8,9},{9,8},{10,11... | collective-permute-start | bytes 4718600 | tf_op jit(solution)/shard_map/ppermute | solution.py:351
  33.1 18.9 %collective-permute-start.3 = (bf16[384,1024]{1,0:T(8,128)(2,1)}, bf16[384,1024]{1,0:T(8,128)(2,1)S(1)}, u32[]{:S(2)}, u32[]{:S(2)}) collective-permute-start(bf16[384,1024]{1,0:T(8,128)(2,1)} %get-tuple-element.8.source), channel_id=1, source_target_pairs={{0,2},{1,15},{2,4},{3,1},{4,6},{5,3},{6,8},{7,5},{8,10},{9,7},{10,... | collective-permute-start | bytes 2359304 | tf_op jit(solution)/shard_map/ppermute | solution.py:351
  33.8 2.7 %collective-permute-start.5 = (bf16[256,1024]{1,0:T(8,128)(2,1)S(1)}, bf16[256,1024]{1,0:T(8,128)(2,1)}, u32[]{:S(2)}, u32[]{:S(2)}) collective-permute-start(bf16[256,1024]{1,0:T(8,128)(2,1)S(1)} %collective-permute-done.4.refs_3_), channel_id=1, source_target_pairs={{4,8},{5,9},{6,10},{7,11},{8,4},{9,5},{10,6},{11,7},{20,24},{21,25... | collective-permute-start | bytes 1572872 | tf_op jit(solution)/shard_map/ppermute | solution.py:362
  35.2 25.6 %collective-permute-start.13 = (bf16[256,1024]{1,0:T(8,128)(2,1)}, bf16[256,1024]{1,0:T(8,128)(2,1)}, u32[]{:S(2)}, u32[]{:S(2)}) collective-permute-start(bf16[256,1024]{1,0:T(8,128)(2,1)} %collective-permute-done.12), channel_id=1, source_target_pairs={{4,0},{5,1},{6,2},{7,3},{8,12},{9,13},{10,14},{11,15},{20,16},{21,... | collective-permute-start | bytes 1572872 | tf_op jit(solution)/shard_map/ppermute | solution.py:362
  36.5 35.5 %collective-permute-start.6 = (bf16[256,1024]{1,0:T(8,128)(2,1)}, bf16[256,1024]{1,0:T(8,128)(2,1)}, u32[]{:S(2)}, u32[]{:S(2)}) collective-permute-start(bf16[256,1024]{1,0:T(8,128)(2,1)} %collective-permute-done.5), channel_id=1, source_target_pairs={{4,0},{5,1},{6,2},{7,3},{8,12},{9,13},{10,14},{11,15},{20,16},{21,... | collective-permute-start | bytes 1572872 | tf_op jit(solution)/shard_map/ppermute | solution.py:362
  52.0 21.2 %collective-permute-start.10 = (bf16[256,1024]{1,0:T(8,128)(2,1)S(1)}, bf16[256,1024]{1,0:T(8,128)(2,1)S(1)}, u32[]{:S(2)}, u32[]{:S(2)}) collective-permute-start(bf16[256,1024]{1,0:T(8,128)(2,1)S(1)} %copy-done.3), channel_id=1, source_target_pairs={{0,1},{1,0},{2,3},{3,2},{4,5},{5,4},{6,7},{7,6},{8,9},{9,8},{10,11... | collective-permute-start | bytes 1572872 | tf_op jit(solution)/shard_map/ppermute | solution.py:351
  55.9 21.1 %copy-start.14 = (bf16[384,1024]{1,0:T(8,128)(2,1)S(1)}, bf16[384,1024]{1,0:T(8,128)(2,1)}, u32[]{:S(2)}) copy-start(bf16[384,1024]{1,0:T(8,128)(2,1)} %copy-done.13) | copy-start | bytes 2359300
  60.8 13.9 %collective-permute-start.15 = (bf16[256,1024]{1,0:T(8,128)(2,1)S(1)}, bf16[256,1024]{1,0:T(8,128)(2,1)S(1)}, u32[]{:S(2)}, u32[]{:S(2)}) collective-permute-start(bf16[256,1024]{1,0:T(8,128)(2,1)S(1)} %copy-done.4), channel_id=1, source_target_pairs={{0,1},{1,0},{2,3},{3,2},{4,5},{5,4},{6,7},{7,6},{8,9},{9,8},{10,11... | collective-permute-start | bytes 1572872 | tf_op jit(solution)/shard_map/ppermute | solution.py:351
  72.1 16.3 %collective-permute-start.11 = (bf16[256,1024]{1,0:T(8,128)(2,1)S(1)}, bf16[256,1024]{1,0:T(8,128)(2,1)S(1)}, u32[]{:S(2)}, u32[]{:S(2)}) collective-permute-start(bf16[256,1024]{1,0:T(8,128)(2,1)S(1)} %collective-permute-done.4.refs_3_), channel_id=1, source_target_pairs={{0,1},{1,0},{2,3},{3,2},{4,5},{5,4},{6,7},{7,6},{8,9},{9,8},{10,11... | collective-permute-start | bytes 1572872 | tf_op jit(solution)/shard_map/ppermute | solution.py:351
  73.2 17.4 %collective-permute-start.16 = (bf16[256,1024]{1,0:T(8,128)(2,1)S(1)}, bf16[256,1024]{1,0:T(8,128)(2,1)S(1)}, u32[]{:S(2)}, u32[]{:S(2)}) collective-permute-start(bf16[256,1024]{1,0:T(8,128)(2,1)S(1)} %collective-permute-done.4.refs_3_), channel_id=1, source_target_pairs={{0,16},{16,0},{1,17},{17,1},{2,18},{18,2},{3,19},{19,3},{4,20},{20... | collective-permute-start | bytes 1572872 | tf_op jit(solution)/shard_map/ppermute | solution.py:368
  74.7 15.8 %collective-permute-start.14 = (bf16[256,1024]{1,0:T(8,128)(2,1)S(1)}, bf16[256,1024]{1,0:T(8,128)(2,1)S(1)}, u32[]{:S(2)}, u32[]{:S(2)}) collective-permute-start(bf16[256,1024]{1,0:T(8,128)(2,1)S(1)} %broadcast_select_fusion.1.refs_5_), channel_id=1, source_target_pairs={{0,1},{1,0},{2,3},{3,2},{4,5},{5,4},{6,7},{7,6},{8,9},{9,8},{10,11... | collective-permute-start | bytes 1572872 | tf_op jit(solution)/shard_map/ppermute | solution.py:351
  75.0 24.2 %collective-permute-start.18 = (bf16[256,1024]{1,0:T(8,128)(2,1)S(1)}, bf16[256,1024]{1,0:T(8,128)(2,1)S(1)}, u32[]{:S(2)}, u32[]{:S(2)}) collective-permute-start(bf16[256,1024]{1,0:T(8,128)(2,1)S(1)} %broadcast_select_fusion.1.refs_5_), channel_id=1, source_target_pairs={{0,16},{16,0},{1,17},{17,1},{2,18},{18,2},{3,19},{19,3},{4,20},{20... | collective-permute-start | bytes 1572872 | tf_op jit(solution)/shard_map/ppermute | solution.py:368
  75.5 34.5 %collective-permute-start.8 = (bf16[256,1024]{1,0:T(8,128)(2,1)S(1)}, bf16[256,1024]{1,0:T(8,128)(2,1)S(1)}, u32[]{:S(2)}, u32[]{:S(2)}) collective-permute-start(bf16[256,1024]{1,0:T(8,128)(2,1)S(1)} %broadcast_select_fusion.2.refs_1_.refs_7_), channel_id=1, source_target_pairs={{0,16},{16,0},{1,17},{17,1},{2,18},{18,2},{3,19},{19,3},{4,20},{20... | collective-permute-start | bytes 1572872 | tf_op jit(solution)/shard_map/ppermute | solution.py:368
  88.4 23.6 %collective-permute-start.20 = (bf16[384,1024]{1,0:T(8,128)(2,1)S(1)}, bf16[384,1024]{1,0:T(8,128)(2,1)S(1)}, u32[]{:S(2)}, u32[]{:S(2)}) collective-permute-start(bf16[384,1024]{1,0:T(8,128)(2,1)S(1)} %get-tuple-element.13.refs_0_), channel_id=1, source_target_pairs={{0,2},{1,3},{2,0},{3,1},{4,6},{5,7},{6,4},{7,5},{8,10},{9,11},{10,... | collective-permute-start | bytes 2359304 | tf_op jit(solution)/shard_map/ppermute | solution.py:351
  90.5 19.5 %collective-permute-start.17 = (bf16[256,1024]{1,0:T(8,128)(2,1)S(1)}, bf16[256,1024]{1,0:T(8,128)(2,1)S(1)}, u32[]{:S(2)}, u32[]{:S(2)}) collective-permute-start(bf16[256,1024]{1,0:T(8,128)(2,1)S(1)} %collective-permute-done.16.refs_9_.refs_11_), channel_id=1, source_target_pairs={{0,1},{1,0},{2,3},{3,2},{4,5},{5,4},{6,7},{7,6},{8,9},{9,8},{10,11... | collective-permute-start | bytes 1572872 | tf_op jit(solution)/shard_map/ppermute | solution.py:351
  90.6 19.5 %collective-permute-start.7 = (bf16[256,1024]{1,0:T(8,128)(2,1)S(1)}, bf16[256,1024]{1,0:T(8,128)(2,1)S(1)}, u32[]{:S(2)}, u32[]{:S(2)}) collective-permute-start(bf16[256,1024]{1,0:T(8,128)(2,1)S(1)} %broadcast_select_fusion.2.refs_1_.refs_7_), channel_id=1, source_target_pairs={{0,1},{1,0},{2,3},{3,2},{4,5},{5,4},{6,7},{7,6},{8,9},{9,8},{10,11... | collective-permute-start | bytes 1572872 | tf_op jit(solution)/shard_map/ppermute | solution.py:351
  99.2 10.9 %collective-permute-start.19 = (bf16[256,1024]{1,0:T(8,128)(2,1)S(1)}, bf16[256,1024]{1,0:T(8,128)(2,1)S(1)}, u32[]{:S(2)}, u32[]{:S(2)}) collective-permute-start(bf16[256,1024]{1,0:T(8,128)(2,1)S(1)} %collective-permute-done.18.refs_11_.refs_13_), channel_id=1, source_target_pairs={{0,1},{1,0},{2,3},{3,2},{4,5},{5,4},{6,7},{7,6},{8,9},{9,8},{10,11... | collective-permute-start | bytes 1572872 | tf_op jit(solution)/shard_map/ppermute | solution.py:351
  110.0 1.9 %collective-permute-start.9 = (bf16[256,1024]{1,0:T(8,128)(2,1)S(1)}, bf16[256,1024]{1,0:T(8,128)(2,1)S(1)}, u32[]{:S(2)}, u32[]{:S(2)}) collective-permute-start(bf16[256,1024]{1,0:T(8,128)(2,1)S(1)} %collective-permute-done.8.refs_3_.refs_15_), channel_id=1, source_target_pairs={{0,1},{1,0},{2,3},{3,2},{4,5},{5,4},{6,7},{7,6},{8,9},{9,8},{10,11... | collective-permute-start | bytes 1572872 | tf_op jit(solution)/shard_map/ppermute | solution.py:351
  117.3 20.0 %collective-permute-start.21 = (bf16[384,1024]{1,0:T(8,128)(2,1)S(1)}, bf16[384,1024]{1,0:T(8,128)(2,1)S(1)}, u32[]{:S(2)}, u32[]{:S(2)}) collective-permute-start(bf16[384,1024]{1,0:T(8,128)(2,1)S(1)} %feed_pieces.5), channel_id=1, source_target_pairs={{0,2},{1,3},{2,0},{3,1},{4,6},{5,7},{6,4},{7,5},{8,10},{9,11},{10,... | collective-permute-start | bytes 2359304 | tf_op jit(solution)/shard_map/ppermute | solution.py:351
  (16 other events, 151.4 us)

commit v3 on v2

v3 whole, which is shorter than its diff:
```python
import functools
import math

import jax
import jax.numpy as jnp
from jax import lax
from jax.experimental import pallas as pl
from jax.experimental.pallas import tpu as pltpu
from jax.sharding import PartitionSpec as P

HEADS = 16
BLOCK = 128
REACH = 2
MAXNZ = 8
EPS = 1e-06
ATTEND_COST = 10**9
MIB = 1024 * 1024


def chip_grid(chips):
    columns = 1 << ((chips.bit_length() - 1) // 2)
    return chips // columns, columns


def chip_cycle(chips):
    rows, columns = chip_grid(chips)
    if columns < 2 or rows % 2:
        return list(range(chips))
    order = [(row, 0) for row in range(rows)]
    for row in reversed(range(rows)):
        inner = list(range(1, columns))
        order += [(row, column) for column in (inner if (rows - 1 - row) % 2 == 0 else inner[::-1])]
    return [row * columns + column for row, column in order]


def cost(flops, moved, part=64):
    return pl.CostEstimate(flops=flops // part, bytes_accessed=moved // part, transcendentals=0)


def ordered_rows(axis, features, order):
    rows = features.shape[0]
    place = lax.broadcasted_iota(jnp.int32, (rows, rows), 0) + lax.axis_index(axis) * rows
    chosen = (place == order[...]).astype(jnp.bfloat16)
    return lax.dot_general(
        chosen, features[...], (((0,), (0,)), ((), ())), preferred_element_type=jnp.float32
    )


def norm_kernel(axis, features, order, gain, normed):
    picked = ordered_rows(axis, features, order)
    factor = lax.rsqrt(jnp.mean(picked * picked, axis=-1, keepdims=True) + EPS)
    normed[...] = (picked * factor * gain[...]).astype(jnp.bfloat16)


def order_kernel(axis, features, order, ordered):
    ordered[...] = ordered_rows(axis, features, order).astype(jnp.bfloat16)


def prepare(features, order, gain=None):
    rows, width = features.shape
    operands = [features, order.reshape(1, rows)]
    if gain is not None:
        operands.append(gain.reshape(1, width))
    return pl.pallas_call(
        functools.partial(order_kernel if gain is None else norm_kernel, "seq"),
        out_shape=jax.ShapeDtypeStruct((rows, width), jnp.bfloat16),
        compiler_params=pltpu.CompilerParams(vmem_limit_bytes=16 * MIB),
        cost_estimate=cost(2 * rows * rows * width, 6 * rows * width),
        name="order" if gain is None else "norm",
    )(*operands)


def choose_kernel(axis, one, other, chosen):
    @pl.when(lax.axis_index(axis) == 0)
    def _():
        chosen[...] = one[...]

    @pl.when(lax.axis_index(axis) != 0)
    def _():
        chosen[...] = other[...]


def choose(axis, one, other):
    return pl.pallas_call(
        functools.partial(choose_kernel, axis),
        out_shape=jax.ShapeDtypeStruct(one.shape, one.dtype),
        compiler_params=pltpu.CompilerParams(vmem_limit_bytes=16 * MIB),
        cost_estimate=cost(0, 6 * one.size),
        name="choose",
    )(one, other)


def head_scale(values, head_dim, gain):
    columns = values.shape[1]
    row = lax.broadcasted_iota(jnp.int32, (columns, columns), 0) // head_dim
    column = lax.broadcasted_iota(jnp.int32, (columns, columns), 1) // head_dim
    same = (row == column).astype(jnp.bfloat16)
    sums = jnp.dot(
        (values * values).astype(jnp.bfloat16), same, preferred_element_type=jnp.float32
    )
    factor = lax.rsqrt(sums * (1.0 / head_dim) + EPS)
    return (values * factor * gain).astype(jnp.bfloat16)


def project_into(source, weights, first, head_dim, scaled, out):
    width = source.shape[1]
    chunk = 4 * head_dim
    at = 0
    for columns, gain in scaled:
        for _ in range(columns // chunk):
            found = jnp.dot(
                source, weights[:, first + at : first + at + chunk],
                preferred_element_type=jnp.float32,
            )
            out(at, found.astype(jnp.bfloat16) if gain is None else head_scale(found, head_dim, gain))
            at += chunk


def project_into(source, weights, first, head_dim, scaled, out):
    width = source.shape[1]
    chunk = 4 * head_dim
    at = 0
    for columns, gain in scaled:
        for _ in range(columns // chunk):
            found = jnp.dot(
                source, weights[:, first + at : first + at + chunk],
                preferred_element_type=jnp.float32,
            )
            out(at, found.astype(jnp.bfloat16) if gain is None else head_scale(found, head_dim, gain))
            at += chunk


def project_kernel(head_dim, scale, count, with_queries, *refs):
    sources = refs[:count]
    weights, query_gain, key_gain, *rest = refs[count:]
    queries = rest[0] if with_queries else None
    key_values, gathered = rest[-2:]
    width = sources[0].shape[1]
    chunk = 4 * head_dim
    at = 0
    for source in sources:
        gathered[at : at + source.shape[0], :] = source[...]
        at += source.shape[0]

    def store_key_value(at, value):
        key_values[:, at : at + chunk] = value

    def store_query(at, value):
        queries[:, at : at + chunk] = value

    if with_queries:
        gain = query_gain[...] * scale
        project_into(sources[0][...], weights, 0, head_dim, [(width, gain)], store_query)
    project_into(
        gathered[...], weights, width, head_dim, [(width, key_gain[...]), (width, None)],
        store_key_value,
    )


def project(sources, weights, query_gain, key_gain, with_queries):
    width = sources[0].shape[1]
    rows = sum(source.shape[0] for source in sources)
    head_dim = query_gain.shape[0]
    shapes = [jax.ShapeDtypeStruct((rows, 2 * width), jnp.bfloat16)]
    if with_queries:
        shapes.insert(0, jax.ShapeDtypeStruct(sources[0].shape, jnp.bfloat16))
    local = pl.BlockSpec(memory_space=pltpu.VMEM)
    return pl.pallas_call(
        functools.partial(
            project_kernel, head_dim, 2.0 / math.sqrt(head_dim), len(sources), with_queries
        ),
        out_shape=shapes,
        in_specs=[local] * (len(sources) + 3),
        out_specs=[local] * len(shapes),
        scratch_shapes=[pltpu.VMEM((rows, width), jnp.bfloat16)],
        compiler_params=pltpu.CompilerParams(vmem_limit_bytes=24 * MIB),
        cost_estimate=cost(4 * rows * width * width, 8 * width * width),
        name="project",
    )(*sources, weights, jnp.tile(query_gain, 4)[None], jnp.tile(key_gain, 4)[None])


def slot_of(block, me, cycle, blocks):
    holder = lax.div(block, blocks)
    away = lax.rem(holder - me + REACH + cycle, cycle) - REACH
    turned = away * (1 - 2 * lax.rem(me, 2))
    return jnp.where(turned > 0, 2 * turned - 1, -2 * turned), lax.rem(block, blocks)


def pick_blocks(lists, counts, picks, at, me, cycle, blocks, wanted):
    found = 0
    count = counts[at]
    for index in range(MAXNZ):
        slot, place = slot_of(lists[at, index], me, cycle, blocks)
        take = (index < count) & wanted(slot)
        spot = found

        @pl.when(take)
        def _(slot=slot, place=place, spot=spot):
            picks[spot] = slot * blocks + place

        found = found + take.astype(jnp.int32)

    @pl.when(lax.rem(found, 2) == 1)
    def _(found=found):
        picks[found] = picks[found - 1]

    return found


def add_blocks(queries, window, picks, sums, here, count):
    width = queries.shape[1]
    pairs = sums.shape[0]
    pair = width // pairs
    low = lax.broadcasted_iota(jnp.int32, (BLOCK, pair), 1) < pair // 2
    key_lane = lax.broadcasted_iota(jnp.int32, (2 * BLOCK, 2 * BLOCK), 1)
    ones = jnp.ones((2 * BLOCK, pair), jnp.bfloat16)

    def two_blocks(step, carry):
        one = pl.ds(pl.multiple_of(picks[2 * step] * BLOCK, BLOCK), BLOCK)
        other = pl.ds(pl.multiple_of(picks[2 * step + 1] * BLOCK, BLOCK), BLOCK)
        kept = key_lane < jnp.where(2 * step + 1 < count, 2 * BLOCK, BLOCK)
        for index in range(pairs):
            columns = pl.ds(index * pair, pair)
            later = pl.ds(width + index * pair, pair)
            asked = queries[here, columns]
            none = jnp.zeros_like(asked)
            both = jnp.concatenate(
                [jnp.where(low, asked, none), jnp.where(low, none, asked)], axis=0
            )
            known = jnp.concatenate([window[one, columns], window[other, columns]], axis=0)
            held = jnp.concatenate([window[one, later], window[other, later]], axis=0)
            scores = lax.dot_general(
                both, known, (((1,), (1,)), ((), ())), preferred_element_type=jnp.float32
            )
            shares = jnp.where(kept, jnp.exp(scores), 0.0).astype(jnp.bfloat16)
            found = jnp.dot(
                shares, jnp.concatenate([held, ones], axis=1), preferred_element_type=jnp.float32
            )
            sums[index] = jnp.where(step == 0, found, sums[index] + found)
        return carry

    lax.fori_loop(0, lax.div(count + 1, 2), two_blocks, 0)


def attend_kernel(
    axis, cycle, lists, counts, queries, own_mate, near_across, mixed, totals,
    sums, window, picks,
):
    rows, width = queries.shape
    blocks = rows // BLOCK
    pairs = sums.shape[0]
    pair = width // pairs
    me = lax.axis_index(axis)
    low = lax.broadcasted_iota(jnp.int32, (BLOCK, pair), 1) < pair // 2
    window[: 2 * rows, :] = own_mate[...]
    window[2 * rows :, :] = near_across[...]
    for at in range(blocks):
        here = pl.ds(at * BLOCK, BLOCK)
        count = pick_blocks(
            lists, counts, picks, at, me, cycle, blocks, lambda slot: slot < 2 * REACH
        )
        add_blocks(queries, window, picks, sums, here, count)
        for index in range(pairs):
            total = sums[index]
            columns = pl.ds(index * pair, pair)
            mixed[here, columns] = jnp.where(low, total[:BLOCK, :pair], total[BLOCK:, :pair])
            totals[here, columns] = jnp.where(low, total[:BLOCK, pair:], total[BLOCK:, pair:])


def attend(axis, cycle, lists, counts, queries, sources):
    rows, width = queries.shape
    shape = jax.ShapeDtypeStruct((rows, width), jnp.float32)
    scalars = pl.BlockSpec(memory_space=pltpu.SMEM)
    local = pl.BlockSpec(memory_space=pltpu.VMEM)
    pairs = width // BLOCK
    slots = 2 * REACH
    work = 2 * rows * MAXNZ * BLOCK * width
    return pl.pallas_call(
        functools.partial(attend_kernel, axis, cycle),
        out_shape=(shape, shape),
        in_specs=[scalars, scalars, local] + [local] * len(sources),
        out_specs=(local, local),
        scratch_shapes=[
            pltpu.VMEM((pairs, 2 * BLOCK, 2 * BLOCK), jnp.float32),
            pltpu.VMEM((slots * rows, 2 * width), jnp.bfloat16),
            pltpu.SMEM((MAXNZ,), jnp.int32),
        ],
        compiler_params=pltpu.CompilerParams(vmem_limit_bytes=32 * MIB),
        cost_estimate=pl.CostEstimate(
            flops=ATTEND_COST, bytes_accessed=4 * slots * rows * width, transcendentals=0
        ),
        name="attend",
    )(lists, counts, queries, *sources)


def finish_kernel(
    axis, cycle, head_dim, lists, counts, queries, far, qkv_weights, key_gain, mixed, totals,
    attention, sums, window, picks,
):
    rows, width = queries.shape
    blocks = rows // BLOCK
    pairs = sums.shape[0]
    pair = width // pairs
    chunk = 4 * head_dim
    me = lax.axis_index(axis)
    low = lax.broadcasted_iota(jnp.int32, (BLOCK, pair), 1) < pair // 2

    def store(at, value):
        window[:, at : at + chunk] = value

    project_into(
        far[...], qkv_weights, width, head_dim, [(width, key_gain[...]), (width, None)], store
    )
    for at in range(blocks):
        here = pl.ds(at * BLOCK, BLOCK)
        count = pick_blocks(
            lists, counts, picks, at, me, cycle, blocks, lambda slot: slot == 2 * REACH
        )
        shift = 2 * REACH * blocks

        @pl.when(count == 0)
        def _():
            sums[...] = jnp.zeros_like(sums)

        for index in range(blocks + 1):
            picks[index] = jnp.clip(picks[index] - shift, 0, blocks - 1)
        add_blocks(queries, window, picks, sums, here, count)
        for index in range(pairs):
            total = sums[index]
            columns = pl.ds(index * pair, pair)
            share = (
                mixed[here, columns] + jnp.where(low, total[:BLOCK, :pair], total[BLOCK:, :pair])
            ) / (
                totals[here, columns] + jnp.where(low, total[:BLOCK, pair:], total[BLOCK:, pair:])
            )
            attention[here, columns] = share.astype(jnp.bfloat16)


def finish(
    axis, cycle, lists, counts, queries, far, qkv_weights, key_gain, mixed, totals,
):
    rows, width = queries.shape
    head_dim = key_gain.shape[0]
    shape = jax.ShapeDtypeStruct((rows, width), jnp.bfloat16)
    scalars = pl.BlockSpec(memory_space=pltpu.SMEM)
    local = pl.BlockSpec(memory_space=pltpu.VMEM)
    pairs = width // BLOCK
    return pl.pallas_call(
        functools.partial(finish_kernel, axis, cycle, head_dim),
        out_shape=shape,
        in_specs=[scalars, scalars] + [local] * 6,
        out_specs=local,
        scratch_shapes=[
            pltpu.VMEM((pairs, 2 * BLOCK, 2 * BLOCK), jnp.float32),
            pltpu.VMEM((rows, 2 * width), jnp.bfloat16),
            pltpu.SMEM((MAXNZ,), jnp.int32),
        ],
        compiler_params=pltpu.CompilerParams(vmem_limit_bytes=32 * MIB),
        cost_estimate=cost(6 * rows * width * width, 8 * width * width),
        name="finish",
    )(
        lists, counts, queries, far, qkv_weights, jnp.tile(key_gain, 4)[None], mixed, totals
    )


def output_kernel(attention, ordered, weights, gain, attended, *seconds):
    product = jnp.dot(attention[...], weights[...], preferred_element_type=jnp.float32)
    result = (ordered[...].astype(jnp.float32) + product).astype(jnp.bfloat16)
    attended[...] = result
    widened = result.astype(jnp.float32)
    factor = lax.rsqrt(jnp.mean(widened * widened, axis=-1, keepdims=True) + EPS)
    second = (widened * factor * gain[...]).astype(jnp.bfloat16)
    part = second.shape[0] // len(seconds)
    for index, kept in enumerate(seconds):
        kept[...] = second[index * part : (index + 1) * part]


def attention_output(attention, ordered, weights, gain, parts):
    rows, width = attention.shape
    shape = jax.ShapeDtypeStruct((rows, width), jnp.bfloat16)
    return pl.pallas_call(
        output_kernel,
        out_shape=[shape] + [jax.ShapeDtypeStruct((rows // parts, width), jnp.bfloat16)] * parts,
        compiler_params=pltpu.CompilerParams(vmem_limit_bytes=24 * MIB),
        cost_estimate=cost(2 * rows * width * width, 2 * width * width),
        name="attention_output",
    )(attention, ordered, weights, gain.reshape(1, width))


def pieces_kernel(axis, swaps, sources, bases, *refs):
    count = len(swaps)
    seconds, refs = refs[:sources], refs[sources:]
    firsts, refs = refs[:count], refs[count:]
    lasts, refs = refs[:count], refs[count:]
    base, results = refs[:bases], refs[bases:]
    straight = lax.axis_index(axis) == 0
    rows = jnp.concatenate([second[...] for second in seconds], axis=0)
    total = None
    for index, swapped in enumerate(swaps):
        first_rows, last_rows = firsts[index][...], lasts[index][...]
        if swapped:
            first_rows, last_rows = (
                jnp.where(straight, first_rows, last_rows),
                jnp.where(straight, last_rows, first_rows),
            )
        before = lax.dot_general(
            rows, first_rows, (((1,), (1,)), ((), ())), preferred_element_type=jnp.float32
        )
        active = jax.nn.gelu(before, approximate=True).astype(jnp.bfloat16)
        part = jnp.dot(active, last_rows, preferred_element_type=jnp.float32)
        total = part if total is None else total + part
    if bases:
        known = jnp.concatenate([part[...] for part in base], axis=0)
        total = total + known.astype(jnp.float32)
    part = total.shape[0] // len(results)
    for index, result in enumerate(results):
        result[...] = total[index * part : (index + 1) * part].astype(result.dtype)


def feed_pieces(axis, seconds, pieces, base, dtype, parts=1):
    rows = sum(second.shape[0] for second in seconds)
    width = seconds[0].shape[1]
    hidden = sum(piece[0].shape[0] for piece in pieces)
    operands = [*seconds] + [piece[0] for piece in pieces] + [piece[1] for piece in pieces]
    return pl.pallas_call(
        functools.partial(
            pieces_kernel, axis, tuple(piece[2] for piece in pieces), len(seconds), len(base)
        ),
        out_shape=[jax.ShapeDtypeStruct((rows // parts, width), dtype)] * parts,
        compiler_params=pltpu.CompilerParams(vmem_limit_bytes=24 * MIB),
        cost_estimate=cost(4 * rows * width * hidden, 4 * hidden * width),
        name="feed_pieces",
    )(*operands, *base)


def total_kernel(attended, own, *refs):
    *returned, result = refs
    part = result.shape[0] // len(returned)
    for index, back in enumerate(returned):
        here = pl.ds(index * part, part)
        result[here, :] = (
            attended[here, :].astype(jnp.float32) + own[here, :] + back[...].astype(jnp.float32)
        ).astype(result.dtype)


def total_of(attended, own, returned):
    return pl.pallas_call(
        total_kernel,
        out_shape=jax.ShapeDtypeStruct(attended.shape, attended.dtype),
        compiler_params=pltpu.CompilerParams(vmem_limit_bytes=16 * MIB),
        cost_estimate=cost(attended.size, 10 * attended.size),
        name="total",
    )(attended, own, *returned)


def feed_kernel(steps, second, first_rows, second_rows, attended, result, total):
    step = pl.program_id(0)
    before = lax.dot_general(
        second[...], first_rows[...], (((1,), (1,)), ((), ())), preferred_element_type=jnp.float32
    )
    active = jax.nn.gelu(before, approximate=True).astype(jnp.bfloat16)
    part = jnp.dot(active, second_rows[...], preferred_element_type=jnp.float32)

    @pl.when(step == 0)
    def _():
        total[...] = part

    @pl.when(step > 0)
    def _():
        total[...] += part

    @pl.when(step == steps - 1)
    def _():
        result[...] = (attended[...].astype(jnp.float32) + total[...]).astype(jnp.bfloat16)


def feed_forward(second, first_rows, second_rows, attended):
    rows, width = second.shape
    hidden = first_rows.shape[0]
    chunk = min(512, hidden)
    steps = hidden // chunk
    whole = pl.BlockSpec((rows, width), lambda i: (0, 0))
    part = pl.BlockSpec((chunk, width), lambda i: (i, 0))
    return pl.pallas_call(
        functools.partial(feed_kernel, steps),
        out_shape=jax.ShapeDtypeStruct((rows, width), jnp.bfloat16),
        grid=(steps,),
        in_specs=[whole, part, part, whole],
        out_specs=whole,
        scratch_shapes=[pltpu.VMEM((rows, width), jnp.float32)],
        compiler_params=pltpu.CompilerParams(vmem_limit_bytes=40 * MIB),
        cost_estimate=pl.CostEstimate(
            flops=4 * rows * width * hidden,
            bytes_accessed=4 * hidden * width + 6 * rows * width,
            transcendentals=rows * hidden,
        ),
        name="feed_forward",
    )(second, first_rows, second_rows, attended)


def shards(
    pore_features,
    pore_order,
    block_lists,
    block_counts,
    norm1_gain,
    w_qkv,
    query_gain,
    key_gain,
    w_attn_out,
    norm2_gain,
    w_in,
    w_out,
):
    rows = pore_features.shape[0]
    cycle = lax.axis_size("seq")
    me = lax.axis_index("seq")

    def moved(value, where):
        return lax.ppermute(value, "seq", [(i, where(i) % cycle) for i in range(cycle)])

    def mate_of(value):
        return moved(value, lambda i: i + 1 - 2 * (i % 2))

    chip_rows, chip_columns = chip_grid(cycle // 2)
    shared = (chip_rows, chip_columns) == (4, 2) and lax.axis_size("parts") == 2
    lane = 2 * chip_columns

    def along(value, targets):
        pairs = [(lane * a + k, lane * b + k) for a, b in targets for k in range(lane)]
        return lax.ppermute(value, "seq", pairs)

    def beside(value):
        return moved(value, lambda i: i + 2 - 4 * (i // 2 % 2))

    def over(value):
        return lax.ppermute(value, "parts", [(0, 1), (1, 0)])

    normed = prepare(pore_features, pore_order, norm1_gain)
    near = moved(normed, lambda i: i - 1 + 2 * (i % 2))
    mate = mate_of(normed)
    queries, own_mate = project([normed, mate], w_qkv, query_gain, key_gain, True)
    queries, near, late_normed, late_features = lax.optimization_barrier(
        (queries, near, normed, pore_features)
    )
    far = moved(late_normed, lambda i: i + 2 - 4 * (i % 2))
    ordered = prepare(late_features, pore_order)
    across = [mate_of(part) for part in jnp.split(near, 4)]

    if shared:
        swap = [(0, 1), (1, 0), (2, 3), (3, 2)]
        prime = choose("parts", w_in, w_out)
        pair_rows = along(prime, swap)
        third = along(prime, [(0, 2), (1, 3), (2, 0), (3, 1)])
    (near_across,) = project([near, *across], w_qkv, query_gain, key_gain, False)
    mixed, totals = attend(
        "seq", cycle, block_lists, block_counts, queries, [own_mate, near_across]
    )
    if shared:
        mixed, totals, third, pair_rows = lax.optimization_barrier(
            (mixed, totals, third, pair_rows)
        )
        other_pair = over(pair_rows)
        fourth = along(third, swap)
        other_third = over(third)
        mixed, totals, far = lax.optimization_barrier((mixed, totals, far))
    attention = finish(
        "seq", cycle, block_lists, block_counts, queries, far, w_qkv, key_gain, mixed, totals
    )
    if shared:
        attention, other_pair = lax.optimization_barrier((attention, other_pair))
    parts = 2 if shared else 1
    attended, *seconds = attention_output(attention, ordered, w_attn_out, norm2_gain, parts)
    if shared:
        guests = [beside(second) for second in seconds]
        mate_seconds = [mate_of(second) for second in seconds]
        attended, fourth = lax.optimization_barrier((attended, fourth))
        other_fourth = over(fourth)
        pieces = [
            (w_in, w_out, False),
            (pair_rows, other_pair, True),
            (third, other_third, True),
            (fourth, other_fourth, True),
        ]
        returned = []
        for guest in guests:
            (guest_mate_part,) = feed_pieces("parts", [mate_of(guest)], pieces, [], jnp.bfloat16)
            (guest_part,) = feed_pieces(
                "parts", [guest], pieces, [mate_of(guest_mate_part)], jnp.bfloat16
            )
            returned.append(beside(guest_part))
        returned[0], *mate_seconds = lax.optimization_barrier((returned[0], *mate_seconds))
        mate_parts = feed_pieces("parts", mate_seconds, pieces, [], jnp.bfloat16, 4)
        (own_part,) = feed_pieces(
            "parts", seconds, pieces, [mate_of(part) for part in mate_parts], jnp.float32
        )
        layer_output = total_of(attended, own_part, returned)
    else:
        ring = [2 * chip + core for chip in chip_cycle(cycle // 2) for core in range(2)]
        gathered_in = lax.all_gather(w_in, "seq", axis=0, tiled=True, axis_index_groups=[ring])
        gathered_out = lax.all_gather(w_out, "seq", axis=0, tiled=True, axis_index_groups=[ring])
        layer_output = feed_forward(seconds[0], gathered_in, gathered_out, attended)
    return (attended, layer_output)


def solution(mesh):
    return jax.shard_map(
        shards,
        mesh=mesh,
        in_specs=(
            P(("parts", "seq"), None),
            P(("parts", "seq")),
            P(("parts", "seq"), None),
            P(("parts", "seq")),
            P(),
            P(),
            P(),
            P(),
            P(),
            P(),
            P("seq", None),
            P("seq", None),
        ),
        out_specs=(P(("parts", "seq"), None), P(("parts", "seq"), None)),
        check_vma=False,
    )
```

time: 139 us -> 118 us (0.85)
  the two profiles are of different devices: /device:TPU:0 before, /device:TPU:15 now
where the time goes in v3:
time: 118 us; the launch traced here: 117 us
  waiting for transfers between devices  45.3 us (38%)
  Pallas kernels  42.3 us (36%)
  starting transfers between devices  21.2 us (18%)
  local copies, waits for them, and re-layouts  7.66 us (6%)
    ppermute x21, waiting for transfers between devices, moved(): lax.ppermute(value, 'seq', [(i, where(i) % cycle) for i in range(cycle)])  35.8 us
    ppermute x21, starting transfers between devices, moved(): lax.ppermute(value, 'seq', [(i, where(i) % cycle) for i in range(cycle)])  17 us
    pallas_call x2, Pallas kernels, project(): pl.pallas_call(functools.partial(project_kernel, head_dim, 2.0 / math.sqr...  13.1 us
    pallas_call x6, Pallas kernels, feed_pieces(): pl.pallas_call(functools.partial(pieces_kernel, axis, tuple((piece[2] for...  12.4 us
    ppermute x3, waiting for transfers between devices, over(): return lax.ppermute(value, 'parts', [(0, 1), (1, 0)])  9.55 us
    unnamed x32, local copies, waits for them, and re-layouts  6.74 us
    pallas_call x1, Pallas kernels, attend(): pl.pallas_call(functools.partial(attend_kernel, axis, cycle), out_shape=(...  6.59 us
    pallas_call x1, Pallas kernels, finish(): pl.pallas_call(functools.partial(finish_kernel, axis, cycle, head_dim), o...  4.98 us
  transfers between devices with their start and end apart: 27, of which 15 were waited for; matrix products, arithmetic and copies ran while one was open for 0% of the time, Pallas kernels for 34%

profile of v3, /device:TPU:15, one launch (start us, length us, event | category | flops | bytes accessed | tf_op | source)
XLA Modules:
  0.0 117.4 jit_solution(13423161275158717452)
XLA Ops:
  11.4 2.8 %copy-done = bf16[1024,3072]{1,0:T(8,128)(2,1)S(1)} copy-done((bf16[1024,3072]{1,0:T(8,128)(2,1)S(1)}, bf16[1024,3072]{1,0:T(8,128)(2,1)}, u32[]{:S(2)}) %copy-start) | copy-done | bytes 6291480
  14.2 7.6 %project.2 = (bf16[384,1024]{1,0:T(8,128)(2,1)S(1)}, bf16[768,2048]{1,0:T(8,128)(2,1)S(1)}) custom-call(bf16[384,1024]{1,0:T(8,128)(2,1)S(1)} %norm.1.refs_0_, bf16[384,1024]{1,0:T(8,128)(2,1)S(1)} %collective-permute-done.refs_1_, bf16[1024,3072]{1,0:T(8,128)(2,1)S(1)} %copy-done, f32[1,256]{1,0:T(1,128)S(1)} %broadcast_in_dim_tile.4.refs_3_.refs_6_, ...), custom_call_target="tpu_custom_call" | custom-call | flops 50331648 | bytes 131072 | tf_op jit(solution)/shard_map/project/pallas_call | solution.py:168
  21.9 10.9 %collective-permute-done.1.refs_0_ = bf16[384,1024]{1,0:T(8,128)(2,1)S(1)} collective-permute-done((bf16[384,1024]{1,0:T(8,128)(2,1)S(1)}, bf16[384,1024]{1,0:T(8,128)(2,1)S(1)}, u32[]{:S(2)}, u32[]{:S(2)}) %collective-permute-start.1) | collective-permute-done | bytes 786464 | tf_op jit(solution)/shard_map/ppermute | solution.py:520
  35.8 5.5 %project.3.near_across = bf16[768,2048]{1,0:T(8,128)(2,1)S(1)} custom-call(bf16[384,1024]{1,0:T(8,128)(2,1)S(1)} %collective-permute-done.1.refs_0_, bf16[96,1024]{1,0:T(8,128)(2,1)S(1)} %collective-permute-done.2.refs_1_, bf16[96,1024]{1,0:T(8,128)(2,1)S(1)} %collective-permute-done.3.refs_2_, bf16[96,1024]{1,0:T(8,128)(2,1)S(1)} %collective-permute-done.4.refs_3_, ...), custom_call_target="tpu_custom_call" | custom-call | flops 50331648 | bytes 131072 | tf_op jit(solution)/shard_map/project/pallas_call | solution.py:168
  41.3 6.6 %attend.1 = (f32[384,1024]{1,0:T(8,128)S(1)}, f32[384,1024]{1,0:T(8,128)S(1)}) custom-call(s32[3,8]{1,0:T(4,128)S(1)} %copy-done.10, s32[3]{0:T(128)S(1)} %copy-done.13, bf16[384,1024]{1,0:T(8,128)(2,1)S(1)} %get-tuple-element.32.queries, bf16[768,2048]{1,0:T(8,128)(2,1)S(1)} %get-tuple-element.33.own_mate, bf16[768,2048]{1,0:T(8,128)(2,1)S(1)} %project.3.near_across), custom_call_target="tpu_custom_call" | custom-call | flops 1000000000 | bytes 6291456 | tf_op jit(solution)/shard_map/attend/pallas_call | solution.py:278
  48.9 2.6 %collective-permute-done.8.far = bf16[384,1024]{1,0:T(8,128)(2,1)S(1)} collective-permute-done((bf16[384,1024]{1,0:T(8,128)(2,1)S(1)}, bf16[384,1024]{1,0:T(8,128)(2,1)S(1)}, u32[]{:S(2)}, u32[]{:S(2)}) %collective-permute-start.8) | collective-permute-done | bytes 786464 | tf_op jit(solution)/shard_map/ppermute | solution.py:520
  51.5 5.0 %finish.1.attention = bf16[384,1024]{1,0:T(8,128)(2,1)S(1)} custom-call(s32[3,8]{1,0:T(4,128)S(1)} %copy-done.10, s32[3]{0:T(128)S(1)} %copy-done.13, bf16[384,1024]{1,0:T(8,128)(2,1)S(1)} %get-tuple-element.32.queries, bf16[384,1024]{1,0:T(8,128)(2,1)S(1)} %collective-permute-done.8.far, bf16[1024,3072]{1,0:T(8,128)(2,1)S(1)} %copy-done.1, ...), custom_call_target="tpu_custom_call" | custom-call | flops 37748736 | bytes 131072 | tf_op jit(solution)/shard_map/finish/pallas_call | solution.py:348
  56.5 4.9 %collective-permute-done.9.refs_6_.refs_7_ = bf16[256,1024]{1,0:T(8,128)(2,1)S(1)} collective-permute-done((bf16[256,1024]{1,0:T(8,128)(2,1)S(1)}, bf16[256,1024]{1,0:T(8,128)(2,1)S(1)}, u32[]{:S(2)}, u32[]{:S(2)}) %collective-permute-start.9) | collective-permute-done | bytes 524320 | tf_op jit(solution)/shard_map/ppermute | solution.py:537
  61.4 1.9 %attention_output.1 = (bf16[384,1024]{1,0:T(8,128)(2,1)}, bf16[192,1024]{1,0:T(8,128)(2,1)S(1)}, bf16[192,1024]{1,0:T(8,128)(2,1)S(1)}) custom-call(bf16[384,1024]{1,0:T(8,128)(2,1)S(1)} %finish.1.attention, bf16[384,1024]{1,0:T(8,128)(2,1)S(1)} %order.1.ordered, bf16[1024,1024]{1,0:T(8,128)(2,1)S(1)} %copy-done.8, f32[1,1024]{1,0:T(1,128)S(1)} %bitcast.3), custom_call_target="tpu_custom_call" | custom-call | flops 12582912 | bytes 32768 | tf_op jit(solution)/shard_map/attention_output/pallas_call | solution.py:381
  66.2 6.7 %collective-permute-done.13.refs_0_ = bf16[192,1024]{1,0:T(8,128)(2,1)S(1)} collective-permute-done((bf16[192,1024]{1,0:T(8,128)(2,1)S(1)}, bf16[192,1024]{1,0:T(8,128)(2,1)S(1)}, u32[]{:S(2)}, u32[]{:S(2)}) %collective-permute-start.13) | collective-permute-done | bytes 393248 | tf_op jit(solution)/shard_map/ppermute | solution.py:520
  73.0 3.3 %collective-permute-start.14 = (bf16[192,1024]{1,0:T(8,128)(2,1)S(1)}, bf16[192,1024]{1,0:T(8,128)(2,1)S(1)}, u32[]{:S(2)}, u32[]{:S(2)}) collective-permute-start(bf16[192,1024]{1,0:T(8,128)(2,1)S(1)} %collective-permute-done.13.refs_0_), channel_id=1, source_target_pairs={{0,1},{1,0},{2,3},{3,2},{4,5},{5,4},{6,7},{7,6},{8,9},{9,8},{10,11... | collective-permute-start | bytes 1179656 | tf_op jit(solution)/shard_map/ppermute | solution.py:520
  76.3 5.1 %collective-permute-done.23.refs_0_ = bf16[192,1024]{1,0:T(8,128)(2,1)S(1)} collective-permute-done((bf16[192,1024]{1,0:T(8,128)(2,1)S(1)}, bf16[192,1024]{1,0:T(8,128)(2,1)S(1)}, u32[]{:S(2)}, u32[]{:S(2)}) %collective-permute-start.23) | collective-permute-done | bytes 393248 | tf_op jit(solution)/shard_map/ppermute | solution.py:520
  81.4 1.9 %collective-permute-start.24 = (bf16[192,1024]{1,0:T(8,128)(2,1)S(1)}, bf16[192,1024]{1,0:T(8,128)(2,1)S(1)}, u32[]{:S(2)}, u32[]{:S(2)}) collective-permute-start(bf16[192,1024]{1,0:T(8,128)(2,1)S(1)} %collective-permute-done.23.refs_0_), channel_id=1, source_target_pairs={{0,1},{1,0},{2,3},{3,2},{4,5},{5,4},{6,7},{7,6},{8,9},{9,8},{10,11... | collective-permute-start | bytes 1179656 | tf_op jit(solution)/shard_map/ppermute | solution.py:520
  83.2 4.6 %collective-permute-done.12.refs_8_.refs_9_ = bf16[256,1024]{1,0:T(8,128)(2,1)S(1)} collective-permute-done((bf16[256,1024]{1,0:T(8,128)(2,1)S(1)}, bf16[256,1024]{1,0:T(8,128)(2,1)S(1)}, u32[]{:S(2)}, u32[]{:S(2)}) %collective-permute-start.12) | collective-permute-done | bytes 524320 | tf_op jit(solution)/shard_map/ppermute | solution.py:537
  87.9 1.8 %feed_pieces.6 = bf16[192,1024]{1,0:T(8,128)(2,1)S(1)} custom-call(bf16[192,1024]{1,0:T(8,128)(2,1)S(1)} %collective-permute-done.14.refs_0_, bf16[256,1024]{1,0:T(8,128)(2,1)S(1)} %copy-done.3, bf16[256,1024]{1,0:T(8,128)(2,1)S(1)} %collective-permute-done.7.refs_2_.refs_3_, bf16[256,1024]{1,0:T(8,128)(2,1)S(1)} %collective-permute-done.6.refs_3_.refs_4_, ...), custom_call_target="tpu_custom_call" | custom-call | flops 12582912 | bytes 65536 | tf_op jit(solution)/shard_map/feed_pieces/pallas_call | solution.py:425
  89.7 2.5 %collective-permute-start.15 = (bf16[192,1024]{1,0:T(8,128)(2,1)S(1)}, bf16[192,1024]{1,0:T(8,128)(2,1)S(1)}, u32[]{:S(2)}, u32[]{:S(2)}) collective-permute-start(bf16[192,1024]{1,0:T(8,128)(2,1)S(1)} %feed_pieces.6), channel_id=1, source_target_pairs={{0,1},{1,0},{2,3},{3,2},{4,5},{5,4},{6,7},{7,6},{8,9},{9,8},{10,11... | collective-permute-start | bytes 1179656 | tf_op jit(solution)/shard_map/ppermute | solution.py:520
  92.3 1.9 %feed_pieces.10 = bf16[192,1024]{1,0:T(8,128)(2,1)S(1)} custom-call(bf16[192,1024]{1,0:T(8,128)(2,1)S(1)} %collective-permute-done.24.refs_0_, bf16[256,1024]{1,0:T(8,128)(2,1)S(1)} %copy-done.3, bf16[256,1024]{1,0:T(8,128)(2,1)S(1)} %collective-permute-done.7.refs_2_.refs_3_, bf16[256,1024]{1,0:T(8,128)(2,1)S(1)} %collective-permute-done.6.refs_3_.refs_4_, ...), custom_call_target="tpu_custom_call" | custom-call | flops 12582912 | bytes 65536 | tf_op jit(solution)/shard_map/feed_pieces/pallas_call | solution.py:425
  94.8 1.8 %feed_pieces.7 = bf16[192,1024]{1,0:T(8,128)(2,1)S(1)} custom-call(bf16[192,1024]{1,0:T(8,128)(2,1)S(1)} %collective-permute-done.13.refs_0_, bf16[256,1024]{1,0:T(8,128)(2,1)S(1)} %copy-done.3, bf16[256,1024]{1,0:T(8,128)(2,1)S(1)} %collective-permute-done.7.refs_2_.refs_3_, bf16[256,1024]{1,0:T(8,128)(2,1)S(1)} %collective-permute-done.6.refs_3_.refs_4_, ...), custom_call_target="tpu_custom_call" | custom-call | flops 12582912 | bytes 65536 | tf_op jit(solution)/shard_map/feed_pieces/pallas_call | solution.py:425
  96.7 1.8 %feed_pieces.11 = bf16[192,1024]{1,0:T(8,128)(2,1)S(1)} custom-call(bf16[192,1024]{1,0:T(8,128)(2,1)S(1)} %collective-permute-done.23.refs_0_, bf16[256,1024]{1,0:T(8,128)(2,1)S(1)} %copy-done.3, bf16[256,1024]{1,0:T(8,128)(2,1)S(1)} %collective-permute-done.7.refs_2_.refs_3_, bf16[256,1024]{1,0:T(8,128)(2,1)S(1)} %collective-permute-done.6.refs_3_.refs_4_, ...), custom_call_target="tpu_custom_call" | custom-call | flops 12582912 | bytes 65536 | tf_op jit(solution)/shard_map/feed_pieces/pallas_call | solution.py:425
  98.6 1.5 %collective-permute-start.26 = (bf16[192,1024]{1,0:T(8,128)(2,1)S(1)}, bf16[192,1024]{1,0:T(8,128)(2,1)S(1)}, u32[]{:S(2)}, u32[]{:S(2)}) collective-permute-start(bf16[192,1024]{1,0:T(8,128)(2,1)S(1)} %feed_pieces.11), channel_id=1, source_target_pairs={{0,2},{1,3},{2,0},{3,1},{4,6},{5,7},{6,4},{7,5},{8,10},{9,11},{10,... | collective-permute-start | bytes 1179656 | tf_op jit(solution)/shard_map/ppermute | solution.py:520
  100.1 6.9 %collective-permute-done.16.refs_0_ = bf16[192,1024]{1,0:T(8,128)(2,1)S(1)} collective-permute-done((bf16[192,1024]{1,0:T(8,128)(2,1)S(1)}, bf16[192,1024]{1,0:T(8,128)(2,1)S(1)}, u32[]{:S(2)}, u32[]{:S(2)}) %collective-permute-start.16) | collective-permute-done | bytes 393248 | tf_op jit(solution)/shard_map/ppermute | solution.py:520
  107.0 2.5 %feed_pieces.8 = (bf16[96,1024]{1,0:T(8,128)(2,1)S(1)}, bf16[96,1024]{1,0:T(8,128)(2,1)S(1)}, bf16[96,1024]{1,0:T(8,128)(2,1)S(1)}, bf16[96,1024]{1,0:T(8,128)(2,1)S(1)}) custom-call(bf16[192,1024]{1,0:T(8,128)(2,1)S(1)} %collective-permute-done.17.refs_0_, bf16[192,1024]{1,0:T(8,128)(2,1)S(1)} %collective-permute-done.18.refs_1_, ...), custom_call_target="tpu_custom_call" | custom-call | flops 25165824 | bytes 65536 | tf_op jit(solution)/shard_map/feed_pieces/pallas_call | solution.py:425
  109.5 2.2 %collective-permute-start.19 = (bf16[96,1024]{1,0:T(8,128)(2,1)S(1)}, bf16[96,1024]{1,0:T(8,128)(2,1)S(1)}, u32[]{:S(2)}, u32[]{:S(2)}) collective-permute-start(bf16[96,1024]{1,0:T(8,128)(2,1)S(1)} %get-tuple-element.55), channel_id=1, source_target_pairs={{0,1},{1,0},{2,3},{3,2},{4,5},{5,4},{6,7},{7,6},{8,9},{9,8},{10,11... | collective-permute-start | bytes 589832 | tf_op jit(solution)/shard_map/ppermute | solution.py:520
  113.7 2.5 %feed_pieces.9.own = f32[384,1024]{1,0:T(8,128)S(1)} custom-call(bf16[192,1024]{1,0:T(8,128)(2,1)S(1)} %get-tuple-element.49.refs_0_, bf16[192,1024]{1,0:T(8,128)(2,1)S(1)} %get-tuple-element.50.refs_1_, bf16[256,1024]{1,0:T(8,128)(2,1)S(1)} %copy-done.3, bf16[256,1024]{1,0:T(8,128)(2,1)S(1)} %collective-permute-done.7.refs_2_.refs_3_, ...), custom_call_target="tpu_custom_call" | custom-call | flops 25165824 | bytes 65536 | tf_op jit(solution)/shard_map/feed_pieces/pallas_call | solution.py:425
  (83 shorter events, 21.6 us)
Async XLA Ops:
  3.9 7.5 %collective-permute-start = (bf16[384,1024]{1,0:T(8,128)(2,1)S(1)}, bf16[384,1024]{1,0:T(8,128)(2,1)S(1)}, u32[]{:S(2)}, u32[]{:S(2)}) collective-permute-start(bf16[384,1024]{1,0:T(8,128)(2,1)S(1)} %norm.1.refs_0_), channel_id=1, source_target_pairs={{0,1},{1,0},{2,3},{3,2},{4,5},{5,4},{6,7},{7,6},{8,9},{9,8},{10,11... | collective-permute-start | bytes 2359304 | tf_op jit(solution)/shard_map/ppermute | solution.py:520
  4.7 28.1 %collective-permute-start.1 = (bf16[384,1024]{1,0:T(8,128)(2,1)S(1)}, bf16[384,1024]{1,0:T(8,128)(2,1)S(1)}, u32[]{:S(2)}, u32[]{:S(2)}) collective-permute-start(bf16[384,1024]{1,0:T(8,128)(2,1)S(1)} %norm.1.refs_0_), channel_id=1, source_target_pairs={{0,15},{1,2},{2,1},{3,4},{4,3},{5,6},{6,5},{7,8},{8,7},{9,10},{10,... | collective-permute-start | bytes 2359304 | tf_op jit(solution)/shard_map/ppermute | solution.py:520
  8.8 39.2 %collective-permute-start.6 = (bf16[256,1024]{1,0:T(8,128)(2,1)}, bf16[256,1024]{1,0:T(8,128)(2,1)S(1)}, u32[]{:S(2)}, u32[]{:S(2)}) collective-permute-start(bf16[256,1024]{1,0:T(8,128)(2,1)} %choose.1), channel_id=1, source_target_pairs={{0,8},{1,9},{2,10},{3,11},{4,12},{5,13},{6,14},{7,15},{8,0},{9,1},... | collective-permute-start | bytes 1572872 | tf_op jit(solution)/shard_map/ppermute | solution.py:531
  9.9 38.1 %collective-permute-start.7 = (bf16[256,1024]{1,0:T(8,128)(2,1)}, bf16[256,1024]{1,0:T(8,128)(2,1)S(1)}, u32[]{:S(2)}, u32[]{:S(2)}) collective-permute-start(bf16[256,1024]{1,0:T(8,128)(2,1)} %choose.1), channel_id=1, source_target_pairs={{0,4},{1,5},{2,6},{3,7},{4,0},{5,1},{6,2},{7,3},{8,12},{9,13},{10,... | collective-permute-start | bytes 1572872 | tf_op jit(solution)/shard_map/ppermute | solution.py:531
  32.8 1.5 %collective-permute-start.2 = (bf16[96,1024]{1,0:T(8,128)(2,1)S(1)}, bf16[96,1024]{1,0:T(8,128)(2,1)S(1)}, u32[]{:S(2)}, u32[]{:S(2)}) collective-permute-start(bf16[96,1024]{1,0:T(8,128)(2,1)S(1)} %get-tuple-element.63), channel_id=1, source_target_pairs={{0,1},{1,0},{2,3},{3,2},{4,5},{5,4},{6,7},{7,6},{8,9},{9,8},{10,11... | collective-permute-start | bytes 589832 | tf_op jit(solution)/shard_map/ppermute | solution.py:520
  32.9 1.7 %collective-permute-start.3 = (bf16[96,1024]{1,0:T(8,128)(2,1)S(1)}, bf16[96,1024]{1,0:T(8,128)(2,1)S(1)}, u32[]{:S(2)}, u32[]{:S(2)}) collective-permute-start(bf16[96,1024]{1,0:T(8,128)(2,1)S(1)} %get-tuple-element.62), channel_id=1, source_target_pairs={{0,1},{1,0},{2,3},{3,2},{4,5},{5,4},{6,7},{7,6},{8,9},{9,8},{10,11... | collective-permute-start | bytes 589832 | tf_op jit(solution)/shard_map/ppermute | solution.py:520
  33.4 1.5 %collective-permute-start.4 = (bf16[96,1024]{1,0:T(8,128)(2,1)S(1)}, bf16[96,1024]{1,0:T(8,128)(2,1)S(1)}, u32[]{:S(2)}, u32[]{:S(2)}) collective-permute-start(bf16[96,1024]{1,0:T(8,128)(2,1)S(1)} %get-tuple-element.61), channel_id=1, source_target_pairs={{0,1},{1,0},{2,3},{3,2},{4,5},{5,4},{6,7},{7,6},{8,9},{9,8},{10,11... | collective-permute-start | bytes 589832 | tf_op jit(solution)/shard_map/ppermute | solution.py:520
  34.6 16.9 %collective-permute-start.8 = (bf16[384,1024]{1,0:T(8,128)(2,1)S(1)}, bf16[384,1024]{1,0:T(8,128)(2,1)S(1)}, u32[]{:S(2)}, u32[]{:S(2)}) collective-permute-start(bf16[384,1024]{1,0:T(8,128)(2,1)S(1)} %norm.1.refs_0_), channel_id=1, source_target_pairs={{0,2},{1,15},{2,4},{3,1},{4,6},{5,3},{6,8},{7,5},{8,10},{9,7},{10,... | collective-permute-start | bytes 2359304 | tf_op jit(solution)/shard_map/ppermute | solution.py:520
  48.0 13.4 %collective-permute-start.9 = (bf16[256,1024]{1,0:T(8,128)(2,1)S(1)}, bf16[256,1024]{1,0:T(8,128)(2,1)S(1)}, u32[]{:S(2)}, u32[]{:S(2)}) collective-permute-start(bf16[256,1024]{1,0:T(8,128)(2,1)S(1)} %collective-permute-done.7.refs_2_.refs_3_), channel_id=1, source_target_pairs={{0,16},{16,0},{1,17},{17,1},{2,18},{18,2},{3,19},{19,3},{4,20},{20... | collective-permute-start | bytes 1572872 | tf_op jit(solution)/shard_map/ppermute | solution.py:537
  48.3 16.5 %collective-permute-start.10 = (bf16[256,1024]{1,0:T(8,128)(2,1)S(1)}, bf16[256,1024]{1,0:T(8,128)(2,1)S(1)}, u32[]{:S(2)}, u32[]{:S(2)}) collective-permute-start(bf16[256,1024]{1,0:T(8,128)(2,1)S(1)} %collective-permute-done.6.refs_3_.refs_4_), channel_id=1, source_target_pairs={{0,4},{1,5},{2,6},{3,7},{4,0},{5,1},{6,2},{7,3},{8,12},{9,13},{10,... | collective-permute-start | bytes 1572872 | tf_op jit(solution)/shard_map/ppermute | solution.py:531
  63.3 9.7 %collective-permute-start.13 = (bf16[192,1024]{1,0:T(8,128)(2,1)S(1)}, bf16[192,1024]{1,0:T(8,128)(2,1)S(1)}, u32[]{:S(2)}, u32[]{:S(2)}) collective-permute-start(bf16[192,1024]{1,0:T(8,128)(2,1)S(1)} %get-tuple-element.49.refs_0_), channel_id=1, source_target_pairs={{0,2},{1,3},{2,0},{3,1},{4,6},{5,7},{6,4},{7,5},{8,10},{9,11},{10,... | collective-permute-start | bytes 1179656 | tf_op jit(solution)/shard_map/ppermute | solution.py:520
  63.3 18.1 %collective-permute-start.23 = (bf16[192,1024]{1,0:T(8,128)(2,1)S(1)}, bf16[192,1024]{1,0:T(8,128)(2,1)S(1)}, u32[]{:S(2)}, u32[]{:S(2)}) collective-permute-start(bf16[192,1024]{1,0:T(8,128)(2,1)S(1)} %get-tuple-element.50.refs_1_), channel_id=1, source_target_pairs={{0,2},{1,3},{2,0},{3,1},{4,6},{5,7},{6,4},{7,5},{8,10},{9,11},{10,... | collective-permute-start | bytes 1179656 | tf_op jit(solution)/shard_map/ppermute | solution.py:520
  64.8 18.5 %collective-permute-start.11 = (bf16[256,1024]{1,0:T(8,128)(2,1)S(1)}, bf16[256,1024]{1,0:T(8,128)(2,1)S(1)}, u32[]{:S(2)}, u32[]{:S(2)}) collective-permute-start(bf16[256,1024]{1,0:T(8,128)(2,1)S(1)} %collective-permute-done.6.refs_3_.refs_4_), channel_id=1, source_target_pairs={{0,16},{16,0},{1,17},{17,1},{2,18},{18,2},{3,19},{19,3},{4,20},{20... | collective-permute-start | bytes 1572872 | tf_op jit(solution)/shard_map/ppermute | solution.py:537
  64.8 23.1 %collective-permute-start.12 = (bf16[256,1024]{1,0:T(8,128)(2,1)S(1)}, bf16[256,1024]{1,0:T(8,128)(2,1)S(1)}, u32[]{:S(2)}, u32[]{:S(2)}) collective-permute-start(bf16[256,1024]{1,0:T(8,128)(2,1)S(1)} %collective-permute-done.10.refs_4_.refs_5_), channel_id=1, source_target_pairs={{0,16},{16,0},{1,17},{17,1},{2,18},{18,2},{3,19},{19,3},{4,20},{20... | collective-permute-start | bytes 1572872 | tf_op jit(solution)/shard_map/ppermute | solution.py:537
  73.0 14.9 %collective-permute-start.14 = (bf16[192,1024]{1,0:T(8,128)(2,1)S(1)}, bf16[192,1024]{1,0:T(8,128)(2,1)S(1)}, u32[]{:S(2)}, u32[]{:S(2)}) collective-permute-start(bf16[192,1024]{1,0:T(8,128)(2,1)S(1)} %collective-permute-done.13.refs_0_), channel_id=1, source_target_pairs={{0,1},{1,0},{2,3},{3,2},{4,5},{5,4},{6,7},{7,6},{8,9},{9,8},{10,11... | collective-permute-start | bytes 1179656 | tf_op jit(solution)/shard_map/ppermute | solution.py:520
  81.4 10.9 %collective-permute-start.24 = (bf16[192,1024]{1,0:T(8,128)(2,1)S(1)}, bf16[192,1024]{1,0:T(8,128)(2,1)S(1)}, u32[]{:S(2)}, u32[]{:S(2)}) collective-permute-start(bf16[192,1024]{1,0:T(8,128)(2,1)S(1)} %collective-permute-done.23.refs_0_), channel_id=1, source_target_pairs={{0,1},{1,0},{2,3},{3,2},{4,5},{5,4},{6,7},{7,6},{8,9},{9,8},{10,11... | collective-permute-start | bytes 1179656 | tf_op jit(solution)/shard_map/ppermute | solution.py:520
  89.7 5.0 %collective-permute-start.15 = (bf16[192,1024]{1,0:T(8,128)(2,1)S(1)}, bf16[192,1024]{1,0:T(8,128)(2,1)S(1)}, u32[]{:S(2)}, u32[]{:S(2)}) collective-permute-start(bf16[192,1024]{1,0:T(8,128)(2,1)S(1)} %feed_pieces.6), channel_id=1, source_target_pairs={{0,1},{1,0},{2,3},{3,2},{4,5},{5,4},{6,7},{7,6},{8,9},{9,8},{10,11... | collective-permute-start | bytes 1179656 | tf_op jit(solution)/shard_map/ppermute | solution.py:520
  94.1 2.6 %collective-permute-start.25 = (bf16[192,1024]{1,0:T(8,128)(2,1)S(1)}, bf16[192,1024]{1,0:T(8,128)(2,1)S(1)}, u32[]{:S(2)}, u32[]{:S(2)}) collective-permute-start(bf16[192,1024]{1,0:T(8,128)(2,1)S(1)} %feed_pieces.10), channel_id=1, source_target_pairs={{0,1},{1,0},{2,3},{3,2},{4,5},{5,4},{6,7},{7,6},{8,9},{9,8},{10,11... | collective-permute-start | bytes 1179656 | tf_op jit(solution)/shard_map/ppermute | solution.py:520
  94.2 5.9 %collective-permute-start.17 = (bf16[192,1024]{1,0:T(8,128)(2,1)S(1)}, bf16[192,1024]{1,0:T(8,128)(2,1)S(1)}, u32[]{:S(2)}, u32[]{:S(2)}) collective-permute-start(bf16[192,1024]{1,0:T(8,128)(2,1)S(1)} %get-tuple-element.49.refs_0_), channel_id=1, source_target_pairs={{0,1},{1,0},{2,3},{3,2},{4,5},{5,4},{6,7},{7,6},{8,9},{9,8},{10,11... | collective-permute-start | bytes 1179656 | tf_op jit(solution)/shard_map/ppermute | solution.py:520
  94.7 5.4 %collective-permute-start.18 = (bf16[192,1024]{1,0:T(8,128)(2,1)S(1)}, bf16[192,1024]{1,0:T(8,128)(2,1)S(1)}, u32[]{:S(2)}, u32[]{:S(2)}) collective-permute-start(bf16[192,1024]{1,0:T(8,128)(2,1)S(1)} %get-tuple-element.50.refs_1_), channel_id=1, source_target_pairs={{0,1},{1,0},{2,3},{3,2},{4,5},{5,4},{6,7},{7,6},{8,9},{9,8},{10,11... | collective-permute-start | bytes 1179656 | tf_op jit(solution)/shard_map/ppermute | solution.py:520
  96.6 10.3 %collective-permute-start.16 = (bf16[192,1024]{1,0:T(8,128)(2,1)S(1)}, bf16[192,1024]{1,0:T(8,128)(2,1)S(1)}, u32[]{:S(2)}, u32[]{:S(2)}) collective-permute-start(bf16[192,1024]{1,0:T(8,128)(2,1)S(1)} %feed_pieces.7), channel_id=1, source_target_pairs={{0,2},{1,3},{2,0},{3,1},{4,6},{5,7},{6,4},{7,5},{8,10},{9,11},{10,... | collective-permute-start | bytes 1179656 | tf_op jit(solution)/shard_map/ppermute | solution.py:520
  98.6 17.7 %collective-permute-start.26 = (bf16[192,1024]{1,0:T(8,128)(2,1)S(1)}, bf16[192,1024]{1,0:T(8,128)(2,1)S(1)}, u32[]{:S(2)}, u32[]{:S(2)}) collective-permute-start(bf16[192,1024]{1,0:T(8,128)(2,1)S(1)} %feed_pieces.11), channel_id=1, source_target_pairs={{0,2},{1,3},{2,0},{3,1},{4,6},{5,7},{6,4},{7,5},{8,10},{9,11},{10,... | collective-permute-start | bytes 1179656 | tf_op jit(solution)/shard_map/ppermute | solution.py:520
  109.5 3.3 %collective-permute-start.19 = (bf16[96,1024]{1,0:T(8,128)(2,1)S(1)}, bf16[96,1024]{1,0:T(8,128)(2,1)S(1)}, u32[]{:S(2)}, u32[]{:S(2)}) collective-permute-start(bf16[96,1024]{1,0:T(8,128)(2,1)S(1)} %get-tuple-element.55), channel_id=1, source_target_pairs={{0,1},{1,0},{2,3},{3,2},{4,5},{5,4},{6,7},{7,6},{8,9},{9,8},{10,11... | collective-permute-start | bytes 589832 | tf_op jit(solution)/shard_map/ppermute | solution.py:520
  111.8 1.6 %collective-permute-start.21 = (bf16[96,1024]{1,0:T(8,128)(2,1)S(1)}, bf16[96,1024]{1,0:T(8,128)(2,1)S(1)}, u32[]{:S(2)}, u32[]{:S(2)}) collective-permute-start(bf16[96,1024]{1,0:T(8,128)(2,1)S(1)} %get-tuple-element.57), channel_id=1, source_target_pairs={{0,1},{1,0},{2,3},{3,2},{4,5},{5,4},{6,7},{7,6},{8,9},{9,8},{10,11... | collective-permute-start | bytes 589832 | tf_op jit(solution)/shard_map/ppermute | solution.py:520
  (19 other events, 166.8 us)

commit v4 on v3

--- a/solution.py
+++ b/solution.py
@@ -13,7 +13,7 @@
 REACH = 2
 MAXNZ = 8
 EPS = 1e-06
-ATTEND_COST = 10**9
+ATTEND_COST = 5 * 10**8
 MIB = 1024 * 1024
 
 
@@ -46,10 +46,14 @@
     )
 
 
-def norm_kernel(axis, features, order, gain, normed):
+def norm_kernel(axis, features, order, gain, normed, *parts):
     picked = ordered_rows(axis, features, order)
     factor = lax.rsqrt(jnp.mean(picked * picked, axis=-1, keepdims=True) + EPS)
-    normed[...] = (picked * factor * gain[...]).astype(jnp.bfloat16)
+    found = (picked * factor * gain[...]).astype(jnp.bfloat16)
+    normed[...] = found
+    size = found.shape[0] // len(parts)
+    for index, part in enumerate(parts):
+        part[...] = found[index * size : (index + 1) * size]
 
 
 def order_kernel(axis, features, order, ordered):
@@ -58,33 +62,54 @@
 
 def prepare(features, order, gain=None):
     rows, width = features.shape
+    shapes = [jax.ShapeDtypeStruct((rows, width), jnp.bfloat16)]
+    if gain is not None:
+        shapes += [jax.ShapeDtypeStruct((rows // 2, width), jnp.bfloat16)] * 2
     operands = [features, order.reshape(1, rows)]
     if gain is not None:
         operands.append(gain.reshape(1, width))
     return pl.pallas_call(
         functools.partial(order_kernel if gain is None else norm_kernel, "seq"),
-        out_shape=jax.ShapeDtypeStruct((rows, width), jnp.bfloat16),
+        out_shape=shapes,
         compiler_params=pltpu.CompilerParams(vmem_limit_bytes=16 * MIB),
         cost_estimate=cost(2 * rows * rows * width, 6 * rows * width),
         name="order" if gain is None else "norm",
     )(*operands)
 
 
-def choose_kernel(axis, one, other, chosen):
-    @pl.when(lax.axis_index(axis) == 0)
+def choose_kernel(axis, one, other, chosen, left, arrived):
+    straight = lax.axis_index(axis) == 0
+
+    def copies(first, second):
+        return (
+            pltpu.make_async_copy(first, chosen, arrived.at[0]),
+            pltpu.make_async_copy(second, left, arrived.at[1]),
+        )
+
+    @pl.when(straight)
     def _():
-        chosen[...] = one[...]
-
-    @pl.when(lax.axis_index(axis) != 0)
+        for copy in copies(one, other):
+            copy.start()
+
+    @pl.when(jnp.logical_not(straight))
     def _():
-        chosen[...] = other[...]
+        for copy in copies(other, one):
+            copy.start()
+
+    for copy in copies(one, other):
+        copy.wait()
 
 
 def choose(axis, one, other):
+    anywhere = pl.BlockSpec(memory_space=pl.ANY)
+    local = pl.BlockSpec(memory_space=pltpu.VMEM)
     return pl.pallas_call(
         functools.partial(choose_kernel, axis),
-        out_shape=jax.ShapeDtypeStruct(one.shape, one.dtype),
-        compiler_params=pltpu.CompilerParams(vmem_limit_bytes=16 * MIB),
+        out_shape=[jax.ShapeDtypeStruct(one.shape, one.dtype)] * 2,
+        in_specs=[anywhere, anywhere],
+        out_specs=[local, local],
+        scratch_shapes=[pltpu.SemaphoreType.DMA((2,))],
+        compiler_params=pltpu.CompilerParams(vmem_limit_bytes=60 * MIB),
         cost_estimate=cost(0, 6 * one.size),
         name="choose",
     )(one, other)
@@ -243,7 +268,7 @@
 
 
 def attend_kernel(
-    axis, cycle, lists, counts, queries, own_mate, near_across, mixed, totals,
+    axis, cycle, lists, counts, queries, own_mate, near, across, mixed, totals,
     sums, window, picks,
 ):
     rows, width = queries.shape
@@ -253,7 +278,8 @@
     me = lax.axis_index(axis)
     low = lax.broadcasted_iota(jnp.int32, (BLOCK, pair), 1) < pair // 2
     window[: 2 * rows, :] = own_mate[...]
-    window[2 * rows :, :] = near_across[...]
+    window[2 * rows : 3 * rows, :] = near[...]
+    window[3 * rows :, :] = across[...]
     for at in range(blocks):
         here = pl.ds(at * BLOCK, BLOCK)
         count = pick_blocks(
@@ -294,23 +320,15 @@
 
 
 def finish_kernel(
-    axis, cycle, head_dim, lists, counts, queries, far, qkv_weights, key_gain, mixed, totals,
-    attention, sums, window, picks,
+    axis, cycle, lists, counts, queries, window, mixed, totals, attention, sums, picks,
 ):
     rows, width = queries.shape
     blocks = rows // BLOCK
     pairs = sums.shape[0]
     pair = width // pairs
-    chunk = 4 * head_dim
     me = lax.axis_index(axis)
     low = lax.broadcasted_iota(jnp.int32, (BLOCK, pair), 1) < pair // 2
 
-    def store(at, value):
-        window[:, at : at + chunk] = value
-
-    project_into(
-        far[...], qkv_weights, width, head_dim, [(width, key_gain[...]), (width, None)], store
-    )
     for at in range(blocks):
         here = pl.ds(at * BLOCK, BLOCK)
         count = pick_blocks(
@@ -337,29 +355,27 @@
 
 
 def finish(
-    axis, cycle, lists, counts, queries, far, qkv_weights, key_gain, mixed, totals,
+    axis, cycle, lists, counts, queries, far_kv, mixed, totals
 ):
     rows, width = queries.shape
-    head_dim = key_gain.shape[0]
     shape = jax.ShapeDtypeStruct((rows, width), jnp.bfloat16)
     scalars = pl.BlockSpec(memory_space=pltpu.SMEM)
     local = pl.BlockSpec(memory_space=pltpu.VMEM)
     pairs = width // BLOCK
     return pl.pallas_call(
-        functools.partial(finish_kernel, axis, cycle, head_dim),
+        functools.partial(finish_kernel, axis, cycle),
         out_shape=shape,
-        in_specs=[scalars, scalars] + [local] * 6,
+        in_specs=[scalars, scalars] + [local] * 4,
         out_specs=local,
         scratch_shapes=[
             pltpu.VMEM((pairs, 2 * BLOCK, 2 * BLOCK), jnp.float32),
-            pltpu.VMEM((rows, 2 * width), jnp.bfloat16),
             pltpu.SMEM((MAXNZ,), jnp.int32),
         ],
         compiler_params=pltpu.CompilerParams(vmem_limit_bytes=32 * MIB),
         cost_estimate=cost(6 * rows * width * width, 8 * width * width),
         name="finish",
     )(
-        lists, counts, queries, far, qkv_weights, jnp.tile(key_gain, 4)[None], mixed, totals
+        lists, counts, queries, far_kv, mixed, totals
     )
 
 
@@ -523,7 +539,6 @@
         return moved(value, lambda i: i + 1 - 2 * (i % 2))
 
     chip_rows, chip_columns = chip_grid(cycle // 2)
-    shared = (chip_rows, chip_columns) == (4, 2) and lax.axis_size("parts") == 2
     lane = 2 * chip_columns
 
     def along(value, targets):
@@ -536,63 +551,76 @@
     def over(value):
         return lax.ppermute(value, "parts", [(0, 1), (1, 0)])
 
-    normed = prepare(pore_features, pore_order, norm1_gain)
-    near = moved(normed, lambda i: i - 1 + 2 * (i % 2))
+    shared = (chip_rows, chip_columns) == (4, 2) and lax.axis_size("parts") == 2
+    if shared:
+        swap = [(0, 1), (1, 0), (2, 3), (3, 2)]
+        prime, left = choose("parts", w_in, w_out)
+        pair_rows = along(prime, swap)
+        third = along(prime, [(0, 2), (1, 3), (2, 0), (3, 1)])
+    normed, *normed_parts = prepare(pore_features, pore_order, norm1_gain)
+    near = [moved(part, lambda i: i - 1 + 2 * (i % 2)) for part in normed_parts]
     mate = mate_of(normed)
     queries, own_mate = project([normed, mate], w_qkv, query_gain, key_gain, True)
-    queries, near, late_normed, late_features = lax.optimization_barrier(
-        (queries, near, normed, pore_features)
+    queries, late_normed, late_features, *near = lax.optimization_barrier(
+        (queries, normed, pore_features, *near)
     )
     far = moved(late_normed, lambda i: i + 2 - 4 * (i % 2))
-    ordered = prepare(late_features, pore_order)
-    across = [mate_of(part) for part in jnp.split(near, 4)]
-
+    (ordered,) = prepare(late_features, pore_order)
+    across = [mate_of(piece) for part in near for piece in jnp.split(part, 2)]
+
+    (near_kv,) = project(near, w_qkv, query_gain, key_gain, False)
     if shared:
-        swap = [(0, 1), (1, 0), (2, 3), (3, 2)]
-        prime = choose("parts", w_in, w_out)
-        pair_rows = along(prime, swap)
-        third = along(prime, [(0, 2), (1, 3), (2, 0), (3, 1)])
-    (near_across,) = project([near, *across], w_qkv, query_gain, key_gain, False)
+        near_kv, *across = lax.optimization_barrier((near_kv, *across))
+    (across_kv,) = project(across, w_qkv, query_gain, key_gain, False)
     mixed, totals = attend(
-        "seq", cycle, block_lists, block_counts, queries, [own_mate, near_across]
+        "seq", cycle, block_lists, block_counts, queries, [own_mate, near_kv, across_kv]
     )
     if shared:
-        mixed, totals, third, pair_rows = lax.optimization_barrier(
-            (mixed, totals, third, pair_rows)
-        )
-        other_pair = over(pair_rows)
+        mixed, totals, third, pair_rows, left = lax.optimization_barrier(
+            (mixed, totals, third, pair_rows, left)
+        )
+        other_pair = along(left, swap)
         fourth = along(third, swap)
         other_third = over(third)
-        mixed, totals, far = lax.optimization_barrier((mixed, totals, far))
+        mixed, totals, far, ordered = lax.optimization_barrier((mixed, totals, far, ordered))
+    (far_kv,) = project([far], w_qkv, query_gain, key_gain, False)
     attention = finish(
-        "seq", cycle, block_lists, block_counts, queries, far, w_qkv, key_gain, mixed, totals
-    )
-    if shared:
-        attention, other_pair = lax.optimization_barrier((attention, other_pair))
+        "seq", cycle, block_lists, block_counts, queries, far_kv, mixed, totals
+    )
     parts = 2 if shared else 1
     attended, *seconds = attention_output(attention, ordered, w_attn_out, norm2_gain, parts)
     if shared:
         guests = [beside(second) for second in seconds]
         mate_seconds = [mate_of(second) for second in seconds]
         attended, fourth = lax.optimization_barrier((attended, fourth))
+        guests[0], other_pair, other_third = lax.optimization_barrier(
+            (guests[0], other_pair, other_third)
+        )
         other_fourth = over(fourth)
         pieces = [
             (w_in, w_out, False),
             (pair_rows, other_pair, True),
             (third, other_third, True),
+        ]
+        guest_mate_parts = [
+            feed_pieces("parts", [mate_of(guest)], pieces, [], jnp.bfloat16)[0] for guest in guests
+        ]
+        other_fourth, *guest_mate_parts = lax.optimization_barrier(
+            (other_fourth, *guest_mate_parts)
+        )
+        every = [
+            *pieces,
             (fourth, other_fourth, True),
+            (mate_of(fourth), mate_of(other_fourth), True),
         ]
         returned = []
-        for guest in guests:
-            (guest_mate_part,) = feed_pieces("parts", [mate_of(guest)], pieces, [], jnp.bfloat16)
-            (guest_part,) = feed_pieces(
-                "parts", [guest], pieces, [mate_of(guest_mate_part)], jnp.bfloat16
-            )
+        for guest, part in zip(guests, guest_mate_parts):
+            (guest_part,) = feed_pieces("parts", [guest], every, [mate_of(part)], jnp.bfloat16)
             returned.append(beside(guest_part))
         returned[0], *mate_seconds = lax.optimization_barrier((returned[0], *mate_seconds))
         mate_parts = feed_pieces("parts", mate_seconds, pieces, [], jnp.bfloat16, 4)
         (own_part,) = feed_pieces(
-            "parts", seconds, pieces, [mate_of(part) for part in mate_parts], jnp.float32
+            "parts", seconds, every, [mate_of(part) for part in mate_parts], jnp.float32
         )
         layer_output = total_of(attended, own_part, returned)
     else:

time: 118 us -> 111 us (0.941)
  the two profiles are of different devices: /device:TPU:15 before, /device:TPU:0 now
where the time goes in v4:
time: 111 us
  Pallas kernels  45.9 us (41%)
  waiting for transfers between devices  31.9 us (29%)
  starting transfers between devices  26.1 us (24%)
  local copies, waits for them, and re-layouts  5.59 us (5%)
    ppermute x24, waiting for transfers between devices, moved(): lax.ppermute(value, 'seq', [(i, where(i) % cycle) for i in range(cycle)])  26.5 us
    ppermute x24, starting transfers between devices, moved(): lax.ppermute(value, 'seq', [(i, where(i) % cycle) for i in range(cycle)])  18.5 us
    pallas_call x4, Pallas kernels, project(): pl.pallas_call(functools.partial(project_kernel, head_dim, 2.0 / math.sqr...  16.9 us
    pallas_call x6, Pallas kernels, feed_pieces(): pl.pallas_call(functools.partial(pieces_kernel, axis, tuple((piece[2] for...  13.2 us
    pallas_call x1, Pallas kernels, attend(): pl.pallas_call(functools.partial(attend_kernel, axis, cycle), out_shape=(...  6.57 us
    ppermute x4, waiting for transfers between devices, along(): return lax.ppermute(value, 'seq', pairs)  5.41 us
    unnamed x30, local copies, waits for them, and re-layouts  4.67 us
    ppermute x4, starting transfers between devices, along(): return lax.ppermute(value, 'seq', pairs)  4.58 us
  transfers between devices with their start and end apart: 30, of which 13 were waited for; matrix products, arithmetic and copies ran while one was open for 0% of the time, Pallas kernels for 39%

profile of v4, /device:TPU:0, one launch (start us, length us, event | category | flops | bytes accessed | tf_op | source)
XLA Modules:
  0.0 110.5 jit_solution(15880760321975755159)
XLA Ops:
  5.2 5.7 %collective-permute-start.1 = (bf16[192,1024]{1,0:T(8,128)(2,1)}, bf16[192,1024]{1,0:T(8,128)(2,1)S(1)}, u32[]{:S(2)}, u32[]{:S(2)}) collective-permute-start(bf16[192,1024]{1,0:T(8,128)(2,1)} %get-tuple-element.50), channel_id=1, source_target_pairs={{0,15},{1,2},{2,1},{3,4},{4,3},{5,6},{6,5},{7,8},{8,7},{9,10},{10,... | collective-permute-start | bytes 1179656 | tf_op jit(solution)/shard_map/ppermute | solution.py:536
  10.9 2.2 %choose.1 = (bf16[256,1024]{1,0:T(8,128)(2,1)}, bf16[256,1024]{1,0:T(8,128)(2,1)}) custom-call(bf16[256,1024]{1,0:T(8,128)(2,1)} %refs_1_.9, bf16[256,1024]{1,0:T(8,128)(2,1)} %refs_6_.3), custom_call_target="tpu_custom_call" | custom-call | bytes 24576 | tf_op jit(solution)/shard_map/choose/pallas_call | solution.py:106
  15.5 2.8 %copy-done = bf16[1024,3072]{1,0:T(8,128)(2,1)S(1)} copy-done((bf16[1024,3072]{1,0:T(8,128)(2,1)S(1)}, bf16[1024,3072]{1,0:T(8,128)(2,1)}, u32[]{:S(2)}) %copy-start) | copy-done | bytes 6291480
  18.2 7.6 %project.4 = (bf16[384,1024]{1,0:T(8,128)(2,1)S(1)}, bf16[768,2048]{1,0:T(8,128)(2,1)S(1)}) custom-call(bf16[384,1024]{1,0:T(8,128)(2,1)S(1)} %get-tuple-element.67.refs_0_, bf16[384,1024]{1,0:T(8,128)(2,1)S(1)} %collective-permute-done.refs_1_, bf16[1024,3072]{1,0:T(8,128)(2,1)S(1)} %copy-done, f32[1,256]{1,0:T(1,128)S(1)} %broadcast_in_dim_tile.4.refs_3_.refs_5_.refs_2_, ...), custom_call_target="tpu_custom_call" | custom-call | flops 50331648 | bytes 131072 | tf_op jit(solution)/shard_map/project/pallas_call | solution.py:193
  25.9 1.8 %collective-permute-done.2.refs_1_ = bf16[192,1024]{1,0:T(8,128)(2,1)S(1)} collective-permute-done((bf16[192,1024]{1,0:T(8,128)(2,1)}, bf16[192,1024]{1,0:T(8,128)(2,1)S(1)}, u32[]{:S(2)}, u32[]{:S(2)}) %collective-permute-start.2) | collective-permute-done | bytes 393248 | tf_op jit(solution)/shard_map/ppermute | solution.py:536
  27.7 4.7 %collective-permute-start.3 = (bf16[96,1024]{1,0:T(8,128)(2,1)S(1)}, bf16[96,1024]{1,0:T(8,128)(2,1)S(1)}, u32[]{:S(2)}, u32[]{:S(2)}) collective-permute-start(bf16[96,1024]{1,0:T(8,128)(2,1)S(1)} %get-tuple-element.97), channel_id=1, source_target_pairs={{0,1},{1,0},{2,3},{3,2},{4,5},{5,4},{6,7},{7,6},{8,9},{9,8},{10,11... | collective-permute-start | bytes 589832 | tf_op jit(solution)/shard_map/ppermute | solution.py:536
  34.1 3.1 %project.5.near = bf16[384,2048]{1,0:T(8,128)(2,1)S(1)} custom-call(bf16[192,1024]{1,0:T(8,128)(2,1)S(1)} %collective-permute-done.1.refs_0_, bf16[192,1024]{1,0:T(8,128)(2,1)S(1)} %collective-permute-done.2.refs_1_, bf16[1024,3072]{1,0:T(8,128)(2,1)S(1)} %copy-done.1, f32[1,256]{1,0:T(1,128)S(1)} %broadcast_in_dim_tile.4.refs_3_.refs_5_.refs_2_, ...), custom_call_target="tpu_custom_call" | custom-call | flops 25165824 | bytes 131072 | tf_op jit(solution)/shard_map/project/pallas_call | solution.py:193
  37.3 3.1 %project.6.across = bf16[384,2048]{1,0:T(8,128)(2,1)S(1)} custom-call(bf16[96,1024]{1,0:T(8,128)(2,1)S(1)} %collective-permute-done.3.refs_0_, bf16[96,1024]{1,0:T(8,128)(2,1)S(1)} %collective-permute-done.4.refs_1_, bf16[96,1024]{1,0:T(8,128)(2,1)S(1)} %collective-permute-done.5.refs_2_, bf16[96,1024]{1,0:T(8,128)(2,1)S(1)} %collective-permute-done.6.refs_3_, ...), custom_call_target="tpu_custom_call" | custom-call | flops 25165824 | bytes 131072 | tf_op jit(solution)/shard_map/project/pallas_call | solution.py:193
  40.4 6.6 %attend.1 = (f32[384,1024]{1,0:T(8,128)S(1)}, f32[384,1024]{1,0:T(8,128)S(1)}) custom-call(s32[3,8]{1,0:T(4,128)S(1)} %copy-done.8, s32[3]{0:T(128)S(1)} %copy-done.11, bf16[384,1024]{1,0:T(8,128)(2,1)S(1)} %get-tuple-element.52.queries, bf16[768,2048]{1,0:T(8,128)(2,1)S(1)} %get-tuple-element.53.own_mate, bf16[384,2048]{1,0:T(8,128)(2,1)S(1)} %project.5.near, ...), custom_call_target="tpu_custom_call" | custom-call | flops 500000000 | bytes 6291456 | tf_op jit(solution)/shard_map/attend/pallas_call | solution.py:304
  47.0 3.1 %collective-permute-done.8.refs_2_.refs_3_ = bf16[256,1024]{1,0:T(8,128)(2,1)S(1)} collective-permute-done((bf16[256,1024]{1,0:T(8,128)(2,1)}, bf16[256,1024]{1,0:T(8,128)(2,1)S(1)}, u32[]{:S(2)}, u32[]{:S(2)}) %collective-permute-start.8) | collective-permute-done | bytes 524320 | tf_op jit(solution)/shard_map/ppermute | solution.py:546
  50.1 2.4 %collective-permute-start.10 = (bf16[256,1024]{1,0:T(8,128)(2,1)S(1)}, bf16[256,1024]{1,0:T(8,128)(2,1)S(1)}, u32[]{:S(2)}, u32[]{:S(2)}) collective-permute-start(bf16[256,1024]{1,0:T(8,128)(2,1)S(1)} %collective-permute-done.7.refs_3_.refs_4_), channel_id=1, source_target_pairs={{0,4},{1,5},{2,6},{3,7},{4,0},{5,1},{6,2},{7,3},{8,12},{9,13},{10,... | collective-permute-start | bytes 1572872 | tf_op jit(solution)/shard_map/ppermute | solution.py:546
  54.6 3.1 %project.7.window = bf16[384,2048]{1,0:T(8,128)(2,1)S(1)} custom-call(bf16[384,1024]{1,0:T(8,128)(2,1)S(1)} %collective-permute-done.9.refs_0_, bf16[1024,3072]{1,0:T(8,128)(2,1)S(1)} %copy-done.1, f32[1,256]{1,0:T(1,128)S(1)} %broadcast_in_dim_tile.4.refs_3_.refs_5_.refs_2_, f32[1,256]{1,0:T(1,128)S(1)} %broadcast_in_dim_tile.5.refs_4_.refs_6_.refs_3_), custom_call_target="tpu_custom_call" | custom-call | flops 25165824 | bytes 131072 | tf_op jit(solution)/shard_map/project/pallas_call | solution.py:193
  57.8 2.0 %finish.1.attention = bf16[384,1024]{1,0:T(8,128)(2,1)S(1)} custom-call(s32[3,8]{1,0:T(4,128)S(1)} %copy-done.8, s32[3]{0:T(128)S(1)} %copy-done.11, bf16[384,1024]{1,0:T(8,128)(2,1)S(1)} %get-tuple-element.52.queries, bf16[384,2048]{1,0:T(8,128)(2,1)S(1)} %project.7.window, f32[384,1024]{1,0:T(8,128)S(1)} %get-tuple-element.70.mixed, ...), custom_call_target="tpu_custom_call" | custom-call | flops 37748736 | bytes 131072 | tf_op jit(solution)/shard_map/finish/pallas_call | solution.py:365
  59.8 1.9 %attention_output.1 = (bf16[384,1024]{1,0:T(8,128)(2,1)}, bf16[192,1024]{1,0:T(8,128)(2,1)S(1)}, bf16[192,1024]{1,0:T(8,128)(2,1)S(1)}) custom-call(bf16[384,1024]{1,0:T(8,128)(2,1)S(1)} %finish.1.attention, bf16[384,1024]{1,0:T(8,128)(2,1)S(1)} %order.1.ordered, bf16[1024,1024]{1,0:T(8,128)(2,1)S(1)} %copy-done.6, f32[1,1024]{1,0:T(1,128)S(1)} %bitcast.3), custom_call_target="tpu_custom_call" | custom-call | flops 12582912 | bytes 32768 | tf_op jit(solution)/shard_map/attention_output/pallas_call | solution.py:397
  61.8 1.9 %collective-permute-start.12 = (bf16[192,1024]{1,0:T(8,128)(2,1)S(1)}, bf16[192,1024]{1,0:T(8,128)(2,1)S(1)}, u32[]{:S(2)}, u32[]{:S(2)}) collective-permute-start(bf16[192,1024]{1,0:T(8,128)(2,1)S(1)} %get-tuple-element.76.refs_0_), channel_id=1, source_target_pairs={{0,2},{1,3},{2,0},{3,1},{4,6},{5,7},{6,4},{7,5},{8,10},{9,11},{10,... | collective-permute-start | bytes 1179656 | tf_op jit(solution)/shard_map/ppermute | solution.py:536
  63.7 1.7 %collective-permute-done.10.refs_4_.refs_5_ = bf16[256,1024]{1,0:T(8,128)(2,1)S(1)} collective-permute-done((bf16[256,1024]{1,0:T(8,128)(2,1)S(1)}, bf16[256,1024]{1,0:T(8,128)(2,1)S(1)}, u32[]{:S(2)}, u32[]{:S(2)}) %collective-permute-start.10) | collective-permute-done | bytes 524320 | tf_op jit(solution)/shard_map/ppermute | solution.py:546
  66.8 6.8 %collective-permute-done.17.refs_0_ = bf16[192,1024]{1,0:T(8,128)(2,1)S(1)} collective-permute-done((bf16[192,1024]{1,0:T(8,128)(2,1)S(1)}, bf16[192,1024]{1,0:T(8,128)(2,1)S(1)}, u32[]{:S(2)}, u32[]{:S(2)}) %collective-permute-start.17) | collective-permute-done | bytes 393248 | tf_op jit(solution)/shard_map/ppermute | solution.py:536
  74.2 6.9 %collective-permute-done.12.refs_0_ = bf16[192,1024]{1,0:T(8,128)(2,1)S(1)} collective-permute-done((bf16[192,1024]{1,0:T(8,128)(2,1)S(1)}, bf16[192,1024]{1,0:T(8,128)(2,1)S(1)}, u32[]{:S(2)}, u32[]{:S(2)}) %collective-permute-start.12) | collective-permute-done | bytes 393248 | tf_op jit(solution)/shard_map/ppermute | solution.py:536
  87.1 2.4 %feed_pieces.8 = bf16[192,1024]{1,0:T(8,128)(2,1)S(1)} custom-call(bf16[192,1024]{1,0:T(8,128)(2,1)S(1)} %collective-permute-done.12.refs_0_, bf16[256,1024]{1,0:T(8,128)(2,1)S(1)} %copy-done.2, bf16[256,1024]{1,0:T(8,128)(2,1)S(1)} %collective-permute-done.8.refs_2_.refs_3_, bf16[256,1024]{1,0:T(8,128)(2,1)S(1)} %collective-permute-done.7.refs_3_.refs_4_, ...), custom_call_target="tpu_custom_call" | custom-call | flops 15728640 | bytes 81920 | tf_op jit(solution)/shard_map/feed_pieces/pallas_call | solution.py:441
  90.1 2.4 %feed_pieces.11 = bf16[192,1024]{1,0:T(8,128)(2,1)S(1)} custom-call(bf16[192,1024]{1,0:T(8,128)(2,1)S(1)} %collective-permute-done.17.refs_0_, bf16[256,1024]{1,0:T(8,128)(2,1)S(1)} %copy-done.2, bf16[256,1024]{1,0:T(8,128)(2,1)S(1)} %collective-permute-done.8.refs_2_.refs_3_, bf16[256,1024]{1,0:T(8,128)(2,1)S(1)} %collective-permute-done.7.refs_3_.refs_4_, ...), custom_call_target="tpu_custom_call" | custom-call | flops 15728640 | bytes 81920 | tf_op jit(solution)/shard_map/feed_pieces/pallas_call | solution.py:441
  92.5 1.6 %collective-permute-start.29 = (bf16[192,1024]{1,0:T(8,128)(2,1)S(1)}, bf16[192,1024]{1,0:T(8,128)(2,1)S(1)}, u32[]{:S(2)}, u32[]{:S(2)}) collective-permute-start(bf16[192,1024]{1,0:T(8,128)(2,1)S(1)} %feed_pieces.11), channel_id=1, source_target_pairs={{0,2},{1,3},{2,0},{3,1},{4,6},{5,7},{6,4},{7,5},{8,10},{9,11},{10,... | collective-permute-start | bytes 1179656 | tf_op jit(solution)/shard_map/ppermute | solution.py:536
  94.2 7.4 %collective-permute-done.21.refs_0_ = bf16[192,1024]{1,0:T(8,128)(2,1)S(1)} collective-permute-done((bf16[192,1024]{1,0:T(8,128)(2,1)S(1)}, bf16[192,1024]{1,0:T(8,128)(2,1)S(1)}, u32[]{:S(2)}, u32[]{:S(2)}) %collective-permute-start.21) | collective-permute-done | bytes 393248 | tf_op jit(solution)/shard_map/ppermute | solution.py:536
  101.6 2.0 %feed_pieces.9 = (bf16[96,1024]{1,0:T(8,128)(2,1)S(1)}, bf16[96,1024]{1,0:T(8,128)(2,1)S(1)}, bf16[96,1024]{1,0:T(8,128)(2,1)S(1)}, bf16[96,1024]{1,0:T(8,128)(2,1)S(1)}) custom-call(bf16[192,1024]{1,0:T(8,128)(2,1)S(1)} %collective-permute-done.22.refs_0_, bf16[192,1024]{1,0:T(8,128)(2,1)S(1)} %collective-permute-done.23.refs_1_, ...), custom_call_target="tpu_custom_call" | custom-call | flops 18874368 | bytes 49152 | tf_op jit(solution)/shard_map/feed_pieces/pallas_call | solution.py:441
  106.0 3.4 %feed_pieces.10.own = f32[384,1024]{1,0:T(8,128)S(1)} custom-call(bf16[192,1024]{1,0:T(8,128)(2,1)S(1)} %get-tuple-element.76.refs_0_, bf16[192,1024]{1,0:T(8,128)(2,1)S(1)} %get-tuple-element.77.refs_1_, bf16[256,1024]{1,0:T(8,128)(2,1)S(1)} %copy-done.2, bf16[256,1024]{1,0:T(8,128)(2,1)S(1)} %collective-permute-done.8.refs_2_.refs_3_, ...), custom_call_target="tpu_custom_call" | custom-call | flops 31457280 | bytes 81920 | tf_op jit(solution)/shard_map/feed_pieces/pallas_call | solution.py:441
  (90 shorter events, 23.1 us)
Async XLA Ops:
  4.8 10.7 %collective-permute-start = (bf16[384,1024]{1,0:T(8,128)(2,1)S(1)}, bf16[384,1024]{1,0:T(8,128)(2,1)S(1)}, u32[]{:S(2)}, u32[]{:S(2)}) collective-permute-start(bf16[384,1024]{1,0:T(8,128)(2,1)S(1)} %get-tuple-element.67.refs_0_), channel_id=1, source_target_pairs={{0,1},{1,0},{2,3},{3,2},{4,5},{5,4},{6,7},{7,6},{8,9},{9,8},{10,11... | collective-permute-start | bytes 2359304 | tf_op jit(solution)/shard_map/ppermute | solution.py:536
  5.2 20.7 %collective-permute-start.1 = (bf16[192,1024]{1,0:T(8,128)(2,1)}, bf16[192,1024]{1,0:T(8,128)(2,1)S(1)}, u32[]{:S(2)}, u32[]{:S(2)}) collective-permute-start(bf16[192,1024]{1,0:T(8,128)(2,1)} %get-tuple-element.50), channel_id=1, source_target_pairs={{0,15},{1,2},{2,1},{3,4},{4,3},{5,6},{6,5},{7,8},{8,7},{9,10},{10,... | collective-permute-start | bytes 1179656 | tf_op jit(solution)/shard_map/ppermute | solution.py:536
  10.9 16.8 %collective-permute-start.2 = (bf16[192,1024]{1,0:T(8,128)(2,1)}, bf16[192,1024]{1,0:T(8,128)(2,1)S(1)}, u32[]{:S(2)}, u32[]{:S(2)}) collective-permute-start(bf16[192,1024]{1,0:T(8,128)(2,1)} %get-tuple-element.51), channel_id=1, source_target_pairs={{0,15},{1,2},{2,1},{3,4},{4,3},{5,6},{6,5},{7,8},{8,7},{9,10},{10,... | collective-permute-start | bytes 1179656 | tf_op jit(solution)/shard_map/ppermute | solution.py:536
  13.1 33.9 %collective-permute-start.7 = (bf16[256,1024]{1,0:T(8,128)(2,1)}, bf16[256,1024]{1,0:T(8,128)(2,1)S(1)}, u32[]{:S(2)}, u32[]{:S(2)}) collective-permute-start(bf16[256,1024]{1,0:T(8,128)(2,1)} %get-tuple-element.63), channel_id=1, source_target_pairs={{0,8},{1,9},{2,10},{3,11},{4,12},{5,13},{6,14},{7,15},{8,0},{9,1},... | collective-permute-start | bytes 1572872 | tf_op jit(solution)/shard_map/ppermute | solution.py:546
  13.7 36.4 %collective-permute-start.8 = (bf16[256,1024]{1,0:T(8,128)(2,1)}, bf16[256,1024]{1,0:T(8,128)(2,1)S(1)}, u32[]{:S(2)}, u32[]{:S(2)}) collective-permute-start(bf16[256,1024]{1,0:T(8,128)(2,1)} %get-tuple-element.63), channel_id=1, source_target_pairs={{0,4},{1,5},{2,6},{3,7},{4,0},{5,1},{6,2},{7,3},{8,12},{9,13},{10,... | collective-permute-start | bytes 1572872 | tf_op jit(solution)/shard_map/ppermute | solution.py:546
  27.6 27.0 %collective-permute-start.9 = (bf16[384,1024]{1,0:T(8,128)(2,1)S(1)}, bf16[384,1024]{1,0:T(8,128)(2,1)S(1)}, u32[]{:S(2)}, u32[]{:S(2)}) collective-permute-start(bf16[384,1024]{1,0:T(8,128)(2,1)S(1)} %get-tuple-element.67.refs_0_), channel_id=1, source_target_pairs={{0,2},{1,15},{2,4},{3,1},{4,6},{5,3},{6,8},{7,5},{8,10},{9,7},{10,... | collective-permute-start | bytes 2359304 | tf_op jit(solution)/shard_map/ppermute | solution.py:536
  27.7 5.8 %collective-permute-start.3 = (bf16[96,1024]{1,0:T(8,128)(2,1)S(1)}, bf16[96,1024]{1,0:T(8,128)(2,1)S(1)}, u32[]{:S(2)}, u32[]{:S(2)}) collective-permute-start(bf16[96,1024]{1,0:T(8,128)(2,1)S(1)} %get-tuple-element.97), channel_id=1, source_target_pairs={{0,1},{1,0},{2,3},{3,2},{4,5},{5,4},{6,7},{7,6},{8,9},{9,8},{10,11... | collective-permute-start | bytes 589832 | tf_op jit(solution)/shard_map/ppermute | solution.py:536
  33.5 3.8 %collective-permute-start.5 = (bf16[96,1024]{1,0:T(8,128)(2,1)S(1)}, bf16[96,1024]{1,0:T(8,128)(2,1)S(1)}, u32[]{:S(2)}, u32[]{:S(2)}) collective-permute-start(bf16[96,1024]{1,0:T(8,128)(2,1)S(1)} %get-tuple-element.95), channel_id=1, source_target_pairs={{0,1},{1,0},{2,3},{3,2},{4,5},{5,4},{6,7},{7,6},{8,9},{9,8},{10,11... | collective-permute-start | bytes 589832 | tf_op jit(solution)/shard_map/ppermute | solution.py:536
  33.9 3.4 %collective-permute-start.6 = (bf16[96,1024]{1,0:T(8,128)(2,1)S(1)}, bf16[96,1024]{1,0:T(8,128)(2,1)S(1)}, u32[]{:S(2)}, u32[]{:S(2)}) collective-permute-start(bf16[96,1024]{1,0:T(8,128)(2,1)S(1)} %get-tuple-element.94), channel_id=1, source_target_pairs={{0,1},{1,0},{2,3},{3,2},{4,5},{5,4},{6,7},{7,6},{8,9},{9,8},{10,11... | collective-permute-start | bytes 589832 | tf_op jit(solution)/shard_map/ppermute | solution.py:536
  50.1 15.2 %collective-permute-start.10 = (bf16[256,1024]{1,0:T(8,128)(2,1)S(1)}, bf16[256,1024]{1,0:T(8,128)(2,1)S(1)}, u32[]{:S(2)}, u32[]{:S(2)}) collective-permute-start(bf16[256,1024]{1,0:T(8,128)(2,1)S(1)} %collective-permute-done.7.refs_3_.refs_4_), channel_id=1, source_target_pairs={{0,4},{1,5},{2,6},{3,7},{4,0},{5,1},{6,2},{7,3},{8,12},{9,13},{10,... | collective-permute-start | bytes 1572872 | tf_op jit(solution)/shard_map/ppermute | solution.py:546
  52.5 21.7 %collective-permute-start.13 = (bf16[256,1024]{1,0:T(8,128)(2,1)S(1)}, bf16[256,1024]{1,0:T(8,128)(2,1)S(1)}, u32[]{:S(2)}, u32[]{:S(2)}) collective-permute-start(bf16[256,1024]{1,0:T(8,128)(2,1)S(1)} %copy-done.14), channel_id=1, source_target_pairs={{0,4},{1,5},{2,6},{3,7},{4,0},{5,1},{6,2},{7,3},{8,12},{9,13},{10,... | collective-permute-start | bytes 1572872 | tf_op jit(solution)/shard_map/ppermute | solution.py:546
  52.5 21.7 %collective-permute-start.14 = (bf16[256,1024]{1,0:T(8,128)(2,1)S(1)}, bf16[256,1024]{1,0:T(8,128)(2,1)S(1)}, u32[]{:S(2)}, u32[]{:S(2)}) collective-permute-start(bf16[256,1024]{1,0:T(8,128)(2,1)S(1)} %collective-permute-done.7.refs_3_.refs_4_), channel_id=1, source_target_pairs={{0,16},{16,0},{1,17},{17,1},{2,18},{18,2},{3,19},{19,3},{4,20},{20... | collective-permute-start | bytes 1572872 | tf_op jit(solution)/shard_map/ppermute | solution.py:552
  61.6 12.0 %collective-permute-start.17 = (bf16[192,1024]{1,0:T(8,128)(2,1)S(1)}, bf16[192,1024]{1,0:T(8,128)(2,1)S(1)}, u32[]{:S(2)}, u32[]{:S(2)}) collective-permute-start(bf16[192,1024]{1,0:T(8,128)(2,1)S(1)} %get-tuple-element.77.refs_1_), channel_id=1, source_target_pairs={{0,2},{1,3},{2,0},{3,1},{4,6},{5,7},{6,4},{7,5},{8,10},{9,11},{10,... | collective-permute-start | bytes 1179656 | tf_op jit(solution)/shard_map/ppermute | solution.py:536
  61.8 19.4 %collective-permute-start.12 = (bf16[192,1024]{1,0:T(8,128)(2,1)S(1)}, bf16[192,1024]{1,0:T(8,128)(2,1)S(1)}, u32[]{:S(2)}, u32[]{:S(2)}) collective-permute-start(bf16[192,1024]{1,0:T(8,128)(2,1)S(1)} %get-tuple-element.76.refs_0_), channel_id=1, source_target_pairs={{0,2},{1,3},{2,0},{3,1},{4,6},{5,7},{6,4},{7,5},{8,10},{9,11},{10,... | collective-permute-start | bytes 1179656 | tf_op jit(solution)/shard_map/ppermute | solution.py:536
  65.3 19.2 %collective-permute-start.15 = (bf16[256,1024]{1,0:T(8,128)(2,1)S(1)}, bf16[256,1024]{1,0:T(8,128)(2,1)S(1)}, u32[]{:S(2)}, u32[]{:S(2)}) collective-permute-start(bf16[256,1024]{1,0:T(8,128)(2,1)S(1)} %collective-permute-done.10.refs_4_.refs_5_), channel_id=1, source_target_pairs={{0,16},{16,0},{1,17},{17,1},{2,18},{18,2},{3,19},{19,3},{4,20},{20... | collective-permute-start | bytes 1572872 | tf_op jit(solution)/shard_map/ppermute | solution.py:552
  73.6 8.0 %collective-permute-start.18 = (bf16[192,1024]{1,0:T(8,128)(2,1)S(1)}, bf16[192,1024]{1,0:T(8,128)(2,1)S(1)}, u32[]{:S(2)}, u32[]{:S(2)}) collective-permute-start(bf16[192,1024]{1,0:T(8,128)(2,1)S(1)} %collective-permute-done.17.refs_0_), channel_id=1, source_target_pairs={{0,1},{1,0},{2,3},{3,2},{4,5},{5,4},{6,7},{7,6},{8,9},{9,8},{10,11... | collective-permute-start | bytes 1179656 | tf_op jit(solution)/shard_map/ppermute | solution.py:536
  81.1 4.5 %collective-permute-start.11 = (bf16[256,1024]{1,0:T(8,128)(2,1)S(1)}, bf16[256,1024]{1,0:T(8,128)(2,1)S(1)}, u32[]{:S(2)}, u32[]{:S(2)}) collective-permute-start(bf16[256,1024]{1,0:T(8,128)(2,1)S(1)} %collective-permute-done.10.refs_4_.refs_5_), channel_id=1, source_target_pairs={{0,1},{1,0},{2,3},{3,2},{4,5},{5,4},{6,7},{7,6},{8,9},{9,8},{10,11... | collective-permute-start | bytes 1572872 | tf_op jit(solution)/shard_map/ppermute | solution.py:536
  84.6 2.5 %collective-permute-start.19 = (bf16[256,1024]{1,0:T(8,128)(2,1)S(1)}, bf16[256,1024]{1,0:T(8,128)(2,1)S(1)}, u32[]{:S(2)}, u32[]{:S(2)}) collective-permute-start(bf16[256,1024]{1,0:T(8,128)(2,1)S(1)} %collective-permute-done.15.refs_9_.refs_10_), channel_id=1, source_target_pairs={{0,1},{1,0},{2,3},{3,2},{4,5},{5,4},{6,7},{7,6},{8,9},{9,8},{10,11... | collective-permute-start | bytes 1572872 | tf_op jit(solution)/shard_map/ppermute | solution.py:536
  84.6 2.5 %collective-permute-start.20 = (bf16[192,1024]{1,0:T(8,128)(2,1)S(1)}, bf16[192,1024]{1,0:T(8,128)(2,1)S(1)}, u32[]{:S(2)}, u32[]{:S(2)}) collective-permute-start(bf16[192,1024]{1,0:T(8,128)(2,1)S(1)} %feed_pieces.6), channel_id=1, source_target_pairs={{0,1},{1,0},{2,3},{3,2},{4,5},{5,4},{6,7},{7,6},{8,9},{9,8},{10,11... | collective-permute-start | bytes 1179656 | tf_op jit(solution)/shard_map/ppermute | solution.py:536
  85.1 5.0 %collective-permute-start.28 = (bf16[192,1024]{1,0:T(8,128)(2,1)S(1)}, bf16[192,1024]{1,0:T(8,128)(2,1)S(1)}, u32[]{:S(2)}, u32[]{:S(2)}) collective-permute-start(bf16[192,1024]{1,0:T(8,128)(2,1)S(1)} %feed_pieces.7), channel_id=1, source_target_pairs={{0,1},{1,0},{2,3},{3,2},{4,5},{5,4},{6,7},{7,6},{8,9},{9,8},{10,11... | collective-permute-start | bytes 1179656 | tf_op jit(solution)/shard_map/ppermute | solution.py:536
  85.2 8.9 %collective-permute-start.22 = (bf16[192,1024]{1,0:T(8,128)(2,1)S(1)}, bf16[192,1024]{1,0:T(8,128)(2,1)S(1)}, u32[]{:S(2)}, u32[]{:S(2)}) collective-permute-start(bf16[192,1024]{1,0:T(8,128)(2,1)S(1)} %get-tuple-element.76.refs_0_), channel_id=1, source_target_pairs={{0,1},{1,0},{2,3},{3,2},{4,5},{5,4},{6,7},{7,6},{8,9},{9,8},{10,11... | collective-permute-start | bytes 1179656 | tf_op jit(solution)/shard_map/ppermute | solution.py:536
  85.7 8.5 %collective-permute-start.23 = (bf16[192,1024]{1,0:T(8,128)(2,1)S(1)}, bf16[192,1024]{1,0:T(8,128)(2,1)S(1)}, u32[]{:S(2)}, u32[]{:S(2)}) collective-permute-start(bf16[192,1024]{1,0:T(8,128)(2,1)S(1)} %get-tuple-element.77.refs_1_), channel_id=1, source_target_pairs={{0,1},{1,0},{2,3},{3,2},{4,5},{5,4},{6,7},{7,6},{8,9},{9,8},{10,11... | collective-permute-start | bytes 1179656 | tf_op jit(solution)/shard_map/ppermute | solution.py:536
  89.6 12.0 %collective-permute-start.21 = (bf16[192,1024]{1,0:T(8,128)(2,1)S(1)}, bf16[192,1024]{1,0:T(8,128)(2,1)S(1)}, u32[]{:S(2)}, u32[]{:S(2)}) collective-permute-start(bf16[192,1024]{1,0:T(8,128)(2,1)S(1)} %feed_pieces.8), channel_id=1, source_target_pairs={{0,2},{1,3},{2,0},{3,1},{4,6},{5,7},{6,4},{7,5},{8,10},{9,11},{10,... | collective-permute-start | bytes 1179656 | tf_op jit(solution)/shard_map/ppermute | solution.py:536
  92.5 16.8 %collective-permute-start.29 = (bf16[192,1024]{1,0:T(8,128)(2,1)S(1)}, bf16[192,1024]{1,0:T(8,128)(2,1)S(1)}, u32[]{:S(2)}, u32[]{:S(2)}) collective-permute-start(bf16[192,1024]{1,0:T(8,128)(2,1)S(1)} %feed_pieces.11), channel_id=1, source_target_pairs={{0,2},{1,3},{2,0},{3,1},{4,6},{5,7},{6,4},{7,5},{8,10},{9,11},{10,... | collective-permute-start | bytes 1179656 | tf_op jit(solution)/shard_map/ppermute | solution.py:536
  (21 other events, 144.6 us)

commit v5 on v4

--- a/solution.py
+++ b/solution.py
@@ -56,25 +56,16 @@
         part[...] = found[index * size : (index + 1) * size]
 
 
-def order_kernel(axis, features, order, ordered):
-    ordered[...] = ordered_rows(axis, features, order).astype(jnp.bfloat16)
-
-
-def prepare(features, order, gain=None):
+def prepare(features, order, gain):
     rows, width = features.shape
-    shapes = [jax.ShapeDtypeStruct((rows, width), jnp.bfloat16)]
-    if gain is not None:
-        shapes += [jax.ShapeDtypeStruct((rows // 2, width), jnp.bfloat16)] * 2
-    operands = [features, order.reshape(1, rows)]
-    if gain is not None:
-        operands.append(gain.reshape(1, width))
-    return pl.pallas_call(
-        functools.partial(order_kernel if gain is None else norm_kernel, "seq"),
-        out_shape=shapes,
+    half = jax.ShapeDtypeStruct((rows // 2, width), jnp.bfloat16)
+    return pl.pallas_call(
+        functools.partial(norm_kernel, "seq"),
+        out_shape=[jax.ShapeDtypeStruct((rows, width), jnp.bfloat16), half, half],
         compiler_params=pltpu.CompilerParams(vmem_limit_bytes=16 * MIB),
         cost_estimate=cost(2 * rows * rows * width, 6 * rows * width),
-        name="order" if gain is None else "norm",
-    )(*operands)
+        name="norm",
+    )(features, order, gain.reshape(1, width))
 
 
 def choose_kernel(axis, one, other, chosen, left, arrived):
@@ -155,7 +146,11 @@
             at += chunk
 
 
-def project_kernel(head_dim, scale, count, with_queries, *refs):
+def project_kernel(axis, head_dim, scale, count, with_queries, *refs):
+    if with_queries:
+        features, order, *refs, ordered, key_values, gathered = refs
+        ordered[...] = ordered_rows(axis, features, order).astype(jnp.bfloat16)
+        refs = [*refs, key_values, gathered]
     sources = refs[:count]
     weights, query_gain, key_gain, *rest = refs[count:]
     queries = rest[0] if with_queries else None
@@ -182,26 +177,27 @@
     )
 
 
-def project(sources, weights, query_gain, key_gain, with_queries):
+def project(sources, weights, query_gain, key_gain, unordered=()):
+    with_queries = bool(unordered)
     width = sources[0].shape[1]
     rows = sum(source.shape[0] for source in sources)
     head_dim = query_gain.shape[0]
     shapes = [jax.ShapeDtypeStruct((rows, 2 * width), jnp.bfloat16)]
     if with_queries:
-        shapes.insert(0, jax.ShapeDtypeStruct(sources[0].shape, jnp.bfloat16))
+        shapes = [jax.ShapeDtypeStruct(sources[0].shape, jnp.bfloat16)] * 2 + shapes
     local = pl.BlockSpec(memory_space=pltpu.VMEM)
     return pl.pallas_call(
         functools.partial(
-            project_kernel, head_dim, 2.0 / math.sqrt(head_dim), len(sources), with_queries
+            project_kernel, "seq", head_dim, 2.0 / math.sqrt(head_dim), len(sources), with_queries
         ),
         out_shape=shapes,
-        in_specs=[local] * (len(sources) + 3),
+        in_specs=[local] * (len(unordered) + len(sources) + 3),
         out_specs=[local] * len(shapes),
         scratch_shapes=[pltpu.VMEM((rows, width), jnp.bfloat16)],
         compiler_params=pltpu.CompilerParams(vmem_limit_bytes=24 * MIB),
         cost_estimate=cost(4 * rows * width * width, 8 * width * width),
         name="project",
-    )(*sources, weights, jnp.tile(query_gain, 4)[None], jnp.tile(key_gain, 4)[None])
+    )(*unordered, *sources, weights, jnp.tile(query_gain, 4)[None], jnp.tile(key_gain, 4)[None])
 
 
 def slot_of(block, me, cycle, blocks):
@@ -403,12 +399,13 @@
     )(attention, ordered, weights, gain.reshape(1, width))
 
 
-def pieces_kernel(axis, swaps, sources, bases, *refs):
+def pieces_kernel(axis, swaps, sources, bases, has_known, *refs):
     count = len(swaps)
     seconds, refs = refs[:sources], refs[sources:]
     firsts, refs = refs[:count], refs[count:]
     lasts, refs = refs[:count], refs[count:]
-    base, results = refs[:bases], refs[bases:]
+    base, refs = refs[:bases], refs[bases:]
+    known, results = (refs[0], refs[1:]) if has_known else (None, refs)
     straight = lax.axis_index(axis) == 0
     rows = jnp.concatenate([second[...] for second in seconds], axis=0)
     total = None
@@ -426,27 +423,29 @@
         part = jnp.dot(active, last_rows, preferred_element_type=jnp.float32)
         total = part if total is None else total + part
     if bases:
-        known = jnp.concatenate([part[...] for part in base], axis=0)
-        total = total + known.astype(jnp.float32)
+        total = total + jnp.concatenate([part[...] for part in base], axis=0).astype(jnp.float32)
+    if has_known:
+        total = total + known[...]
     part = total.shape[0] // len(results)
     for index, result in enumerate(results):
         result[...] = total[index * part : (index + 1) * part].astype(result.dtype)
 
 
-def feed_pieces(axis, seconds, pieces, base, dtype, parts=1):
+def feed_pieces(axis, seconds, pieces, base, dtype, parts=1, known=None):
     rows = sum(second.shape[0] for second in seconds)
     width = seconds[0].shape[1]
     hidden = sum(piece[0].shape[0] for piece in pieces)
     operands = [*seconds] + [piece[0] for piece in pieces] + [piece[1] for piece in pieces]
     return pl.pallas_call(
         functools.partial(
-            pieces_kernel, axis, tuple(piece[2] for piece in pieces), len(seconds), len(base)
+            pieces_kernel, axis, tuple(piece[2] for piece in pieces), len(seconds), len(base),
+            known is not None,
         ),
         out_shape=[jax.ShapeDtypeStruct((rows // parts, width), dtype)] * parts,
         compiler_params=pltpu.CompilerParams(vmem_limit_bytes=24 * MIB),
         cost_estimate=cost(4 * rows * width * hidden, 4 * hidden * width),
         name="feed_pieces",
-    )(*operands, *base)
+    )(*operands, *base, *([] if known is None else [known]))
 
 
 def total_kernel(attended, own, *refs):
@@ -557,21 +556,21 @@
         prime, left = choose("parts", w_in, w_out)
         pair_rows = along(prime, swap)
         third = along(prime, [(0, 2), (1, 3), (2, 0), (3, 1)])
-    normed, *normed_parts = prepare(pore_features, pore_order, norm1_gain)
+    order = pore_order.reshape(1, rows)
+    normed, *normed_parts = prepare(pore_features, order, norm1_gain)
     near = [moved(part, lambda i: i - 1 + 2 * (i % 2)) for part in normed_parts]
     mate = mate_of(normed)
-    queries, own_mate = project([normed, mate], w_qkv, query_gain, key_gain, True)
-    queries, late_normed, late_features, *near = lax.optimization_barrier(
-        (queries, normed, pore_features, *near)
-    )
+    queries, ordered, own_mate = project(
+        [normed, mate], w_qkv, query_gain, key_gain, (pore_features, order)
+    )
+    queries, late_normed, *near = lax.optimization_barrier((queries, normed, *near))
     far = moved(late_normed, lambda i: i + 2 - 4 * (i % 2))
-    (ordered,) = prepare(late_features, pore_order)
     across = [mate_of(piece) for part in near for piece in jnp.split(part, 2)]
 
-    (near_kv,) = project(near, w_qkv, query_gain, key_gain, False)
+    (near_kv,) = project(near, w_qkv, query_gain, key_gain)
     if shared:
         near_kv, *across = lax.optimization_barrier((near_kv, *across))
-    (across_kv,) = project(across, w_qkv, query_gain, key_gain, False)
+    (across_kv,) = project(across, w_qkv, query_gain, key_gain)
     mixed, totals = attend(
         "seq", cycle, block_lists, block_counts, queries, [own_mate, near_kv, across_kv]
     )
@@ -582,8 +581,8 @@
         other_pair = along(left, swap)
         fourth = along(third, swap)
         other_third = over(third)
-        mixed, totals, far, ordered = lax.optimization_barrier((mixed, totals, far, ordered))
-    (far_kv,) = project([far], w_qkv, query_gain, key_gain, False)
+        mixed, totals, far = lax.optimization_barrier((mixed, totals, far))
+    (far_kv,) = project([far], w_qkv, query_gain, key_gain)
     attention = finish(
         "seq", cycle, block_lists, block_counts, queries, far_kv, mixed, totals
     )
@@ -602,25 +601,28 @@
             (pair_rows, other_pair, True),
             (third, other_third, True),
         ]
-        guest_mate_parts = [
-            feed_pieces("parts", [mate_of(guest)], pieces, [], jnp.bfloat16)[0] for guest in guests
-        ]
+        guest_mate_parts = feed_pieces(
+            "parts", [mate_of(guest) for guest in guests], pieces, [], jnp.bfloat16, parts
+        )
         other_fourth, *guest_mate_parts = lax.optimization_barrier(
             (other_fourth, *guest_mate_parts)
         )
-        every = [
-            *pieces,
+        last = [
             (fourth, other_fourth, True),
             (mate_of(fourth), mate_of(other_fourth), True),
         ]
+        guest_parts = feed_pieces("parts", guests, pieces, [], jnp.float32, parts)
         returned = []
-        for guest, part in zip(guests, guest_mate_parts):
-            (guest_part,) = feed_pieces("parts", [guest], every, [mate_of(part)], jnp.bfloat16)
+        for guest, part, base in zip(guests, guest_parts, guest_mate_parts):
+            (guest_part,) = feed_pieces(
+                "parts", [guest], last, [mate_of(base)], jnp.bfloat16, 1, part
+            )
             returned.append(beside(guest_part))
-        returned[0], *mate_seconds = lax.optimization_barrier((returned[0], *mate_seconds))
         mate_parts = feed_pieces("parts", mate_seconds, pieces, [], jnp.bfloat16, 4)
+        (own_main,) = feed_pieces("parts", seconds, pieces, [], jnp.float32)
+        returned[0], own_main = lax.optimization_barrier((returned[0], own_main))
         (own_part,) = feed_pieces(
-            "parts", seconds, every, [mate_of(part) for part in mate_parts], jnp.float32
+            "parts", seconds, last, [mate_of(part) for part in mate_parts], jnp.float32, 1, own_main
         )
         layer_output = total_of(attended, own_part, returned)
     else:

time: 111 us -> 109 us (0.982)
    ppermute x24, waiting for transfers between devices: 26.5 us -> 17.9 us  [moved(): lax.ppermute(value, 'seq', [(i, where(i) % cycle) for i in range(cycle)])]
    ppermute x4, waiting for transfers between devices: 5.41 us -> 13 us  [along(): return lax.ppermute(value, 'seq', pairs)]
    pallas_call x6 -> x7, Pallas kernels: 13.2 us -> 11.1 us  [feed_pieces(): pl.pallas_call(functools.partial(pieces_kernel, axis, tuple((piece[2] for...]
    pallas_call x6 -> x5, Pallas kernels: 19.1 us -> 20.3 us  [the longest x4 18.7 us: project(): pl.pallas_call(functools.partial(project_kernel, 'seq', head_dim, 2.0 / m...]
  transfers between devices with their start and end apart: 30 -> 30, of which waited for: 13 -> 8; matrix products, arithmetic and copies ran while one was open for 0% -> 0% of each run, Pallas kernels for 39% -> 39%
where the time goes in v5:
time: 109 us; the launch traced here: 108 us
  Pallas kernels  44.8 us (41%)
  waiting for transfers between devices  30.9 us (28%)
  starting transfers between devices  25.7 us (24%)
  local copies, waits for them, and re-layouts  5.59 us (5%)
    pallas_call x4, Pallas kernels, project(): pl.pallas_call(functools.partial(project_kernel, 'seq', head_dim, 2.0 / m...  18.7 us
    ppermute x24, starting transfers between devices, moved(): lax.ppermute(value, 'seq', [(i, where(i) % cycle) for i in range(cycle)])  18.2 us
    ppermute x24, waiting for transfers between devices, moved(): lax.ppermute(value, 'seq', [(i, where(i) % cycle) for i in range(cycle)])  17.9 us
    ppermute x4, waiting for transfers between devices, along(): return lax.ppermute(value, 'seq', pairs)  13 us
    pallas_call x7, Pallas kernels, feed_pieces(): pl.pallas_call(functools.partial(pieces_kernel, axis, tuple((piece[2] for...  11.1 us
    pallas_call x1, Pallas kernels, attend(): pl.pallas_call(functools.partial(attend_kernel, axis, cycle), out_shape=(...  6.39 us
    unnamed x30, local copies, waits for them, and re-layouts  4.67 us
    ppermute x4, starting transfers between devices, along(): return lax.ppermute(value, 'seq', pairs)  4.58 us
  transfers between devices with their start and end apart: 30, of which 8 were waited for; matrix products, arithmetic and copies ran while one was open for 0% of the time, Pallas kernels for 39%

profile of v5, /device:TPU:0, one launch (start us, length us, event | category | flops | bytes accessed | tf_op | source)
XLA Modules:
  0.0 108.0 jit_solution(2962265633043801296)
XLA Ops:
  3.2 1.6 %norm.1 = (bf16[384,1024]{1,0:T(8,128)(2,1)S(1)}, bf16[192,1024]{1,0:T(8,128)(2,1)}, bf16[192,1024]{1,0:T(8,128)(2,1)}) custom-call(bf16[384,1024]{1,0:T(8,128)(2,1)S(1)} %copy-done.4, s32[1,384]{1,0:T(1,128)S(1)} %reshape.15.order.refs_1_, f32[1,1024]{1,0:T(1,128)S(1)} %bitcast.2), custom_call_target="tpu_custom_call" | custom-call | flops 4718592 | bytes 36864 | tf_op jit(solution)/shard_map/norm/pallas_call | solution.py:62
  5.2 5.7 %collective-permute-start.1 = (bf16[192,1024]{1,0:T(8,128)(2,1)}, bf16[192,1024]{1,0:T(8,128)(2,1)S(1)}, u32[]{:S(2)}, u32[]{:S(2)}) collective-permute-start(bf16[192,1024]{1,0:T(8,128)(2,1)} %get-tuple-element.52), channel_id=1, source_target_pairs={{0,15},{1,2},{2,1},{3,4},{4,3},{5,6},{6,5},{7,8},{8,7},{9,10},{10,... | collective-permute-start | bytes 1179656 | tf_op jit(solution)/shard_map/ppermute | solution.py:535
  10.9 2.2 %choose.1 = (bf16[256,1024]{1,0:T(8,128)(2,1)}, bf16[256,1024]{1,0:T(8,128)(2,1)}) custom-call(bf16[256,1024]{1,0:T(8,128)(2,1)} %refs_2_.9, bf16[256,1024]{1,0:T(8,128)(2,1)} %refs_5_.7), custom_call_target="tpu_custom_call" | custom-call | bytes 24576 | tf_op jit(solution)/shard_map/choose/pallas_call | solution.py:97
  13.7 1.6 %collective-permute-start.8 = (bf16[256,1024]{1,0:T(8,128)(2,1)}, bf16[256,1024]{1,0:T(8,128)(2,1)S(1)}, u32[]{:S(2)}, u32[]{:S(2)}) collective-permute-start(bf16[256,1024]{1,0:T(8,128)(2,1)} %get-tuple-element.65), channel_id=1, source_target_pairs={{0,4},{1,5},{2,6},{3,7},{4,0},{5,1},{6,2},{7,3},{8,12},{9,13},{10,... | collective-permute-start | bytes 1572872 | tf_op jit(solution)/shard_map/ppermute | solution.py:545
  15.5 2.8 %copy-done = bf16[1024,3072]{1,0:T(8,128)(2,1)S(1)} copy-done((bf16[1024,3072]{1,0:T(8,128)(2,1)S(1)}, bf16[1024,3072]{1,0:T(8,128)(2,1)}, u32[]{:S(2)}) %copy-start) | copy-done | bytes 6291480
  18.2 9.4 %project.4 = (bf16[384,1024]{1,0:T(8,128)(2,1)S(1)}, bf16[384,1024]{1,0:T(8,128)(2,1)S(1)}, bf16[768,2048]{1,0:T(8,128)(2,1)S(1)}) custom-call(bf16[384,1024]{1,0:T(8,128)(2,1)S(1)} %copy-done.5, s32[1,384]{1,0:T(1,128)S(1)} %reshape.15.order.refs_1_, bf16[384,1024]{1,0:T(8,128)(2,1)S(1)} %get-tuple-element.69.refs_2_, ...), custom_call_target="tpu_custom_call" | custom-call | flops 50331648 | bytes 131072 | tf_op jit(solution)/shard_map/project/pallas_call | solution.py:189
  28.6 3.8 %collective-permute-start.3 = (bf16[96,1024]{1,0:T(8,128)(2,1)S(1)}, bf16[96,1024]{1,0:T(8,128)(2,1)S(1)}, u32[]{:S(2)}, u32[]{:S(2)}) collective-permute-start(bf16[96,1024]{1,0:T(8,128)(2,1)S(1)} %get-tuple-element.101), channel_id=1, source_target_pairs={{0,1},{1,0},{2,3},{3,2},{4,5},{5,4},{6,7},{7,6},{8,9},{9,8},{10,11... | collective-permute-start | bytes 589832 | tf_op jit(solution)/shard_map/ppermute | solution.py:535
  34.1 3.1 %project.5.near = bf16[384,2048]{1,0:T(8,128)(2,1)S(1)} custom-call(bf16[192,1024]{1,0:T(8,128)(2,1)S(1)} %collective-permute-done.1.refs_0_, bf16[192,1024]{1,0:T(8,128)(2,1)S(1)} %collective-permute-done.2.refs_1_, bf16[1024,3072]{1,0:T(8,128)(2,1)S(1)} %copy-done.1, f32[1,256]{1,0:T(1,128)S(1)} %broadcast_in_dim_tile.4.refs_5_.refs_3_.refs_2_, ...), custom_call_target="tpu_custom_call" | custom-call | flops 25165824 | bytes 131072 | tf_op jit(solution)/shard_map/project/pallas_call | solution.py:189
  37.3 3.1 %project.6.across = bf16[384,2048]{1,0:T(8,128)(2,1)S(1)} custom-call(bf16[96,1024]{1,0:T(8,128)(2,1)S(1)} %collective-permute-done.3.refs_0_, bf16[96,1024]{1,0:T(8,128)(2,1)S(1)} %collective-permute-done.4.refs_1_, bf16[96,1024]{1,0:T(8,128)(2,1)S(1)} %collective-permute-done.5.refs_2_, bf16[96,1024]{1,0:T(8,128)(2,1)S(1)} %collective-permute-done.6.refs_3_, ...), custom_call_target="tpu_custom_call" | custom-call | flops 25165824 | bytes 131072 | tf_op jit(solution)/shard_map/project/pallas_call | solution.py:189
  40.4 6.4 %attend.1 = (f32[384,1024]{1,0:T(8,128)S(1)}, f32[384,1024]{1,0:T(8,128)S(1)}) custom-call(s32[3,8]{1,0:T(4,128)S(1)} %copy-done.8, s32[3]{0:T(128)S(1)} %copy-done.11, bf16[384,1024]{1,0:T(8,128)(2,1)S(1)} %get-tuple-element.54.queries, bf16[768,2048]{1,0:T(8,128)(2,1)S(1)} %get-tuple-element.55.own_mate, bf16[384,2048]{1,0:T(8,128)(2,1)S(1)} %project.5.near, ...), custom_call_target="tpu_custom_call" | custom-call | flops 500000000 | bytes 6291456 | tf_op jit(solution)/shard_map/attend/pallas_call | solution.py:300
  46.8 3.3 %collective-permute-done.8.refs_3_ = bf16[256,1024]{1,0:T(8,128)(2,1)S(1)} collective-permute-done((bf16[256,1024]{1,0:T(8,128)(2,1)}, bf16[256,1024]{1,0:T(8,128)(2,1)S(1)}, u32[]{:S(2)}, u32[]{:S(2)}) %collective-permute-start.8) | collective-permute-done | bytes 524320 | tf_op jit(solution)/shard_map/ppermute | solution.py:545
  50.1 2.4 %collective-permute-start.10 = (bf16[256,1024]{1,0:T(8,128)(2,1)S(1)}, bf16[256,1024]{1,0:T(8,128)(2,1)S(1)}, u32[]{:S(2)}, u32[]{:S(2)}) collective-permute-start(bf16[256,1024]{1,0:T(8,128)(2,1)S(1)} %collective-permute-done.7.refs_4_), channel_id=1, source_target_pairs={{0,4},{1,5},{2,6},{3,7},{4,0},{5,1},{6,2},{7,3},{8,12},{9,13},{10,... | collective-permute-start | bytes 1572872 | tf_op jit(solution)/shard_map/ppermute | solution.py:545
  54.0 3.1 %project.7.window = bf16[384,2048]{1,0:T(8,128)(2,1)S(1)} custom-call(bf16[384,1024]{1,0:T(8,128)(2,1)S(1)} %collective-permute-done.9.refs_0_, bf16[1024,3072]{1,0:T(8,128)(2,1)S(1)} %copy-done.1, f32[1,256]{1,0:T(1,128)S(1)} %broadcast_in_dim_tile.4.refs_5_.refs_3_.refs_2_, f32[1,256]{1,0:T(1,128)S(1)} %broadcast_in_dim_tile.5.refs_6_.refs_4_.refs_3_), custom_call_target="tpu_custom_call" | custom-call | flops 25165824 | bytes 131072 | tf_op jit(solution)/shard_map/project/pallas_call | solution.py:189
  57.1 2.0 %finish.1.attention = bf16[384,1024]{1,0:T(8,128)(2,1)S(1)} custom-call(s32[3,8]{1,0:T(4,128)S(1)} %copy-done.8, s32[3]{0:T(128)S(1)} %copy-done.11, bf16[384,1024]{1,0:T(8,128)(2,1)S(1)} %get-tuple-element.54.queries, bf16[384,2048]{1,0:T(8,128)(2,1)S(1)} %project.7.window, f32[384,1024]{1,0:T(8,128)S(1)} %get-tuple-element.71.mixed, ...), custom_call_target="tpu_custom_call" | custom-call | flops 37748736 | bytes 131072 | tf_op jit(solution)/shard_map/finish/pallas_call | solution.py:361
  59.1 1.9 %attention_output.1 = (bf16[384,1024]{1,0:T(8,128)(2,1)}, bf16[192,1024]{1,0:T(8,128)(2,1)S(1)}, bf16[192,1024]{1,0:T(8,128)(2,1)S(1)}) custom-call(bf16[384,1024]{1,0:T(8,128)(2,1)S(1)} %finish.1.attention, bf16[384,1024]{1,0:T(8,128)(2,1)S(1)} %get-tuple-element.73.ordered, bf16[1024,1024]{1,0:T(8,128)(2,1)S(1)} %copy-done.6, f32[1,1024]{1,0:T(1,128)S(1)} %bitcast.3), custom_call_target="tpu_custom_call" | custom-call | flops 12582912 | bytes 32768 | tf_op jit(solution)/shard_map/attention_output/pallas_call | solution.py:393
  63.0 2.3 %collective-permute-done.10.refs_1_.refs_2_ = bf16[256,1024]{1,0:T(8,128)(2,1)S(1)} collective-permute-done((bf16[256,1024]{1,0:T(8,128)(2,1)S(1)}, bf16[256,1024]{1,0:T(8,128)(2,1)S(1)}, u32[]{:S(2)}, u32[]{:S(2)}) %collective-permute-start.10) | collective-permute-done | bytes 524320 | tf_op jit(solution)/shard_map/ppermute | solution.py:545
  66.8 7.4 %collective-permute-done.14.refs_6_ = bf16[256,1024]{1,0:T(8,128)(2,1)S(1)} collective-permute-done((bf16[256,1024]{1,0:T(8,128)(2,1)S(1)}, bf16[256,1024]{1,0:T(8,128)(2,1)S(1)}, u32[]{:S(2)}, u32[]{:S(2)}) %collective-permute-start.14) | collective-permute-done | bytes 524320 | tf_op jit(solution)/shard_map/ppermute | solution.py:545
  74.3 4.8 %collective-permute-done.17.refs_1_.refs_0_ = bf16[192,1024]{1,0:T(8,128)(2,1)S(1)} collective-permute-done((bf16[192,1024]{1,0:T(8,128)(2,1)S(1)}, bf16[192,1024]{1,0:T(8,128)(2,1)S(1)}, u32[]{:S(2)}, u32[]{:S(2)}) %collective-permute-start.17) | collective-permute-done | bytes 393248 | tf_op jit(solution)/shard_map/ppermute | solution.py:535
  80.8 2.0 %feed_pieces.7 = (bf16[192,1024]{1,0:T(8,128)(2,1)S(1)}, bf16[192,1024]{1,0:T(8,128)(2,1)S(1)}) custom-call(bf16[192,1024]{1,0:T(8,128)(2,1)S(1)} %collective-permute-done.16.refs_0_, bf16[192,1024]{1,0:T(8,128)(2,1)S(1)} %collective-permute-done.18.refs_1_, bf16[256,1024]{1,0:T(8,128)(2,1)S(1)} %copy-done.2, ...), custom_call_target="tpu_custom_call" | custom-call | flops 18874368 | bytes 49152 | tf_op jit(solution)/shard_map/feed_pieces/pallas_call | solution.py:439
  84.1 2.0 %feed_pieces.9 = (f32[192,1024]{1,0:T(8,128)S(1)}, f32[192,1024]{1,0:T(8,128)S(1)}) custom-call(bf16[192,1024]{1,0:T(8,128)(2,1)S(1)} %collective-permute-done.13.refs_0_, bf16[192,1024]{1,0:T(8,128)(2,1)S(1)} %collective-permute-done.17.refs_1_.refs_0_, bf16[256,1024]{1,0:T(8,128)(2,1)S(1)} %copy-done.2, ...), custom_call_target="tpu_custom_call" | custom-call | flops 18874368 | bytes 49152 | tf_op jit(solution)/shard_map/feed_pieces/pallas_call | solution.py:439
  90.1 2.0 %feed_pieces.8 = (bf16[96,1024]{1,0:T(8,128)(2,1)S(1)}, bf16[96,1024]{1,0:T(8,128)(2,1)S(1)}, bf16[96,1024]{1,0:T(8,128)(2,1)S(1)}, bf16[96,1024]{1,0:T(8,128)(2,1)S(1)}) custom-call(bf16[192,1024]{1,0:T(8,128)(2,1)S(1)} %collective-permute-done.20.refs_0_, bf16[192,1024]{1,0:T(8,128)(2,1)S(1)} %collective-permute-done.21.refs_1_, ...), custom_call_target="tpu_custom_call" | custom-call | flops 18874368 | bytes 49152 | tf_op jit(solution)/shard_map/feed_pieces/pallas_call | solution.py:439
  92.8 6.2 %collective-permute-done.27.refs_0_ = bf16[192,1024]{1,0:T(8,128)(2,1)S(1)} collective-permute-done((bf16[192,1024]{1,0:T(8,128)(2,1)S(1)}, bf16[192,1024]{1,0:T(8,128)(2,1)S(1)}, u32[]{:S(2)}, u32[]{:S(2)}) %collective-permute-start.27) | collective-permute-done | bytes 393248 | tf_op jit(solution)/shard_map/ppermute | solution.py:535
  99.0 2.0 %feed_pieces.11.refs_10_ = f32[384,1024]{1,0:T(8,128)S(1)} custom-call(bf16[192,1024]{1,0:T(8,128)(2,1)S(1)} %get-tuple-element.77.refs_0_, bf16[192,1024]{1,0:T(8,128)(2,1)S(1)} %get-tuple-element.78.refs_1_, bf16[256,1024]{1,0:T(8,128)(2,1)S(1)} %copy-done.2, bf16[256,1024]{1,0:T(8,128)(2,1)S(1)} %collective-permute-done.8.refs_3_, ...), custom_call_target="tpu_custom_call" | custom-call | flops 18874368 | bytes 49152 | tf_op jit(solution)/shard_map/feed_pieces/pallas_call | solution.py:439
  102.3 4.6 %collective-permute-done.29.refs_1_ = bf16[192,1024]{1,0:T(8,128)(2,1)S(1)} collective-permute-done((bf16[192,1024]{1,0:T(8,128)(2,1)S(1)}, bf16[192,1024]{1,0:T(8,128)(2,1)S(1)}, u32[]{:S(2)}, u32[]{:S(2)}) %collective-permute-start.29) | collective-permute-done | bytes 393248 | tf_op jit(solution)/shard_map/ppermute | solution.py:535
  (90 shorter events, 21.4 us)
Async XLA Ops:
  4.7 10.7 %collective-permute-start = (bf16[384,1024]{1,0:T(8,128)(2,1)S(1)}, bf16[384,1024]{1,0:T(8,128)(2,1)}, u32[]{:S(2)}, u32[]{:S(2)}) collective-permute-start(bf16[384,1024]{1,0:T(8,128)(2,1)S(1)} %get-tuple-element.69.refs_2_), channel_id=1, source_target_pairs={{0,1},{1,0},{2,3},{3,2},{4,5},{5,4},{6,7},{7,6},{8,9},{9,8},{10,11... | collective-permute-start | bytes 2359304 | tf_op jit(solution)/shard_map/ppermute | solution.py:535
  5.2 22.5 %collective-permute-start.1 = (bf16[192,1024]{1,0:T(8,128)(2,1)}, bf16[192,1024]{1,0:T(8,128)(2,1)S(1)}, u32[]{:S(2)}, u32[]{:S(2)}) collective-permute-start(bf16[192,1024]{1,0:T(8,128)(2,1)} %get-tuple-element.52), channel_id=1, source_target_pairs={{0,15},{1,2},{2,1},{3,4},{4,3},{5,6},{6,5},{7,8},{8,7},{9,10},{10,... | collective-permute-start | bytes 1179656 | tf_op jit(solution)/shard_map/ppermute | solution.py:535
  10.9 16.8 %collective-permute-start.2 = (bf16[192,1024]{1,0:T(8,128)(2,1)}, bf16[192,1024]{1,0:T(8,128)(2,1)S(1)}, u32[]{:S(2)}, u32[]{:S(2)}) collective-permute-start(bf16[192,1024]{1,0:T(8,128)(2,1)} %get-tuple-element.53), channel_id=1, source_target_pairs={{0,15},{1,2},{2,1},{3,4},{4,3},{5,6},{6,5},{7,8},{8,7},{9,10},{10,... | collective-permute-start | bytes 1179656 | tf_op jit(solution)/shard_map/ppermute | solution.py:535
  13.1 33.7 %collective-permute-start.7 = (bf16[256,1024]{1,0:T(8,128)(2,1)}, bf16[256,1024]{1,0:T(8,128)(2,1)S(1)}, u32[]{:S(2)}, u32[]{:S(2)}) collective-permute-start(bf16[256,1024]{1,0:T(8,128)(2,1)} %get-tuple-element.65), channel_id=1, source_target_pairs={{0,8},{1,9},{2,10},{3,11},{4,12},{5,13},{6,14},{7,15},{8,0},{9,1},... | collective-permute-start | bytes 1572872 | tf_op jit(solution)/shard_map/ppermute | solution.py:545
  13.7 36.4 %collective-permute-start.8 = (bf16[256,1024]{1,0:T(8,128)(2,1)}, bf16[256,1024]{1,0:T(8,128)(2,1)S(1)}, u32[]{:S(2)}, u32[]{:S(2)}) collective-permute-start(bf16[256,1024]{1,0:T(8,128)(2,1)} %get-tuple-element.65), channel_id=1, source_target_pairs={{0,4},{1,5},{2,6},{3,7},{4,0},{5,1},{6,2},{7,3},{8,12},{9,13},{10,... | collective-permute-start | bytes 1572872 | tf_op jit(solution)/shard_map/ppermute | solution.py:545
  27.7 26.3 %collective-permute-start.9 = (bf16[384,1024]{1,0:T(8,128)(2,1)S(1)}, bf16[384,1024]{1,0:T(8,128)(2,1)S(1)}, u32[]{:S(2)}, u32[]{:S(2)}) collective-permute-start(bf16[384,1024]{1,0:T(8,128)(2,1)S(1)} %get-tuple-element.69.refs_2_), channel_id=1, source_target_pairs={{0,2},{1,15},{2,4},{3,1},{4,6},{5,3},{6,8},{7,5},{8,10},{9,7},{10,... | collective-permute-start | bytes 2359304 | tf_op jit(solution)/shard_map/ppermute | solution.py:535
  28.6 4.9 %collective-permute-start.3 = (bf16[96,1024]{1,0:T(8,128)(2,1)S(1)}, bf16[96,1024]{1,0:T(8,128)(2,1)S(1)}, u32[]{:S(2)}, u32[]{:S(2)}) collective-permute-start(bf16[96,1024]{1,0:T(8,128)(2,1)S(1)} %get-tuple-element.101), channel_id=1, source_target_pairs={{0,1},{1,0},{2,3},{3,2},{4,5},{5,4},{6,7},{7,6},{8,9},{9,8},{10,11... | collective-permute-start | bytes 589832 | tf_op jit(solution)/shard_map/ppermute | solution.py:535
  33.5 3.8 %collective-permute-start.5 = (bf16[96,1024]{1,0:T(8,128)(2,1)S(1)}, bf16[96,1024]{1,0:T(8,128)(2,1)S(1)}, u32[]{:S(2)}, u32[]{:S(2)}) collective-permute-start(bf16[96,1024]{1,0:T(8,128)(2,1)S(1)} %get-tuple-element.99), channel_id=1, source_target_pairs={{0,1},{1,0},{2,3},{3,2},{4,5},{5,4},{6,7},{7,6},{8,9},{9,8},{10,11... | collective-permute-start | bytes 589832 | tf_op jit(solution)/shard_map/ppermute | solution.py:535
  50.1 15.2 %collective-permute-start.10 = (bf16[256,1024]{1,0:T(8,128)(2,1)S(1)}, bf16[256,1024]{1,0:T(8,128)(2,1)S(1)}, u32[]{:S(2)}, u32[]{:S(2)}) collective-permute-start(bf16[256,1024]{1,0:T(8,128)(2,1)S(1)} %collective-permute-done.7.refs_4_), channel_id=1, source_target_pairs={{0,4},{1,5},{2,6},{3,7},{4,0},{5,1},{6,2},{7,3},{8,12},{9,13},{10,... | collective-permute-start | bytes 1572872 | tf_op jit(solution)/shard_map/ppermute | solution.py:545
  52.5 21.7 %collective-permute-start.14 = (bf16[256,1024]{1,0:T(8,128)(2,1)S(1)}, bf16[256,1024]{1,0:T(8,128)(2,1)S(1)}, u32[]{:S(2)}, u32[]{:S(2)}) collective-permute-start(bf16[256,1024]{1,0:T(8,128)(2,1)S(1)} %copy-done.14), channel_id=1, source_target_pairs={{0,4},{1,5},{2,6},{3,7},{4,0},{5,1},{6,2},{7,3},{8,12},{9,13},{10,... | collective-permute-start | bytes 1572872 | tf_op jit(solution)/shard_map/ppermute | solution.py:545
  52.5 21.7 %collective-permute-start.15 = (bf16[256,1024]{1,0:T(8,128)(2,1)S(1)}, bf16[256,1024]{1,0:T(8,128)(2,1)S(1)}, u32[]{:S(2)}, u32[]{:S(2)}) collective-permute-start(bf16[256,1024]{1,0:T(8,128)(2,1)S(1)} %collective-permute-done.7.refs_4_), channel_id=1, source_target_pairs={{0,16},{16,0},{1,17},{17,1},{2,18},{18,2},{3,19},{19,3},{4,20},{20... | collective-permute-start | bytes 1572872 | tf_op jit(solution)/shard_map/ppermute | solution.py:551
  61.0 13.2 %collective-permute-start.13 = (bf16[192,1024]{1,0:T(8,128)(2,1)S(1)}, bf16[192,1024]{1,0:T(8,128)(2,1)S(1)}, u32[]{:S(2)}, u32[]{:S(2)}) collective-permute-start(bf16[192,1024]{1,0:T(8,128)(2,1)S(1)} %get-tuple-element.77.refs_0_), channel_id=1, source_target_pairs={{0,2},{1,3},{2,0},{3,1},{4,6},{5,7},{6,4},{7,5},{8,10},{9,11},{10,... | collective-permute-start | bytes 1179656 | tf_op jit(solution)/shard_map/ppermute | solution.py:535
  62.5 16.6 %collective-permute-start.17 = (bf16[192,1024]{1,0:T(8,128)(2,1)S(1)}, bf16[192,1024]{1,0:T(8,128)(2,1)S(1)}, u32[]{:S(2)}, u32[]{:S(2)}) collective-permute-start(bf16[192,1024]{1,0:T(8,128)(2,1)S(1)} %get-tuple-element.78.refs_1_), channel_id=1, source_target_pairs={{0,2},{1,3},{2,0},{3,1},{4,6},{5,7},{6,4},{7,5},{8,10},{9,11},{10,... | collective-permute-start | bytes 1179656 | tf_op jit(solution)/shard_map/ppermute | solution.py:535
  65.3 17.5 %collective-permute-start.12 = (bf16[256,1024]{1,0:T(8,128)(2,1)S(1)}, bf16[256,1024]{1,0:T(8,128)(2,1)S(1)}, u32[]{:S(2)}, u32[]{:S(2)}) collective-permute-start(bf16[256,1024]{1,0:T(8,128)(2,1)S(1)} %collective-permute-done.10.refs_1_.refs_2_), channel_id=1, source_target_pairs={{0,16},{16,0},{1,17},{17,1},{2,18},{18,2},{3,19},{19,3},{4,20},{20... | collective-permute-start | bytes 1572872 | tf_op jit(solution)/shard_map/ppermute | solution.py:551
  74.2 5.3 %collective-permute-start.16 = (bf16[192,1024]{1,0:T(8,128)(2,1)S(1)}, bf16[192,1024]{1,0:T(8,128)(2,1)S(1)}, u32[]{:S(2)}, u32[]{:S(2)}) collective-permute-start(bf16[192,1024]{1,0:T(8,128)(2,1)S(1)} %collective-permute-done.13.refs_0_), channel_id=1, source_target_pairs={{0,1},{1,0},{2,3},{3,2},{4,5},{5,4},{6,7},{7,6},{8,9},{9,8},{10,11... | collective-permute-start | bytes 1179656 | tf_op jit(solution)/shard_map/ppermute | solution.py:535
  79.1 4.8 %collective-permute-start.11 = (bf16[256,1024]{1,0:T(8,128)(2,1)S(1)}, bf16[256,1024]{1,0:T(8,128)(2,1)S(1)}, u32[]{:S(2)}, u32[]{:S(2)}) collective-permute-start(bf16[256,1024]{1,0:T(8,128)(2,1)S(1)} %collective-permute-done.10.refs_1_.refs_2_), channel_id=1, source_target_pairs={{0,1},{1,0},{2,3},{3,2},{4,5},{5,4},{6,7},{7,6},{8,9},{9,8},{10,11... | collective-permute-start | bytes 1572872 | tf_op jit(solution)/shard_map/ppermute | solution.py:535
  83.4 4.7 %collective-permute-start.28 = (bf16[192,1024]{1,0:T(8,128)(2,1)S(1)}, bf16[192,1024]{1,0:T(8,128)(2,1)S(1)}, u32[]{:S(2)}, u32[]{:S(2)}) collective-permute-start(bf16[192,1024]{1,0:T(8,128)(2,1)S(1)} %get-tuple-element.96), channel_id=1, source_target_pairs={{0,1},{1,0},{2,3},{3,2},{4,5},{5,4},{6,7},{7,6},{8,9},{9,8},{10,11... | collective-permute-start | bytes 1179656 | tf_op jit(solution)/shard_map/ppermute | solution.py:535
  83.5 6.5 %collective-permute-start.20 = (bf16[192,1024]{1,0:T(8,128)(2,1)S(1)}, bf16[192,1024]{1,0:T(8,128)(2,1)S(1)}, u32[]{:S(2)}, u32[]{:S(2)}) collective-permute-start(bf16[192,1024]{1,0:T(8,128)(2,1)S(1)} %get-tuple-element.77.refs_0_), channel_id=1, source_target_pairs={{0,1},{1,0},{2,3},{3,2},{4,5},{5,4},{6,7},{7,6},{8,9},{9,8},{10,11... | collective-permute-start | bytes 1179656 | tf_op jit(solution)/shard_map/ppermute | solution.py:535
  83.9 6.2 %collective-permute-start.21 = (bf16[192,1024]{1,0:T(8,128)(2,1)S(1)}, bf16[192,1024]{1,0:T(8,128)(2,1)S(1)}, u32[]{:S(2)}, u32[]{:S(2)}) collective-permute-start(bf16[192,1024]{1,0:T(8,128)(2,1)S(1)} %get-tuple-element.78.refs_1_), channel_id=1, source_target_pairs={{0,1},{1,0},{2,3},{3,2},{4,5},{5,4},{6,7},{7,6},{8,9},{9,8},{10,11... | collective-permute-start | bytes 1179656 | tf_op jit(solution)/shard_map/ppermute | solution.py:535
  87.0 12.0 %collective-permute-start.27 = (bf16[192,1024]{1,0:T(8,128)(2,1)S(1)}, bf16[192,1024]{1,0:T(8,128)(2,1)S(1)}, u32[]{:S(2)}, u32[]{:S(2)}) collective-permute-start(bf16[192,1024]{1,0:T(8,128)(2,1)S(1)} %feed_pieces.10), channel_id=1, source_target_pairs={{0,2},{1,3},{2,0},{3,1},{4,6},{5,7},{6,4},{7,5},{8,10},{9,11},{10,... | collective-permute-start | bytes 1179656 | tf_op jit(solution)/shard_map/ppermute | solution.py:535
  89.0 17.9 %collective-permute-start.29 = (bf16[192,1024]{1,0:T(8,128)(2,1)S(1)}, bf16[192,1024]{1,0:T(8,128)(2,1)S(1)}, u32[]{:S(2)}, u32[]{:S(2)}) collective-permute-start(bf16[192,1024]{1,0:T(8,128)(2,1)S(1)} %feed_pieces.13), channel_id=1, source_target_pairs={{0,2},{1,3},{2,0},{3,1},{4,6},{5,7},{6,4},{7,5},{8,10},{9,11},{10,... | collective-permute-start | bytes 1179656 | tf_op jit(solution)/shard_map/ppermute | solution.py:535
  92.1 8.9 %collective-permute-start.22 = (bf16[96,1024]{1,0:T(8,128)(2,1)S(1)}, bf16[96,1024]{1,0:T(8,128)(2,1)S(1)}, u32[]{:S(2)}, u32[]{:S(2)}) collective-permute-start(bf16[96,1024]{1,0:T(8,128)(2,1)S(1)} %get-tuple-element.88), channel_id=1, source_target_pairs={{0,1},{1,0},{2,3},{3,2},{4,5},{5,4},{6,7},{7,6},{8,9},{9,8},{10,11... | collective-permute-start | bytes 589832 | tf_op jit(solution)/shard_map/ppermute | solution.py:535
  92.2 8.9 %collective-permute-start.23 = (bf16[96,1024]{1,0:T(8,128)(2,1)S(1)}, bf16[96,1024]{1,0:T(8,128)(2,1)S(1)}, u32[]{:S(2)}, u32[]{:S(2)}) collective-permute-start(bf16[96,1024]{1,0:T(8,128)(2,1)S(1)} %get-tuple-element.89), channel_id=1, source_target_pairs={{0,1},{1,0},{2,3},{3,2},{4,5},{5,4},{6,7},{7,6},{8,9},{9,8},{10,11... | collective-permute-start | bytes 589832 | tf_op jit(solution)/shard_map/ppermute | solution.py:535
  92.7 8.4 %collective-permute-start.24 = (bf16[96,1024]{1,0:T(8,128)(2,1)S(1)}, bf16[96,1024]{1,0:T(8,128)(2,1)S(1)}, u32[]{:S(2)}, u32[]{:S(2)}) collective-permute-start(bf16[96,1024]{1,0:T(8,128)(2,1)S(1)} %get-tuple-element.90), channel_id=1, source_target_pairs={{0,1},{1,0},{2,3},{3,2},{4,5},{5,4},{6,7},{7,6},{8,9},{9,8},{10,11... | collective-permute-start | bytes 589832 | tf_op jit(solution)/shard_map/ppermute | solution.py:535
  (21 other events, 148.6 us)

commit v6 on v5

--- a/solution.py
+++ b/solution.py
@@ -601,17 +601,23 @@
             (pair_rows, other_pair, True),
             (third, other_third, True),
         ]
-        guest_mate_parts = feed_pieces(
-            "parts", [mate_of(guest) for guest in guests], pieces, [], jnp.bfloat16, parts
-        )
-        other_fourth, *guest_mate_parts = lax.optimization_barrier(
-            (other_fourth, *guest_mate_parts)
-        )
+        guest_mate_parts = []
+        guest_parts = []
+        for index in range(parts):
+            guest_mate_parts += feed_pieces(
+                "parts", [mate_of(part) for part in jnp.split(guests[index], 2)], pieces, [], jnp.bfloat16
+            )
+            guest_parts += feed_pieces("parts", [guests[index]], pieces, [], jnp.float32)
+            if index == 0:
+                guests[1], guest_mate_parts[0], guest_parts[0], other_fourth = (
+                    lax.optimization_barrier(
+                        (guests[1], guest_mate_parts[0], guest_parts[0], other_fourth)
+                    )
+                )
         last = [
             (fourth, other_fourth, True),
             (mate_of(fourth), mate_of(other_fourth), True),
         ]
-        guest_parts = feed_pieces("parts", guests, pieces, [], jnp.float32, parts)
         returned = []
         for guest, part, base in zip(guests, guest_parts, guest_mate_parts):
             (guest_part,) = feed_pieces(

time: 109 us -> 107 us (0.982)
  waiting for transfers between devices: 30.9 us -> 22.9 us
  Pallas kernels: 44.8 us -> 49.7 us
  starting transfers between devices: 25.7 us -> 26.8 us
    ppermute x24 -> x26, waiting for transfers between devices: 17.9 us -> 13.6 us  [moved(): lax.ppermute(value, 'seq', [(i, where(i) % cycle) for i in range(cycle)])]
    ppermute x4, waiting for transfers between devices: 13 us -> 9.36 us  [along(): return lax.ppermute(value, 'seq', pairs)]
    pallas_call x1, Pallas kernels: 6.39 us -> 8.9 us  [attend(): pl.pallas_call(functools.partial(attend_kernel, axis, cycle), out_shape=(...]
    pallas_call x7 -> x9, Pallas kernels: 11.1 us -> 12.8 us  [feed_pieces(): pl.pallas_call(functools.partial(pieces_kernel, axis, tuple((piece[2] for...]
    ppermute x24 -> x26, starting transfers between devices: 18.2 us -> 19.3 us  [moved(): lax.ppermute(value, 'seq', [(i, where(i) % cycle) for i in range(cycle)])]
  transfers between devices with their start and end apart: 30 -> 32, of which waited for: 8 -> 9; matrix products, arithmetic and copies ran while one was open for 0% -> 0% of each run, Pallas kernels for 39% -> 44%
where the time goes in v6:
time: 107 us; the launch traced here: 106 us
  Pallas kernels  49.7 us (46%)
  starting transfers between devices  26.8 us (25%)
  waiting for transfers between devices  22.9 us (21%)
  local copies, waits for them, and re-layouts  5.64 us (5%)
    ppermute x26, starting transfers between devices, moved(): lax.ppermute(value, 'seq', [(i, where(i) % cycle) for i in range(cycle)])  19.3 us
    pallas_call x4, Pallas kernels, project(): pl.pallas_call(functools.partial(project_kernel, 'seq', head_dim, 2.0 / m...  18.7 us
    ppermute x26, waiting for transfers between devices, moved(): lax.ppermute(value, 'seq', [(i, where(i) % cycle) for i in range(cycle)])  13.6 us
    pallas_call x9, Pallas kernels, feed_pieces(): pl.pallas_call(functools.partial(pieces_kernel, axis, tuple((piece[2] for...  12.8 us
    ppermute x4, waiting for transfers between devices, along(): return lax.ppermute(value, 'seq', pairs)  9.36 us
    pallas_call x1, Pallas kernels, attend(): pl.pallas_call(functools.partial(attend_kernel, axis, cycle), out_shape=(...  8.9 us
    unnamed x30, local copies, waits for them, and re-layouts  4.67 us
    ppermute x4, starting transfers between devices, along(): return lax.ppermute(value, 'seq', pairs)  4.58 us
  transfers between devices with their start and end apart: 32, of which 9 were waited for; matrix products, arithmetic and copies ran while one was open for 0% of the time, Pallas kernels for 44%

profile of v6, /device:TPU:0, one launch (start us, length us, event | category | flops | bytes accessed | tf_op | source)
XLA Modules:
  0.0 106.2 jit_solution(3550684778292500692)
XLA Ops:
  3.2 1.6 %norm.1 = (bf16[384,1024]{1,0:T(8,128)(2,1)S(1)}, bf16[192,1024]{1,0:T(8,128)(2,1)}, bf16[192,1024]{1,0:T(8,128)(2,1)}) custom-call(bf16[384,1024]{1,0:T(8,128)(2,1)S(1)} %copy-done.4, s32[1,384]{1,0:T(1,128)S(1)} %reshape.15.order.refs_1_, f32[1,1024]{1,0:T(1,128)S(1)} %bitcast.2), custom_call_target="tpu_custom_call" | custom-call | flops 4718592 | bytes 36864 | tf_op jit(solution)/shard_map/norm/pallas_call | solution.py:62
  5.2 5.7 %collective-permute-start.1 = (bf16[192,1024]{1,0:T(8,128)(2,1)}, bf16[192,1024]{1,0:T(8,128)(2,1)S(1)}, u32[]{:S(2)}, u32[]{:S(2)}) collective-permute-start(bf16[192,1024]{1,0:T(8,128)(2,1)} %get-tuple-element.49), channel_id=1, source_target_pairs={{0,15},{1,2},{2,1},{3,4},{4,3},{5,6},{6,5},{7,8},{8,7},{9,10},{10,... | collective-permute-start | bytes 1179656 | tf_op jit(solution)/shard_map/ppermute | solution.py:535
  10.9 2.2 %choose.1 = (bf16[256,1024]{1,0:T(8,128)(2,1)}, bf16[256,1024]{1,0:T(8,128)(2,1)}) custom-call(bf16[256,1024]{1,0:T(8,128)(2,1)} %refs_1_.5, bf16[256,1024]{1,0:T(8,128)(2,1)} %refs_4_.7), custom_call_target="tpu_custom_call" | custom-call | bytes 24576 | tf_op jit(solution)/shard_map/choose/pallas_call | solution.py:97
  13.7 1.6 %collective-permute-start.8 = (bf16[256,1024]{1,0:T(8,128)(2,1)}, bf16[256,1024]{1,0:T(8,128)(2,1)S(1)}, u32[]{:S(2)}, u32[]{:S(2)}) collective-permute-start(bf16[256,1024]{1,0:T(8,128)(2,1)} %get-tuple-element.62), channel_id=1, source_target_pairs={{0,4},{1,5},{2,6},{3,7},{4,0},{5,1},{6,2},{7,3},{8,12},{9,13},{10,... | collective-permute-start | bytes 1572872 | tf_op jit(solution)/shard_map/ppermute | solution.py:545
  15.4 2.8 %copy-done = bf16[1024,3072]{1,0:T(8,128)(2,1)S(1)} copy-done((bf16[1024,3072]{1,0:T(8,128)(2,1)S(1)}, bf16[1024,3072]{1,0:T(8,128)(2,1)}, u32[]{:S(2)}) %copy-start) | copy-done | bytes 6291480
  18.2 9.4 %project.4 = (bf16[384,1024]{1,0:T(8,128)(2,1)S(1)}, bf16[384,1024]{1,0:T(8,128)(2,1)S(1)}, bf16[768,2048]{1,0:T(8,128)(2,1)S(1)}) custom-call(bf16[384,1024]{1,0:T(8,128)(2,1)S(1)} %copy-done.5, s32[1,384]{1,0:T(1,128)S(1)} %reshape.15.order.refs_1_, bf16[384,1024]{1,0:T(8,128)(2,1)S(1)} %get-tuple-element.66.refs_2_, ...), custom_call_target="tpu_custom_call" | custom-call | flops 50331648 | bytes 131072 | tf_op jit(solution)/shard_map/project/pallas_call | solution.py:189
  28.6 3.8 %collective-permute-start.3 = (bf16[96,1024]{1,0:T(8,128)(2,1)S(1)}, bf16[96,1024]{1,0:T(8,128)(2,1)S(1)}, u32[]{:S(2)}, u32[]{:S(2)}) collective-permute-start(bf16[96,1024]{1,0:T(8,128)(2,1)S(1)} %get-tuple-element.99), channel_id=1, source_target_pairs={{0,1},{1,0},{2,3},{3,2},{4,5},{5,4},{6,7},{7,6},{8,9},{9,8},{10,11... | collective-permute-start | bytes 589832 | tf_op jit(solution)/shard_map/ppermute | solution.py:535
  34.1 3.1 %project.5.near = bf16[384,2048]{1,0:T(8,128)(2,1)S(1)} custom-call(bf16[192,1024]{1,0:T(8,128)(2,1)S(1)} %collective-permute-done.1.refs_0_, bf16[192,1024]{1,0:T(8,128)(2,1)S(1)} %collective-permute-done.2.refs_1_, bf16[1024,3072]{1,0:T(8,128)(2,1)S(1)} %copy-done.1, f32[1,256]{1,0:T(1,128)S(1)} %broadcast_in_dim_tile.4.refs_5_.refs_3_.refs_2_, ...), custom_call_target="tpu_custom_call" | custom-call | flops 25165824 | bytes 131072 | tf_op jit(solution)/shard_map/project/pallas_call | solution.py:189
  37.3 3.1 %project.6.across = bf16[384,2048]{1,0:T(8,128)(2,1)S(1)} custom-call(bf16[96,1024]{1,0:T(8,128)(2,1)S(1)} %collective-permute-done.3.refs_0_, bf16[96,1024]{1,0:T(8,128)(2,1)S(1)} %collective-permute-done.4.refs_1_, bf16[96,1024]{1,0:T(8,128)(2,1)S(1)} %collective-permute-done.5.refs_2_, bf16[96,1024]{1,0:T(8,128)(2,1)S(1)} %collective-permute-done.6.refs_3_, ...), custom_call_target="tpu_custom_call" | custom-call | flops 25165824 | bytes 131072 | tf_op jit(solution)/shard_map/project/pallas_call | solution.py:189
  40.4 8.9 %attend.1 = (f32[384,1024]{1,0:T(8,128)S(1)}, f32[384,1024]{1,0:T(8,128)S(1)}) custom-call(s32[3,8]{1,0:T(4,128)S(1)} %copy-done.8, s32[3]{0:T(128)S(1)} %copy-done.11, bf16[384,1024]{1,0:T(8,128)(2,1)S(1)} %get-tuple-element.51.queries, bf16[768,2048]{1,0:T(8,128)(2,1)S(1)} %get-tuple-element.52.own_mate, bf16[384,2048]{1,0:T(8,128)(2,1)S(1)} %project.5.near, ...), custom_call_target="tpu_custom_call" | custom-call | flops 500000000 | bytes 6291456 | tf_op jit(solution)/shard_map/attend/pallas_call | solution.py:300
  50.1 2.4 %collective-permute-start.10 = (bf16[256,1024]{1,0:T(8,128)(2,1)S(1)}, bf16[256,1024]{1,0:T(8,128)(2,1)S(1)}, u32[]{:S(2)}, u32[]{:S(2)}) collective-permute-start(bf16[256,1024]{1,0:T(8,128)(2,1)S(1)} %collective-permute-done.7.refs_4_.refs_3_), channel_id=1, source_target_pairs={{0,4},{1,5},{2,6},{3,7},{4,0},{5,1},{6,2},{7,3},{8,12},{9,13},{10,... | collective-permute-start | bytes 1572872 | tf_op jit(solution)/shard_map/ppermute | solution.py:545
  52.5 1.5 %collective-permute-start.15 = (bf16[256,1024]{1,0:T(8,128)(2,1)S(1)}, bf16[256,1024]{1,0:T(8,128)(2,1)S(1)}, u32[]{:S(2)}, u32[]{:S(2)}) collective-permute-start(bf16[256,1024]{1,0:T(8,128)(2,1)S(1)} %collective-permute-done.7.refs_4_.refs_3_), channel_id=1, source_target_pairs={{0,16},{16,0},{1,17},{17,1},{2,18},{18,2},{3,19},{19,3},{4,20},{20... | collective-permute-start | bytes 1572872 | tf_op jit(solution)/shard_map/ppermute | solution.py:551
  54.0 3.1 %project.7.window = bf16[384,2048]{1,0:T(8,128)(2,1)S(1)} custom-call(bf16[384,1024]{1,0:T(8,128)(2,1)S(1)} %collective-permute-done.9.refs_0_, bf16[1024,3072]{1,0:T(8,128)(2,1)S(1)} %copy-done.1, f32[1,256]{1,0:T(1,128)S(1)} %broadcast_in_dim_tile.4.refs_5_.refs_3_.refs_2_, f32[1,256]{1,0:T(1,128)S(1)} %broadcast_in_dim_tile.5.refs_6_.refs_4_.refs_3_), custom_call_target="tpu_custom_call" | custom-call | flops 25165824 | bytes 131072 | tf_op jit(solution)/shard_map/project/pallas_call | solution.py:189
  57.1 2.7 %finish.1.attention = bf16[384,1024]{1,0:T(8,128)(2,1)S(1)} custom-call(s32[3,8]{1,0:T(4,128)S(1)} %copy-done.8, s32[3]{0:T(128)S(1)} %copy-done.11, bf16[384,1024]{1,0:T(8,128)(2,1)S(1)} %get-tuple-element.51.queries, bf16[384,2048]{1,0:T(8,128)(2,1)S(1)} %project.7.window, f32[384,1024]{1,0:T(8,128)S(1)} %get-tuple-element.68.mixed, ...), custom_call_target="tpu_custom_call" | custom-call | flops 37748736 | bytes 131072 | tf_op jit(solution)/shard_map/finish/pallas_call | solution.py:361
  59.8 1.9 %attention_output.1 = (bf16[384,1024]{1,0:T(8,128)(2,1)}, bf16[192,1024]{1,0:T(8,128)(2,1)S(1)}, bf16[192,1024]{1,0:T(8,128)(2,1)S(1)}) custom-call(bf16[384,1024]{1,0:T(8,128)(2,1)S(1)} %finish.1.attention, bf16[384,1024]{1,0:T(8,128)(2,1)S(1)} %get-tuple-element.70.ordered, bf16[1024,1024]{1,0:T(8,128)(2,1)S(1)} %copy-done.6, f32[1,1024]{1,0:T(1,128)S(1)} %bitcast.3), custom_call_target="tpu_custom_call" | custom-call | flops 12582912 | bytes 32768 | tf_op jit(solution)/shard_map/attention_output/pallas_call | solution.py:393
  62.6 2.7 %collective-permute-done.10.refs_1_.refs_2_ = bf16[256,1024]{1,0:T(8,128)(2,1)S(1)} collective-permute-done((bf16[256,1024]{1,0:T(8,128)(2,1)S(1)}, bf16[256,1024]{1,0:T(8,128)(2,1)S(1)}, u32[]{:S(2)}, u32[]{:S(2)}) %collective-permute-start.10) | collective-permute-done | bytes 524320 | tf_op jit(solution)/shard_map/ppermute | solution.py:545
  65.3 1.5 %collective-permute-start.18 = (bf16[256,1024]{1,0:T(8,128)(2,1)S(1)}, bf16[256,1024]{1,0:T(8,128)(2,1)S(1)}, u32[]{:S(2)}, u32[]{:S(2)}) collective-permute-start(bf16[256,1024]{1,0:T(8,128)(2,1)S(1)} %collective-permute-done.10.refs_1_.refs_2_), channel_id=1, source_target_pairs={{0,16},{16,0},{1,17},{17,1},{2,18},{18,2},{3,19},{19,3},{4,20},{20... | collective-permute-start | bytes 1572872 | tf_op jit(solution)/shard_map/ppermute | solution.py:551
  66.8 1.6 %collective-permute-start.12 = (bf16[192,1024]{1,0:T(8,128)(2,1)S(1)}, bf16[192,1024]{1,0:T(8,128)(2,1)S(1)}, u32[]{:S(2)}, u32[]{:S(2)}) collective-permute-start(bf16[192,1024]{1,0:T(8,128)(2,1)S(1)} %get-tuple-element.75.refs_1_), channel_id=1, source_target_pairs={{0,2},{1,3},{2,0},{3,1},{4,6},{5,7},{6,4},{7,5},{8,10},{9,11},{10,... | collective-permute-start | bytes 1179656 | tf_op jit(solution)/shard_map/ppermute | solution.py:535
  68.4 5.9 %collective-permute-done.14.refs_6_.refs_5_ = bf16[256,1024]{1,0:T(8,128)(2,1)S(1)} collective-permute-done((bf16[256,1024]{1,0:T(8,128)(2,1)S(1)}, bf16[256,1024]{1,0:T(8,128)(2,1)S(1)}, u32[]{:S(2)}, u32[]{:S(2)}) %collective-permute-start.14) | collective-permute-done | bytes 524320 | tf_op jit(solution)/shard_map/ppermute | solution.py:545
  80.2 1.6 %collective-permute-done.28.refs_0_ = bf16[96,1024]{1,0:T(8,128)(2,1)S(1)} collective-permute-done((bf16[96,1024]{1,0:T(8,128)(2,1)S(1)}, bf16[96,1024]{1,0:T(8,128)(2,1)S(1)}, u32[]{:S(2)}, u32[]{:S(2)}) %collective-permute-start.28) | collective-permute-done | bytes 196640 | tf_op jit(solution)/shard_map/ppermute | solution.py:535
  89.7 2.0 %feed_pieces.11 = (bf16[96,1024]{1,0:T(8,128)(2,1)S(1)}, bf16[96,1024]{1,0:T(8,128)(2,1)S(1)}, bf16[96,1024]{1,0:T(8,128)(2,1)S(1)}, bf16[96,1024]{1,0:T(8,128)(2,1)S(1)}) custom-call(bf16[192,1024]{1,0:T(8,128)(2,1)S(1)} %collective-permute-done.20.refs_0_, bf16[192,1024]{1,0:T(8,128)(2,1)S(1)} %collective-permute-done.21.refs_1_, ...), custom_call_target="tpu_custom_call" | custom-call | flops 18874368 | bytes 49152 | tf_op jit(solution)/shard_map/feed_pieces/pallas_call | solution.py:439
  92.4 4.8 %collective-permute-done.27.refs_0_ = bf16[192,1024]{1,0:T(8,128)(2,1)S(1)} collective-permute-done((bf16[192,1024]{1,0:T(8,128)(2,1)S(1)}, bf16[192,1024]{1,0:T(8,128)(2,1)S(1)}, u32[]{:S(2)}, u32[]{:S(2)}) %collective-permute-start.27) | collective-permute-done | bytes 393248 | tf_op jit(solution)/shard_map/ppermute | solution.py:535
  97.2 2.0 %feed_pieces.13.refs_10_ = f32[384,1024]{1,0:T(8,128)S(1)} custom-call(bf16[192,1024]{1,0:T(8,128)(2,1)S(1)} %get-tuple-element.74.refs_0_, bf16[192,1024]{1,0:T(8,128)(2,1)S(1)} %get-tuple-element.75.refs_1_, bf16[256,1024]{1,0:T(8,128)(2,1)S(1)} %copy-done.2, bf16[256,1024]{1,0:T(8,128)(2,1)S(1)} %collective-permute-done.8.refs_3_.refs_2_, ...), custom_call_target="tpu_custom_call" | custom-call | flops 18874368 | bytes 49152 | tf_op jit(solution)/shard_map/feed_pieces/pallas_call | solution.py:439
  100.5 4.6 %collective-permute-done.31.refs_1_ = bf16[192,1024]{1,0:T(8,128)(2,1)S(1)} collective-permute-done((bf16[192,1024]{1,0:T(8,128)(2,1)S(1)}, bf16[192,1024]{1,0:T(8,128)(2,1)S(1)}, u32[]{:S(2)}, u32[]{:S(2)}) %collective-permute-start.31) | collective-permute-done | bytes 393248 | tf_op jit(solution)/shard_map/ppermute | solution.py:535
  (98 shorter events, 24.9 us)
Async XLA Ops:
  4.7 10.7 %collective-permute-start = (bf16[384,1024]{1,0:T(8,128)(2,1)S(1)}, bf16[384,1024]{1,0:T(8,128)(2,1)}, u32[]{:S(2)}, u32[]{:S(2)}) collective-permute-start(bf16[384,1024]{1,0:T(8,128)(2,1)S(1)} %get-tuple-element.66.refs_2_), channel_id=1, source_target_pairs={{0,1},{1,0},{2,3},{3,2},{4,5},{5,4},{6,7},{7,6},{8,9},{9,8},{10,11... | collective-permute-start | bytes 2359304 | tf_op jit(solution)/shard_map/ppermute | solution.py:535
  5.2 22.5 %collective-permute-start.1 = (bf16[192,1024]{1,0:T(8,128)(2,1)}, bf16[192,1024]{1,0:T(8,128)(2,1)S(1)}, u32[]{:S(2)}, u32[]{:S(2)}) collective-permute-start(bf16[192,1024]{1,0:T(8,128)(2,1)} %get-tuple-element.49), channel_id=1, source_target_pairs={{0,15},{1,2},{2,1},{3,4},{4,3},{5,6},{6,5},{7,8},{8,7},{9,10},{10,... | collective-permute-start | bytes 1179656 | tf_op jit(solution)/shard_map/ppermute | solution.py:535
  10.9 16.8 %collective-permute-start.2 = (bf16[192,1024]{1,0:T(8,128)(2,1)}, bf16[192,1024]{1,0:T(8,128)(2,1)S(1)}, u32[]{:S(2)}, u32[]{:S(2)}) collective-permute-start(bf16[192,1024]{1,0:T(8,128)(2,1)} %get-tuple-element.50), channel_id=1, source_target_pairs={{0,15},{1,2},{2,1},{3,4},{4,3},{5,6},{6,5},{7,8},{8,7},{9,10},{10,... | collective-permute-start | bytes 1179656 | tf_op jit(solution)/shard_map/ppermute | solution.py:535
  13.1 36.2 %collective-permute-start.7 = (bf16[256,1024]{1,0:T(8,128)(2,1)}, bf16[256,1024]{1,0:T(8,128)(2,1)S(1)}, u32[]{:S(2)}, u32[]{:S(2)}) collective-permute-start(bf16[256,1024]{1,0:T(8,128)(2,1)} %get-tuple-element.62), channel_id=1, source_target_pairs={{0,8},{1,9},{2,10},{3,11},{4,12},{5,13},{6,14},{7,15},{8,0},{9,1},... | collective-permute-start | bytes 1572872 | tf_op jit(solution)/shard_map/ppermute | solution.py:545
  13.7 36.4 %collective-permute-start.8 = (bf16[256,1024]{1,0:T(8,128)(2,1)}, bf16[256,1024]{1,0:T(8,128)(2,1)S(1)}, u32[]{:S(2)}, u32[]{:S(2)}) collective-permute-start(bf16[256,1024]{1,0:T(8,128)(2,1)} %get-tuple-element.62), channel_id=1, source_target_pairs={{0,4},{1,5},{2,6},{3,7},{4,0},{5,1},{6,2},{7,3},{8,12},{9,13},{10,... | collective-permute-start | bytes 1572872 | tf_op jit(solution)/shard_map/ppermute | solution.py:545
  27.7 26.3 %collective-permute-start.9 = (bf16[384,1024]{1,0:T(8,128)(2,1)S(1)}, bf16[384,1024]{1,0:T(8,128)(2,1)S(1)}, u32[]{:S(2)}, u32[]{:S(2)}) collective-permute-start(bf16[384,1024]{1,0:T(8,128)(2,1)S(1)} %get-tuple-element.66.refs_2_), channel_id=1, source_target_pairs={{0,2},{1,15},{2,4},{3,1},{4,6},{5,3},{6,8},{7,5},{8,10},{9,7},{10,... | collective-permute-start | bytes 2359304 | tf_op jit(solution)/shard_map/ppermute | solution.py:535
  28.6 4.9 %collective-permute-start.3 = (bf16[96,1024]{1,0:T(8,128)(2,1)S(1)}, bf16[96,1024]{1,0:T(8,128)(2,1)S(1)}, u32[]{:S(2)}, u32[]{:S(2)}) collective-permute-start(bf16[96,1024]{1,0:T(8,128)(2,1)S(1)} %get-tuple-element.99), channel_id=1, source_target_pairs={{0,1},{1,0},{2,3},{3,2},{4,5},{5,4},{6,7},{7,6},{8,9},{9,8},{10,11... | collective-permute-start | bytes 589832 | tf_op jit(solution)/shard_map/ppermute | solution.py:535
  50.1 15.2 %collective-permute-start.10 = (bf16[256,1024]{1,0:T(8,128)(2,1)S(1)}, bf16[256,1024]{1,0:T(8,128)(2,1)S(1)}, u32[]{:S(2)}, u32[]{:S(2)}) collective-permute-start(bf16[256,1024]{1,0:T(8,128)(2,1)S(1)} %collective-permute-done.7.refs_4_.refs_3_), channel_id=1, source_target_pairs={{0,4},{1,5},{2,6},{3,7},{4,0},{5,1},{6,2},{7,3},{8,12},{9,13},{10,... | collective-permute-start | bytes 1572872 | tf_op jit(solution)/shard_map/ppermute | solution.py:545
  52.5 21.7 %collective-permute-start.14 = (bf16[256,1024]{1,0:T(8,128)(2,1)S(1)}, bf16[256,1024]{1,0:T(8,128)(2,1)S(1)}, u32[]{:S(2)}, u32[]{:S(2)}) collective-permute-start(bf16[256,1024]{1,0:T(8,128)(2,1)S(1)} %copy-done.14), channel_id=1, source_target_pairs={{0,4},{1,5},{2,6},{3,7},{4,0},{5,1},{6,2},{7,3},{8,12},{9,13},{10,... | collective-permute-start | bytes 1572872 | tf_op jit(solution)/shard_map/ppermute | solution.py:545
  52.5 21.7 %collective-permute-start.15 = (bf16[256,1024]{1,0:T(8,128)(2,1)S(1)}, bf16[256,1024]{1,0:T(8,128)(2,1)S(1)}, u32[]{:S(2)}, u32[]{:S(2)}) collective-permute-start(bf16[256,1024]{1,0:T(8,128)(2,1)S(1)} %collective-permute-done.7.refs_4_.refs_3_), channel_id=1, source_target_pairs={{0,16},{16,0},{1,17},{17,1},{2,18},{18,2},{3,19},{19,3},{4,20},{20... | collective-permute-start | bytes 1572872 | tf_op jit(solution)/shard_map/ppermute | solution.py:551
  61.7 12.5 %collective-permute-start.13 = (bf16[192,1024]{1,0:T(8,128)(2,1)S(1)}, bf16[192,1024]{1,0:T(8,128)(2,1)S(1)}, u32[]{:S(2)}, u32[]{:S(2)}) collective-permute-start(bf16[192,1024]{1,0:T(8,128)(2,1)S(1)} %get-tuple-element.74.refs_0_), channel_id=1, source_target_pairs={{0,2},{1,3},{2,0},{3,1},{4,6},{5,7},{6,4},{7,5},{8,10},{9,11},{10,... | collective-permute-start | bytes 1179656 | tf_op jit(solution)/shard_map/ppermute | solution.py:535
  65.3 13.7 %collective-permute-start.18 = (bf16[256,1024]{1,0:T(8,128)(2,1)S(1)}, bf16[256,1024]{1,0:T(8,128)(2,1)S(1)}, u32[]{:S(2)}, u32[]{:S(2)}) collective-permute-start(bf16[256,1024]{1,0:T(8,128)(2,1)S(1)} %collective-permute-done.10.refs_1_.refs_2_), channel_id=1, source_target_pairs={{0,16},{16,0},{1,17},{17,1},{2,18},{18,2},{3,19},{19,3},{4,20},{20... | collective-permute-start | bytes 1572872 | tf_op jit(solution)/shard_map/ppermute | solution.py:551
  66.8 12.3 %collective-permute-start.12 = (bf16[192,1024]{1,0:T(8,128)(2,1)S(1)}, bf16[192,1024]{1,0:T(8,128)(2,1)S(1)}, u32[]{:S(2)}, u32[]{:S(2)}) collective-permute-start(bf16[192,1024]{1,0:T(8,128)(2,1)S(1)} %get-tuple-element.75.refs_1_), channel_id=1, source_target_pairs={{0,2},{1,3},{2,0},{3,1},{4,6},{5,7},{6,4},{7,5},{8,10},{9,11},{10,... | collective-permute-start | bytes 1179656 | tf_op jit(solution)/shard_map/ppermute | solution.py:535
  74.8 9.3 %collective-permute-start.11 = (bf16[256,1024]{1,0:T(8,128)(2,1)S(1)}, bf16[256,1024]{1,0:T(8,128)(2,1)S(1)}, u32[]{:S(2)}, u32[]{:S(2)}) collective-permute-start(bf16[256,1024]{1,0:T(8,128)(2,1)S(1)} %collective-permute-done.10.refs_1_.refs_2_), channel_id=1, source_target_pairs={{0,1},{1,0},{2,3},{3,2},{4,5},{5,4},{6,7},{7,6},{8,9},{9,8},{10,11... | collective-permute-start | bytes 1572872 | tf_op jit(solution)/shard_map/ppermute | solution.py:535
  79.1 5.2 %collective-permute-start.19 = (bf16[256,1024]{1,0:T(8,128)(2,1)S(1)}, bf16[256,1024]{1,0:T(8,128)(2,1)S(1)}, u32[]{:S(2)}, u32[]{:S(2)}) collective-permute-start(bf16[256,1024]{1,0:T(8,128)(2,1)S(1)} %collective-permute-done.18.refs_3_.refs_4_), channel_id=1, source_target_pairs={{0,1},{1,0},{2,3},{3,2},{4,5},{5,4},{6,7},{7,6},{8,9},{9,8},{10,11... | collective-permute-start | bytes 1572872 | tf_op jit(solution)/shard_map/ppermute | solution.py:535
  79.1 5.2 %collective-permute-start.26 = (bf16[192,1024]{1,0:T(8,128)(2,1)S(1)}, bf16[192,1024]{1,0:T(8,128)(2,1)S(1)}, u32[]{:S(2)}, u32[]{:S(2)}) collective-permute-start(bf16[192,1024]{1,0:T(8,128)(2,1)S(1)} %feed_pieces.9), channel_id=1, source_target_pairs={{0,1},{1,0},{2,3},{3,2},{4,5},{5,4},{6,7},{7,6},{8,9},{9,8},{10,11... | collective-permute-start | bytes 1179656 | tf_op jit(solution)/shard_map/ppermute | solution.py:535
  83.5 4.3 %collective-permute-start.30 = (bf16[192,1024]{1,0:T(8,128)(2,1)S(1)}, bf16[192,1024]{1,0:T(8,128)(2,1)S(1)}, u32[]{:S(2)}, u32[]{:S(2)}) collective-permute-start(bf16[192,1024]{1,0:T(8,128)(2,1)S(1)} %feed_pieces.15), channel_id=1, source_target_pairs={{0,1},{1,0},{2,3},{3,2},{4,5},{5,4},{6,7},{7,6},{8,9},{9,8},{10,11... | collective-permute-start | bytes 1179656 | tf_op jit(solution)/shard_map/ppermute | solution.py:535
  83.7 6.0 %collective-permute-start.20 = (bf16[192,1024]{1,0:T(8,128)(2,1)S(1)}, bf16[192,1024]{1,0:T(8,128)(2,1)S(1)}, u32[]{:S(2)}, u32[]{:S(2)}) collective-permute-start(bf16[192,1024]{1,0:T(8,128)(2,1)S(1)} %get-tuple-element.74.refs_0_), channel_id=1, source_target_pairs={{0,1},{1,0},{2,3},{3,2},{4,5},{5,4},{6,7},{7,6},{8,9},{9,8},{10,11... | collective-permute-start | bytes 1179656 | tf_op jit(solution)/shard_map/ppermute | solution.py:535
  84.1 5.6 %collective-permute-start.21 = (bf16[192,1024]{1,0:T(8,128)(2,1)S(1)}, bf16[192,1024]{1,0:T(8,128)(2,1)S(1)}, u32[]{:S(2)}, u32[]{:S(2)}) collective-permute-start(bf16[192,1024]{1,0:T(8,128)(2,1)S(1)} %get-tuple-element.75.refs_1_), channel_id=1, source_target_pairs={{0,1},{1,0},{2,3},{3,2},{4,5},{5,4},{6,7},{7,6},{8,9},{9,8},{10,11... | collective-permute-start | bytes 1179656 | tf_op jit(solution)/shard_map/ppermute | solution.py:535
  85.2 12.0 %collective-permute-start.27 = (bf16[192,1024]{1,0:T(8,128)(2,1)S(1)}, bf16[192,1024]{1,0:T(8,128)(2,1)S(1)}, u32[]{:S(2)}, u32[]{:S(2)}) collective-permute-start(bf16[192,1024]{1,0:T(8,128)(2,1)S(1)} %feed_pieces.12), channel_id=1, source_target_pairs={{0,2},{1,3},{2,0},{3,1},{4,6},{5,7},{6,4},{7,5},{8,10},{9,11},{10,... | collective-permute-start | bytes 1179656 | tf_op jit(solution)/shard_map/ppermute | solution.py:535
  88.7 16.4 %collective-permute-start.31 = (bf16[192,1024]{1,0:T(8,128)(2,1)S(1)}, bf16[192,1024]{1,0:T(8,128)(2,1)S(1)}, u32[]{:S(2)}, u32[]{:S(2)}) collective-permute-start(bf16[192,1024]{1,0:T(8,128)(2,1)S(1)} %feed_pieces.17), channel_id=1, source_target_pairs={{0,2},{1,3},{2,0},{3,1},{4,6},{5,7},{6,4},{7,5},{8,10},{9,11},{10,... | collective-permute-start | bytes 1179656 | tf_op jit(solution)/shard_map/ppermute | solution.py:535
  91.7 7.5 %collective-permute-start.22 = (bf16[96,1024]{1,0:T(8,128)(2,1)S(1)}, bf16[96,1024]{1,0:T(8,128)(2,1)S(1)}, u32[]{:S(2)}, u32[]{:S(2)}) collective-permute-start(bf16[96,1024]{1,0:T(8,128)(2,1)S(1)} %get-tuple-element.83), channel_id=1, source_target_pairs={{0,1},{1,0},{2,3},{3,2},{4,5},{5,4},{6,7},{7,6},{8,9},{9,8},{10,11... | collective-permute-start | bytes 589832 | tf_op jit(solution)/shard_map/ppermute | solution.py:535
  91.8 7.4 %collective-permute-start.23 = (bf16[96,1024]{1,0:T(8,128)(2,1)S(1)}, bf16[96,1024]{1,0:T(8,128)(2,1)S(1)}, u32[]{:S(2)}, u32[]{:S(2)}) collective-permute-start(bf16[96,1024]{1,0:T(8,128)(2,1)S(1)} %get-tuple-element.84), channel_id=1, source_target_pairs={{0,1},{1,0},{2,3},{3,2},{4,5},{5,4},{6,7},{7,6},{8,9},{9,8},{10,11... | collective-permute-start | bytes 589832 | tf_op jit(solution)/shard_map/ppermute | solution.py:535
  92.3 7.0 %collective-permute-start.24 = (bf16[96,1024]{1,0:T(8,128)(2,1)S(1)}, bf16[96,1024]{1,0:T(8,128)(2,1)S(1)}, u32[]{:S(2)}, u32[]{:S(2)}) collective-permute-start(bf16[96,1024]{1,0:T(8,128)(2,1)S(1)} %get-tuple-element.85), channel_id=1, source_target_pairs={{0,1},{1,0},{2,3},{3,2},{4,5},{5,4},{6,7},{7,6},{8,9},{9,8},{10,11... | collective-permute-start | bytes 589832 | tf_op jit(solution)/shard_map/ppermute | solution.py:535
  (23 other events, 141.4 us)

commit v7 on v6

--- a/solution.py
+++ b/solution.py
@@ -68,39 +68,29 @@
     )(features, order, gain.reshape(1, width))
 
 
-def choose_kernel(axis, one, other, chosen, left, arrived):
+def choose_kernel(axis, one, other, chosen, arrived):
     straight = lax.axis_index(axis) == 0
-
-    def copies(first, second):
-        return (
-            pltpu.make_async_copy(first, chosen, arrived.at[0]),
-            pltpu.make_async_copy(second, left, arrived.at[1]),
-        )
 
     @pl.when(straight)
     def _():
-        for copy in copies(one, other):
-            copy.start()
+        pltpu.make_async_copy(one, chosen, arrived).start()
 
     @pl.when(jnp.logical_not(straight))
     def _():
-        for copy in copies(other, one):
-            copy.start()
-
-    for copy in copies(one, other):
-        copy.wait()
-
-
-def choose(axis, one, other):
+        pltpu.make_async_copy(other, chosen, arrived).start()
+
+    pltpu.make_async_copy(one, chosen, arrived).wait()
+
+
+def choose(axis, one, other, limit):
     anywhere = pl.BlockSpec(memory_space=pl.ANY)
-    local = pl.BlockSpec(memory_space=pltpu.VMEM)
     return pl.pallas_call(
         functools.partial(choose_kernel, axis),
-        out_shape=[jax.ShapeDtypeStruct(one.shape, one.dtype)] * 2,
+        out_shape=jax.ShapeDtypeStruct(one.shape, one.dtype),
         in_specs=[anywhere, anywhere],
-        out_specs=[local, local],
-        scratch_shapes=[pltpu.SemaphoreType.DMA((2,))],
-        compiler_params=pltpu.CompilerParams(vmem_limit_bytes=60 * MIB),
+        out_specs=pl.BlockSpec(memory_space=pltpu.VMEM),
+        scratch_shapes=[pltpu.SemaphoreType.DMA],
+        compiler_params=pltpu.CompilerParams(vmem_limit_bytes=limit * MIB),
         cost_estimate=cost(0, 6 * one.size),
         name="choose",
     )(one, other)
@@ -553,7 +543,7 @@
     shared = (chip_rows, chip_columns) == (4, 2) and lax.axis_size("parts") == 2
     if shared:
         swap = [(0, 1), (1, 0), (2, 3), (3, 2)]
-        prime, left = choose("parts", w_in, w_out)
+        prime = choose("parts", w_in, w_out, 60)
         pair_rows = along(prime, swap)
         third = along(prime, [(0, 2), (1, 3), (2, 0), (3, 1)])
     order = pore_order.reshape(1, rows)
@@ -569,7 +559,8 @@
 
     (near_kv,) = project(near, w_qkv, query_gain, key_gain)
     if shared:
-        near_kv, *across = lax.optimization_barrier((near_kv, *across))
+        left = choose("parts", w_out, w_in, 8)
+        near_kv, left, *across = lax.optimization_barrier((near_kv, left, *across))
     (across_kv,) = project(across, w_qkv, query_gain, key_gain)
     mixed, totals = attend(
         "seq", cycle, block_lists, block_counts, queries, [own_mate, near_kv, across_kv]

time: 107 us -> 107 us (level); the launches traced: 106 us -> 107 us
  waiting for transfers between devices: 22.9 us -> 26.7 us
  starting transfers between devices: 26.8 us -> 24.4 us
    ppermute x26, starting transfers between devices: 19.3 us -> 16.9 us  [moved(): lax.ppermute(value, 'seq', [(i, where(i) % cycle) for i in range(cycle)])]
    ppermute x4, waiting for transfers between devices: 9.36 us -> 11.7 us  [along(): return lax.ppermute(value, 'seq', pairs)]
    ppermute x26, waiting for transfers between devices: 13.6 us -> 15 us  [moved(): lax.ppermute(value, 'seq', [(i, where(i) % cycle) for i in range(cycle)])]
    pallas_call x1 -> x2, Pallas kernels: 2.18 us -> 2.07 us  [choose(): pl.pallas_call(functools.partial(choose_kernel, axis), out_shape=jax.Shap...]
    unnamed x30 -> x28, local copies, waits for them, and re-layouts: 4.67 us -> 4.67 us
  transfers between devices with their start and end apart: 32 -> 32, of which waited for: 9 -> 11; matrix products, arithmetic and copies ran while one was open for 0% -> 0% of each run, Pallas kernels for 44% -> 44%
where the time goes in v7:
time: 107 us
  Pallas kernels  49.6 us (46%)
  waiting for transfers between devices  26.7 us (25%)
  starting transfers between devices  24.4 us (23%)
  local copies, waits for them, and re-layouts  5.64 us (5%)
    pallas_call x4, Pallas kernels, project(): pl.pallas_call(functools.partial(project_kernel, 'seq', head_dim, 2.0 / m...  18.7 us
    ppermute x26, starting transfers between devices, moved(): lax.ppermute(value, 'seq', [(i, where(i) % cycle) for i in range(cycle)])  16.9 us
    ppermute x26, waiting for transfers between devices, moved(): lax.ppermute(value, 'seq', [(i, where(i) % cycle) for i in range(cycle)])  15 us
    pallas_call x9, Pallas kernels, feed_pieces(): pl.pallas_call(functools.partial(pieces_kernel, axis, tuple((piece[2] for...  12.8 us
    ppermute x4, waiting for transfers between devices, along(): return lax.ppermute(value, 'seq', pairs)  11.7 us
    pallas_call x1, Pallas kernels, attend(): pl.pallas_call(functools.partial(attend_kernel, axis, cycle), out_shape=(...  8.06 us
    unnamed x28, local copies, waits for them, and re-layouts  4.67 us
    ppermute x4, starting transfers between devices, along(): return lax.ppermute(value, 'seq', pairs)  4.58 us
  transfers between devices with their start and end apart: 32, of which 11 were waited for; matrix products, arithmetic and copies ran while one was open for 0% of the time, Pallas kernels for 44%

profile of v7, /device:TPU:0, one launch (start us, length us, event | category | flops | bytes accessed | tf_op | source)
XLA Modules:
  0.0 107.4 jit_solution(9087931848103811857)
XLA Ops:
  3.2 1.6 %norm.1 = (bf16[384,1024]{1,0:T(8,128)(2,1)S(1)}, bf16[192,1024]{1,0:T(8,128)(2,1)}, bf16[192,1024]{1,0:T(8,128)(2,1)}) custom-call(bf16[384,1024]{1,0:T(8,128)(2,1)S(1)} %copy-done.4, s32[1,384]{1,0:T(1,128)S(1)} %reshape.15.order.refs_1_, f32[1,1024]{1,0:T(1,128)S(1)} %bitcast.2), custom_call_target="tpu_custom_call" | custom-call | flops 4718592 | bytes 36864 | tf_op jit(solution)/shard_map/norm/pallas_call | solution.py:62
  5.2 5.7 %collective-permute-start.1 = (bf16[192,1024]{1,0:T(8,128)(2,1)}, bf16[192,1024]{1,0:T(8,128)(2,1)S(1)}, u32[]{:S(2)}, u32[]{:S(2)}) collective-permute-start(bf16[192,1024]{1,0:T(8,128)(2,1)} %get-tuple-element.48), channel_id=1, source_target_pairs={{0,15},{1,2},{2,1},{3,4},{4,3},{5,6},{6,5},{7,8},{8,7},{9,10},{10,... | collective-permute-start | bytes 1179656 | tf_op jit(solution)/shard_map/ppermute | solution.py:525
  10.9 1.8 %choose.3 = bf16[256,1024]{1,0:T(8,128)(2,1)} custom-call(bf16[256,1024]{1,0:T(8,128)(2,1)} %refs_1_.5, bf16[256,1024]{1,0:T(8,128)(2,1)} %refs_4_.7), custom_call_target="tpu_custom_call" | custom-call | bytes 24576 | tf_op jit(solution)/shard_map/choose/pallas_call | solution.py:87
  13.4 1.6 %collective-permute-start.8 = (bf16[256,1024]{1,0:T(8,128)(2,1)}, bf16[256,1024]{1,0:T(8,128)(2,1)S(1)}, u32[]{:S(2)}, u32[]{:S(2)}) collective-permute-start(bf16[256,1024]{1,0:T(8,128)(2,1)} %choose.3), channel_id=1, source_target_pairs={{0,4},{1,5},{2,6},{3,7},{4,0},{5,1},{6,2},{7,3},{8,12},{9,13},{10,... | collective-permute-start | bytes 1572872 | tf_op jit(solution)/shard_map/ppermute | solution.py:535
  15.1 2.8 %copy-done = bf16[1024,3072]{1,0:T(8,128)(2,1)S(1)} copy-done((bf16[1024,3072]{1,0:T(8,128)(2,1)S(1)}, bf16[1024,3072]{1,0:T(8,128)(2,1)}, u32[]{:S(2)}) %copy-start) | copy-done | bytes 6291480
  17.9 9.4 %project.4 = (bf16[384,1024]{1,0:T(8,128)(2,1)S(1)}, bf16[384,1024]{1,0:T(8,128)(2,1)S(1)}, bf16[768,2048]{1,0:T(8,128)(2,1)S(1)}) custom-call(bf16[384,1024]{1,0:T(8,128)(2,1)S(1)} %copy-done.5, s32[1,384]{1,0:T(1,128)S(1)} %reshape.15.order.refs_1_, bf16[384,1024]{1,0:T(8,128)(2,1)S(1)} %get-tuple-element.64.refs_2_, ...), custom_call_target="tpu_custom_call" | custom-call | flops 50331648 | bytes 131072 | tf_op jit(solution)/shard_map/project/pallas_call | solution.py:179
  28.1 4.7 %collective-permute-start.3 = (bf16[96,1024]{1,0:T(8,128)(2,1)S(1)}, bf16[96,1024]{1,0:T(8,128)(2,1)S(1)}, u32[]{:S(2)}, u32[]{:S(2)}) collective-permute-start(bf16[96,1024]{1,0:T(8,128)(2,1)S(1)} %get-tuple-element.97), channel_id=1, source_target_pairs={{0,1},{1,0},{2,3},{3,2},{4,5},{5,4},{6,7},{7,6},{8,9},{9,8},{10,11... | collective-permute-start | bytes 589832 | tf_op jit(solution)/shard_map/ppermute | solution.py:525
  34.8 3.1 %project.5.near = bf16[384,2048]{1,0:T(8,128)(2,1)S(1)} custom-call(bf16[192,1024]{1,0:T(8,128)(2,1)S(1)} %collective-permute-done.1.refs_0_, bf16[192,1024]{1,0:T(8,128)(2,1)S(1)} %collective-permute-done.2.refs_1_, bf16[1024,3072]{1,0:T(8,128)(2,1)S(1)} %copy-done.1, f32[1,256]{1,0:T(1,128)S(1)} %broadcast_in_dim_tile.4.refs_5_.refs_3_.refs_2_, ...), custom_call_target="tpu_custom_call" | custom-call | flops 25165824 | bytes 131072 | tf_op jit(solution)/shard_map/project/pallas_call | solution.py:179
  37.9 3.1 %project.6.across = bf16[384,2048]{1,0:T(8,128)(2,1)S(1)} custom-call(bf16[96,1024]{1,0:T(8,128)(2,1)S(1)} %collective-permute-done.3.refs_0_, bf16[96,1024]{1,0:T(8,128)(2,1)S(1)} %collective-permute-done.4.refs_1_, bf16[96,1024]{1,0:T(8,128)(2,1)S(1)} %collective-permute-done.5.refs_2_, bf16[96,1024]{1,0:T(8,128)(2,1)S(1)} %collective-permute-done.6.refs_3_, ...), custom_call_target="tpu_custom_call" | custom-call | flops 25165824 | bytes 131072 | tf_op jit(solution)/shard_map/project/pallas_call | solution.py:179
  41.0 8.1 %attend.1 = (f32[384,1024]{1,0:T(8,128)S(1)}, f32[384,1024]{1,0:T(8,128)S(1)}) custom-call(s32[3,8]{1,0:T(4,128)S(1)} %copy-done.8, s32[3]{0:T(128)S(1)} %copy-done.11, bf16[384,1024]{1,0:T(8,128)(2,1)S(1)} %get-tuple-element.50.queries, bf16[768,2048]{1,0:T(8,128)(2,1)S(1)} %get-tuple-element.51.own_mate, bf16[384,2048]{1,0:T(8,128)(2,1)S(1)} %project.5.near, ...), custom_call_target="tpu_custom_call" | custom-call | flops 500000000 | bytes 6291456 | tf_op jit(solution)/shard_map/attend/pallas_call | solution.py:290
  50.5 2.4 %collective-permute-start.10 = (bf16[256,1024]{1,0:T(8,128)(2,1)S(1)}, bf16[256,1024]{1,0:T(8,128)(2,1)S(1)}, u32[]{:S(2)}, u32[]{:S(2)}) collective-permute-start(bf16[256,1024]{1,0:T(8,128)(2,1)S(1)} %collective-permute-done.7.refs_4_.refs_3_), channel_id=1, source_target_pairs={{0,4},{1,5},{2,6},{3,7},{4,0},{5,1},{6,2},{7,3},{8,12},{9,13},{10,... | collective-permute-start | bytes 1572872 | tf_op jit(solution)/shard_map/ppermute | solution.py:535
  52.9 1.5 %collective-permute-start.15 = (bf16[256,1024]{1,0:T(8,128)(2,1)S(1)}, bf16[256,1024]{1,0:T(8,128)(2,1)S(1)}, u32[]{:S(2)}, u32[]{:S(2)}) collective-permute-start(bf16[256,1024]{1,0:T(8,128)(2,1)S(1)} %collective-permute-done.7.refs_4_.refs_3_), channel_id=1, source_target_pairs={{0,16},{16,0},{1,17},{17,1},{2,18},{18,2},{3,19},{19,3},{4,20},{20... | collective-permute-start | bytes 1572872 | tf_op jit(solution)/shard_map/ppermute | solution.py:541
  54.4 3.1 %project.7.window = bf16[384,2048]{1,0:T(8,128)(2,1)S(1)} custom-call(bf16[384,1024]{1,0:T(8,128)(2,1)S(1)} %collective-permute-done.9.refs_0_, bf16[1024,3072]{1,0:T(8,128)(2,1)S(1)} %copy-done.1, f32[1,256]{1,0:T(1,128)S(1)} %broadcast_in_dim_tile.4.refs_5_.refs_3_.refs_2_, f32[1,256]{1,0:T(1,128)S(1)} %broadcast_in_dim_tile.5.refs_6_.refs_4_.refs_3_), custom_call_target="tpu_custom_call" | custom-call | flops 25165824 | bytes 131072 | tf_op jit(solution)/shard_map/project/pallas_call | solution.py:179
  57.5 3.4 %finish.1.attention = bf16[384,1024]{1,0:T(8,128)(2,1)S(1)} custom-call(s32[3,8]{1,0:T(4,128)S(1)} %copy-done.8, s32[3]{0:T(128)S(1)} %copy-done.11, bf16[384,1024]{1,0:T(8,128)(2,1)S(1)} %get-tuple-element.50.queries, bf16[384,2048]{1,0:T(8,128)(2,1)S(1)} %project.7.window, f32[384,1024]{1,0:T(8,128)S(1)} %get-tuple-element.66.mixed, ...), custom_call_target="tpu_custom_call" | custom-call | flops 37748736 | bytes 131072 | tf_op jit(solution)/shard_map/finish/pallas_call | solution.py:351
  60.9 1.9 %attention_output.1 = (bf16[384,1024]{1,0:T(8,128)(2,1)}, bf16[192,1024]{1,0:T(8,128)(2,1)S(1)}, bf16[192,1024]{1,0:T(8,128)(2,1)S(1)}) custom-call(bf16[384,1024]{1,0:T(8,128)(2,1)S(1)} %finish.1.attention, bf16[384,1024]{1,0:T(8,128)(2,1)S(1)} %get-tuple-element.68.ordered, bf16[1024,1024]{1,0:T(8,128)(2,1)S(1)} %copy-done.6, f32[1,1024]{1,0:T(1,128)S(1)} %bitcast.3), custom_call_target="tpu_custom_call" | custom-call | flops 12582912 | bytes 32768 | tf_op jit(solution)/shard_map/attention_output/pallas_call | solution.py:383
  62.8 2.9 %collective-permute-done.10.refs_1_.refs_2_ = bf16[256,1024]{1,0:T(8,128)(2,1)S(1)} collective-permute-done((bf16[256,1024]{1,0:T(8,128)(2,1)S(1)}, bf16[256,1024]{1,0:T(8,128)(2,1)S(1)}, u32[]{:S(2)}, u32[]{:S(2)}) %collective-permute-start.10) | collective-permute-done | bytes 524320 | tf_op jit(solution)/shard_map/ppermute | solution.py:535
  67.2 7.4 %collective-permute-done.14.refs_6_.refs_5_ = bf16[256,1024]{1,0:T(8,128)(2,1)S(1)} collective-permute-done((bf16[256,1024]{1,0:T(8,128)(2,1)S(1)}, bf16[256,1024]{1,0:T(8,128)(2,1)S(1)}, u32[]{:S(2)}, u32[]{:S(2)}) %collective-permute-start.14) | collective-permute-done | bytes 524320 | tf_op jit(solution)/shard_map/ppermute | solution.py:535
  78.4 1.9 %collective-permute-done.12.refs_0_ = bf16[192,1024]{1,0:T(8,128)(2,1)S(1)} collective-permute-done((bf16[192,1024]{1,0:T(8,128)(2,1)S(1)}, bf16[192,1024]{1,0:T(8,128)(2,1)S(1)}, u32[]{:S(2)}, u32[]{:S(2)}) %collective-permute-start.12) | collective-permute-done | bytes 393248 | tf_op jit(solution)/shard_map/ppermute | solution.py:525
  81.4 1.6 %collective-permute-done.28.refs_0_ = bf16[96,1024]{1,0:T(8,128)(2,1)S(1)} collective-permute-done((bf16[96,1024]{1,0:T(8,128)(2,1)S(1)}, bf16[96,1024]{1,0:T(8,128)(2,1)S(1)}, u32[]{:S(2)}, u32[]{:S(2)}) %collective-permute-start.28) | collective-permute-done | bytes 196640 | tf_op jit(solution)/shard_map/ppermute | solution.py:525
  86.4 1.8 %collective-permute-start.27 = (bf16[192,1024]{1,0:T(8,128)(2,1)S(1)}, bf16[192,1024]{1,0:T(8,128)(2,1)S(1)}, u32[]{:S(2)}, u32[]{:S(2)}) collective-permute-start(bf16[192,1024]{1,0:T(8,128)(2,1)S(1)} %feed_pieces.12), channel_id=1, source_target_pairs={{0,2},{1,3},{2,0},{3,1},{4,6},{5,7},{6,4},{7,5},{8,10},{9,11},{10,... | collective-permute-start | bytes 1179656 | tf_op jit(solution)/shard_map/ppermute | solution.py:525
  91.0 2.0 %feed_pieces.11 = (bf16[96,1024]{1,0:T(8,128)(2,1)S(1)}, bf16[96,1024]{1,0:T(8,128)(2,1)S(1)}, bf16[96,1024]{1,0:T(8,128)(2,1)S(1)}, bf16[96,1024]{1,0:T(8,128)(2,1)S(1)}) custom-call(bf16[192,1024]{1,0:T(8,128)(2,1)S(1)} %collective-permute-done.20.refs_0_, bf16[192,1024]{1,0:T(8,128)(2,1)S(1)} %collective-permute-done.21.refs_1_, ...), custom_call_target="tpu_custom_call" | custom-call | flops 18874368 | bytes 49152 | tf_op jit(solution)/shard_map/feed_pieces/pallas_call | solution.py:429
  93.6 4.8 %collective-permute-done.27.refs_0_ = bf16[192,1024]{1,0:T(8,128)(2,1)S(1)} collective-permute-done((bf16[192,1024]{1,0:T(8,128)(2,1)S(1)}, bf16[192,1024]{1,0:T(8,128)(2,1)S(1)}, u32[]{:S(2)}, u32[]{:S(2)}) %collective-permute-start.27) | collective-permute-done | bytes 393248 | tf_op jit(solution)/shard_map/ppermute | solution.py:525
  98.4 2.0 %feed_pieces.13.refs_10_ = f32[384,1024]{1,0:T(8,128)S(1)} custom-call(bf16[192,1024]{1,0:T(8,128)(2,1)S(1)} %get-tuple-element.72.refs_0_, bf16[192,1024]{1,0:T(8,128)(2,1)S(1)} %get-tuple-element.73.refs_1_, bf16[256,1024]{1,0:T(8,128)(2,1)S(1)} %copy-done.2, bf16[256,1024]{1,0:T(8,128)(2,1)S(1)} %collective-permute-done.8.refs_3_.refs_2_, ...), custom_call_target="tpu_custom_call" | custom-call | flops 18874368 | bytes 49152 | tf_op jit(solution)/shard_map/feed_pieces/pallas_call | solution.py:429
  101.7 4.6 %collective-permute-done.31.refs_1_ = bf16[192,1024]{1,0:T(8,128)(2,1)S(1)} collective-permute-done((bf16[192,1024]{1,0:T(8,128)(2,1)S(1)}, bf16[192,1024]{1,0:T(8,128)(2,1)S(1)}, u32[]{:S(2)}, u32[]{:S(2)}) %collective-permute-start.31) | collective-permute-done | bytes 393248 | tf_op jit(solution)/shard_map/ppermute | solution.py:525
  (97 shorter events, 23.3 us)
Async XLA Ops:
  4.7 10.4 %collective-permute-start = (bf16[384,1024]{1,0:T(8,128)(2,1)S(1)}, bf16[384,1024]{1,0:T(8,128)(2,1)}, u32[]{:S(2)}, u32[]{:S(2)}) collective-permute-start(bf16[384,1024]{1,0:T(8,128)(2,1)S(1)} %get-tuple-element.64.refs_2_), channel_id=1, source_target_pairs={{0,1},{1,0},{2,3},{3,2},{4,5},{5,4},{6,7},{7,6},{8,9},{9,8},{10,11... | collective-permute-start | bytes 2359304 | tf_op jit(solution)/shard_map/ppermute | solution.py:525
  5.2 22.1 %collective-permute-start.1 = (bf16[192,1024]{1,0:T(8,128)(2,1)}, bf16[192,1024]{1,0:T(8,128)(2,1)S(1)}, u32[]{:S(2)}, u32[]{:S(2)}) collective-permute-start(bf16[192,1024]{1,0:T(8,128)(2,1)} %get-tuple-element.48), channel_id=1, source_target_pairs={{0,15},{1,2},{2,1},{3,4},{4,3},{5,6},{6,5},{7,8},{8,7},{9,10},{10,... | collective-permute-start | bytes 1179656 | tf_op jit(solution)/shard_map/ppermute | solution.py:525
  10.9 17.2 %collective-permute-start.2 = (bf16[192,1024]{1,0:T(8,128)(2,1)}, bf16[192,1024]{1,0:T(8,128)(2,1)S(1)}, u32[]{:S(2)}, u32[]{:S(2)}) collective-permute-start(bf16[192,1024]{1,0:T(8,128)(2,1)} %get-tuple-element.49), channel_id=1, source_target_pairs={{0,15},{1,2},{2,1},{3,4},{4,3},{5,6},{6,5},{7,8},{8,7},{9,10},{10,... | collective-permute-start | bytes 1179656 | tf_op jit(solution)/shard_map/ppermute | solution.py:525
  12.8 36.4 %collective-permute-start.7 = (bf16[256,1024]{1,0:T(8,128)(2,1)}, bf16[256,1024]{1,0:T(8,128)(2,1)S(1)}, u32[]{:S(2)}, u32[]{:S(2)}) collective-permute-start(bf16[256,1024]{1,0:T(8,128)(2,1)} %choose.3), channel_id=1, source_target_pairs={{0,8},{1,9},{2,10},{3,11},{4,12},{5,13},{6,14},{7,15},{8,0},{9,1},... | collective-permute-start | bytes 1572872 | tf_op jit(solution)/shard_map/ppermute | solution.py:535
  13.4 37.1 %collective-permute-start.8 = (bf16[256,1024]{1,0:T(8,128)(2,1)}, bf16[256,1024]{1,0:T(8,128)(2,1)S(1)}, u32[]{:S(2)}, u32[]{:S(2)}) collective-permute-start(bf16[256,1024]{1,0:T(8,128)(2,1)} %choose.3), channel_id=1, source_target_pairs={{0,4},{1,5},{2,6},{3,7},{4,0},{5,1},{6,2},{7,3},{8,12},{9,13},{10,... | collective-permute-start | bytes 1572872 | tf_op jit(solution)/shard_map/ppermute | solution.py:535
  28.0 26.4 %collective-permute-start.9 = (bf16[384,1024]{1,0:T(8,128)(2,1)S(1)}, bf16[384,1024]{1,0:T(8,128)(2,1)S(1)}, u32[]{:S(2)}, u32[]{:S(2)}) collective-permute-start(bf16[384,1024]{1,0:T(8,128)(2,1)S(1)} %get-tuple-element.64.refs_2_), channel_id=1, source_target_pairs={{0,2},{1,15},{2,4},{3,1},{4,6},{5,3},{6,8},{7,5},{8,10},{9,7},{10,... | collective-permute-start | bytes 2359304 | tf_op jit(solution)/shard_map/ppermute | solution.py:525
  28.1 5.8 %collective-permute-start.3 = (bf16[96,1024]{1,0:T(8,128)(2,1)S(1)}, bf16[96,1024]{1,0:T(8,128)(2,1)S(1)}, u32[]{:S(2)}, u32[]{:S(2)}) collective-permute-start(bf16[96,1024]{1,0:T(8,128)(2,1)S(1)} %get-tuple-element.97), channel_id=1, source_target_pairs={{0,1},{1,0},{2,3},{3,2},{4,5},{5,4},{6,7},{7,6},{8,9},{9,8},{10,11... | collective-permute-start | bytes 589832 | tf_op jit(solution)/shard_map/ppermute | solution.py:525
  50.5 15.2 %collective-permute-start.10 = (bf16[256,1024]{1,0:T(8,128)(2,1)S(1)}, bf16[256,1024]{1,0:T(8,128)(2,1)S(1)}, u32[]{:S(2)}, u32[]{:S(2)}) collective-permute-start(bf16[256,1024]{1,0:T(8,128)(2,1)S(1)} %collective-permute-done.7.refs_4_.refs_3_), channel_id=1, source_target_pairs={{0,4},{1,5},{2,6},{3,7},{4,0},{5,1},{6,2},{7,3},{8,12},{9,13},{10,... | collective-permute-start | bytes 1572872 | tf_op jit(solution)/shard_map/ppermute | solution.py:535
  52.9 21.7 %collective-permute-start.14 = (bf16[256,1024]{1,0:T(8,128)(2,1)S(1)}, bf16[256,1024]{1,0:T(8,128)(2,1)S(1)}, u32[]{:S(2)}, u32[]{:S(2)}) collective-permute-start(bf16[256,1024]{1,0:T(8,128)(2,1)S(1)} %choose.2), channel_id=1, source_target_pairs={{0,4},{1,5},{2,6},{3,7},{4,0},{5,1},{6,2},{7,3},{8,12},{9,13},{10,... | collective-permute-start | bytes 1572872 | tf_op jit(solution)/shard_map/ppermute | solution.py:535
  52.9 21.7 %collective-permute-start.15 = (bf16[256,1024]{1,0:T(8,128)(2,1)S(1)}, bf16[256,1024]{1,0:T(8,128)(2,1)S(1)}, u32[]{:S(2)}, u32[]{:S(2)}) collective-permute-start(bf16[256,1024]{1,0:T(8,128)(2,1)S(1)} %collective-permute-done.7.refs_4_.refs_3_), channel_id=1, source_target_pairs={{0,16},{16,0},{1,17},{17,1},{2,18},{18,2},{3,19},{19,3},{4,20},{20... | collective-permute-start | bytes 1572872 | tf_op jit(solution)/shard_map/ppermute | solution.py:541
  62.8 12.1 %collective-permute-start.13 = (bf16[192,1024]{1,0:T(8,128)(2,1)S(1)}, bf16[192,1024]{1,0:T(8,128)(2,1)S(1)}, u32[]{:S(2)}, u32[]{:S(2)}) collective-permute-start(bf16[192,1024]{1,0:T(8,128)(2,1)S(1)} %get-tuple-element.72.refs_0_), channel_id=1, source_target_pairs={{0,2},{1,3},{2,0},{3,1},{4,6},{5,7},{6,4},{7,5},{8,10},{9,11},{10,... | collective-permute-start | bytes 1179656 | tf_op jit(solution)/shard_map/ppermute | solution.py:525
  65.7 14.6 %collective-permute-start.18 = (bf16[256,1024]{1,0:T(8,128)(2,1)S(1)}, bf16[256,1024]{1,0:T(8,128)(2,1)S(1)}, u32[]{:S(2)}, u32[]{:S(2)}) collective-permute-start(bf16[256,1024]{1,0:T(8,128)(2,1)S(1)} %collective-permute-done.10.refs_1_.refs_2_), channel_id=1, source_target_pairs={{0,16},{16,0},{1,17},{17,1},{2,18},{18,2},{3,19},{19,3},{4,20},{20... | collective-permute-start | bytes 1572872 | tf_op jit(solution)/shard_map/ppermute | solution.py:541
  67.2 13.1 %collective-permute-start.12 = (bf16[192,1024]{1,0:T(8,128)(2,1)S(1)}, bf16[192,1024]{1,0:T(8,128)(2,1)S(1)}, u32[]{:S(2)}, u32[]{:S(2)}) collective-permute-start(bf16[192,1024]{1,0:T(8,128)(2,1)S(1)} %get-tuple-element.73.refs_1_), channel_id=1, source_target_pairs={{0,2},{1,3},{2,0},{3,1},{4,6},{5,7},{6,4},{7,5},{8,10},{9,11},{10,... | collective-permute-start | bytes 1179656 | tf_op jit(solution)/shard_map/ppermute | solution.py:525
  75.5 9.9 %collective-permute-start.11 = (bf16[256,1024]{1,0:T(8,128)(2,1)S(1)}, bf16[256,1024]{1,0:T(8,128)(2,1)S(1)}, u32[]{:S(2)}, u32[]{:S(2)}) collective-permute-start(bf16[256,1024]{1,0:T(8,128)(2,1)S(1)} %collective-permute-done.10.refs_1_.refs_2_), channel_id=1, source_target_pairs={{0,1},{1,0},{2,3},{3,2},{4,5},{5,4},{6,7},{7,6},{8,9},{9,8},{10,11... | collective-permute-start | bytes 1572872 | tf_op jit(solution)/shard_map/ppermute | solution.py:525
  80.3 5.2 %collective-permute-start.19 = (bf16[256,1024]{1,0:T(8,128)(2,1)S(1)}, bf16[256,1024]{1,0:T(8,128)(2,1)S(1)}, u32[]{:S(2)}, u32[]{:S(2)}) collective-permute-start(bf16[256,1024]{1,0:T(8,128)(2,1)S(1)} %collective-permute-done.18.refs_3_.refs_4_), channel_id=1, source_target_pairs={{0,1},{1,0},{2,3},{3,2},{4,5},{5,4},{6,7},{7,6},{8,9},{9,8},{10,11... | collective-permute-start | bytes 1572872 | tf_op jit(solution)/shard_map/ppermute | solution.py:525
  80.3 5.2 %collective-permute-start.26 = (bf16[192,1024]{1,0:T(8,128)(2,1)S(1)}, bf16[192,1024]{1,0:T(8,128)(2,1)S(1)}, u32[]{:S(2)}, u32[]{:S(2)}) collective-permute-start(bf16[192,1024]{1,0:T(8,128)(2,1)S(1)} %feed_pieces.9), channel_id=1, source_target_pairs={{0,1},{1,0},{2,3},{3,2},{4,5},{5,4},{6,7},{7,6},{8,9},{9,8},{10,11... | collective-permute-start | bytes 1179656 | tf_op jit(solution)/shard_map/ppermute | solution.py:525
  84.8 4.9 %collective-permute-start.30 = (bf16[192,1024]{1,0:T(8,128)(2,1)S(1)}, bf16[192,1024]{1,0:T(8,128)(2,1)S(1)}, u32[]{:S(2)}, u32[]{:S(2)}) collective-permute-start(bf16[192,1024]{1,0:T(8,128)(2,1)S(1)} %feed_pieces.15), channel_id=1, source_target_pairs={{0,1},{1,0},{2,3},{3,2},{4,5},{5,4},{6,7},{7,6},{8,9},{9,8},{10,11... | collective-permute-start | bytes 1179656 | tf_op jit(solution)/shard_map/ppermute | solution.py:525
  85.0 6.0 %collective-permute-start.20 = (bf16[192,1024]{1,0:T(8,128)(2,1)S(1)}, bf16[192,1024]{1,0:T(8,128)(2,1)S(1)}, u32[]{:S(2)}, u32[]{:S(2)}) collective-permute-start(bf16[192,1024]{1,0:T(8,128)(2,1)S(1)} %get-tuple-element.72.refs_0_), channel_id=1, source_target_pairs={{0,1},{1,0},{2,3},{3,2},{4,5},{5,4},{6,7},{7,6},{8,9},{9,8},{10,11... | collective-permute-start | bytes 1179656 | tf_op jit(solution)/shard_map/ppermute | solution.py:525
  85.4 5.6 %collective-permute-start.21 = (bf16[192,1024]{1,0:T(8,128)(2,1)S(1)}, bf16[192,1024]{1,0:T(8,128)(2,1)S(1)}, u32[]{:S(2)}, u32[]{:S(2)}) collective-permute-start(bf16[192,1024]{1,0:T(8,128)(2,1)S(1)} %get-tuple-element.73.refs_1_), channel_id=1, source_target_pairs={{0,1},{1,0},{2,3},{3,2},{4,5},{5,4},{6,7},{7,6},{8,9},{9,8},{10,11... | collective-permute-start | bytes 1179656 | tf_op jit(solution)/shard_map/ppermute | solution.py:525
  86.4 12.0 %collective-permute-start.27 = (bf16[192,1024]{1,0:T(8,128)(2,1)S(1)}, bf16[192,1024]{1,0:T(8,128)(2,1)S(1)}, u32[]{:S(2)}, u32[]{:S(2)}) collective-permute-start(bf16[192,1024]{1,0:T(8,128)(2,1)S(1)} %feed_pieces.12), channel_id=1, source_target_pairs={{0,2},{1,3},{2,0},{3,1},{4,6},{5,7},{6,4},{7,5},{8,10},{9,11},{10,... | collective-permute-start | bytes 1179656 | tf_op jit(solution)/shard_map/ppermute | solution.py:525
  90.6 15.7 %collective-permute-start.31 = (bf16[192,1024]{1,0:T(8,128)(2,1)S(1)}, bf16[192,1024]{1,0:T(8,128)(2,1)S(1)}, u32[]{:S(2)}, u32[]{:S(2)}) collective-permute-start(bf16[192,1024]{1,0:T(8,128)(2,1)S(1)} %feed_pieces.17), channel_id=1, source_target_pairs={{0,2},{1,3},{2,0},{3,1},{4,6},{5,7},{6,4},{7,5},{8,10},{9,11},{10,... | collective-permute-start | bytes 1179656 | tf_op jit(solution)/shard_map/ppermute | solution.py:525
  93.0 7.5 %collective-permute-start.22 = (bf16[96,1024]{1,0:T(8,128)(2,1)S(1)}, bf16[96,1024]{1,0:T(8,128)(2,1)S(1)}, u32[]{:S(2)}, u32[]{:S(2)}) collective-permute-start(bf16[96,1024]{1,0:T(8,128)(2,1)S(1)} %get-tuple-element.81), channel_id=1, source_target_pairs={{0,1},{1,0},{2,3},{3,2},{4,5},{5,4},{6,7},{7,6},{8,9},{9,8},{10,11... | collective-permute-start | bytes 589832 | tf_op jit(solution)/shard_map/ppermute | solution.py:525
  93.1 7.4 %collective-permute-start.23 = (bf16[96,1024]{1,0:T(8,128)(2,1)S(1)}, bf16[96,1024]{1,0:T(8,128)(2,1)S(1)}, u32[]{:S(2)}, u32[]{:S(2)}) collective-permute-start(bf16[96,1024]{1,0:T(8,128)(2,1)S(1)} %get-tuple-element.82), channel_id=1, source_target_pairs={{0,1},{1,0},{2,3},{3,2},{4,5},{5,4},{6,7},{7,6},{8,9},{9,8},{10,11... | collective-permute-start | bytes 589832 | tf_op jit(solution)/shard_map/ppermute | solution.py:525
  93.6 6.9 %collective-permute-start.24 = (bf16[96,1024]{1,0:T(8,128)(2,1)S(1)}, bf16[96,1024]{1,0:T(8,128)(2,1)S(1)}, u32[]{:S(2)}, u32[]{:S(2)}) collective-permute-start(bf16[96,1024]{1,0:T(8,128)(2,1)S(1)} %get-tuple-element.83), channel_id=1, source_target_pairs={{0,1},{1,0},{2,3},{3,2},{4,5},{5,4},{6,7},{7,6},{8,9},{9,8},{10,11... | collective-permute-start | bytes 589832 | tf_op jit(solution)/shard_map/ppermute | solution.py:525
  (22 other events, 115.4 us)
